TPU v7x, 128 devices: a whole 4x4x4 slice. The times are simulated.
128 devices in a mesh: fsdp: 8 (over y_lo, x), rep: 16 (over z, y_hi, core).
Axes of the slice: x: 4, y: 4 (y_hi: 2, y_lo: 2; y = y_hi * 2 + y_lo), z: 4, core: 2. Of those that a mesh axis runs over, the one named last changes fastest.
Arguments:
- partial_grads: bfloat16 [16, 8, 2, 256, 8192], P('rep', 'fsdp'), may hold values from -400 to 400
- params: float32 [2, 256, 8192], P(None, 'fsdp'), may hold values from -4 to 4
- moment: float32 [2, 256, 8192], P(None, 'fsdp'), may hold values from -3 to 3
- second_moment: float32 [2, 256, 8192], P(None, 'fsdp'), may hold values from 0.05 to 1
- snapshot: float32 [16, 2, 256, 8192], P('rep', None, 'fsdp'), may hold values from -6 to 6
Outputs:
- new_params: float32 [2, 256, 8192], P(None, 'fsdp')
- new_moment: float32 [2, 256, 8192], P(None, 'fsdp')
- new_second: float32 [2, 256, 8192], P(None, 'fsdp')
- held_delta: float32 [16, 2, 256, 8192], P('rep', None, 'fsdp')
All inputs are finite; a program needn't handle non-finite values.
Results may differ from a plain program's by a relative error of at most 0.0028.
Values may be sent and summed in bfloat16 or wider, within the bound.
No kernel may reach another device: no remote copies, remote signals or barrier semaphores. Data moves between devices by JAX's collectives and lax.ppermute only.
A program may use at most 128 MiB of HBM per device.

v0:
```python
import jax
import jax.numpy as jnp
from jax import lax
from jax.sharding import PartitionSpec as P

QBLOCK = 128


beta_first = 0.9
beta_second = 0.95
learn_rate = 0.02
decay_rate = 0.1
adam_eps = 1e-08
scale_eps = 1e-06
rms_eps = 1e-06


def shifted(value, axis, by):
    length = lax.axis_size(axis)
    return lax.ppermute(value, axis, [(i, (i + by) % length) for i in range(length)])


def encode(weight_delta):
    num_layers, num_rows, full_width = weight_delta.shape
    blocks = weight_delta.reshape(num_layers, num_rows, full_width // QBLOCK, QBLOCK)
    scales = (jnp.max(jnp.abs(blocks), axis=-1) + scale_eps).astype(jnp.bfloat16)
    scales = lax.optimization_barrier(scales)
    wide_scales = scales.astype(jnp.float32)[..., None]
    code_words = (
        (blocks / wide_scales).astype(jnp.bfloat16).reshape(num_layers, num_rows, full_width)
    )
    return (code_words, scales)


def decode(code_words, scales):
    lead_shape = code_words.shape[:-1]
    full_width = code_words.shape[-1]
    blocks = code_words.astype(jnp.float32).reshape(lead_shape + (full_width // QBLOCK, QBLOCK))
    return (blocks * scales.astype(jnp.float32)[..., None]).reshape(lead_shape + (full_width,))


def local(partial_grads, params, moment, second_moment, snapshot):
    summands = partial_grads[0, 0].astype(jnp.float32)
    cell_count = params.shape[0] * params.shape[1] * lax.axis_size("fsdp") * params.shape[2]
    row_shard = lax.psum_scatter(summands, "fsdp", scatter_dimension=1, tiled=True)
    reduced = lax.psum(row_shard, "rep")
    squares = lax.psum(jnp.sum(reduced * reduced), "fsdp")
    grad_rms = jnp.sqrt(squares / cell_count + rms_eps)
    clip_factor = 1.0 / grad_rms
    clipped = clip_factor * reduced
    new_moment = beta_first * moment + (1.0 - beta_first) * clipped
    new_second = beta_second * second_moment + (1.0 - beta_second) * clipped * clipped
    new_params = params - learn_rate * (
        new_moment / (jnp.sqrt(new_second) + adam_eps) + decay_rate * params
    )
    code_words, scales = encode(new_params - snapshot[0])
    received = []
    for layer_idx in range(code_words.shape[0]):
        got_codes, got_scales = shifted((code_words[layer_idx], scales[layer_idx]), "rep", 1)
        received.append(decode(got_codes, got_scales))
    held_delta = jnp.stack(received)
    return (new_params, new_moment, new_second, held_delta[None])


def solution(mesh):
    return jax.shard_map(
        local,
        mesh=mesh,
        in_specs=(
            P("rep", "fsdp", None, None, None),
            P(None, "fsdp", None),
            P(None, "fsdp", None),
            P(None, "fsdp", None),
            P("rep", None, "fsdp", None),
        ),
        out_specs=(
            P(None, "fsdp", None),
            P(None, "fsdp", None),
            P(None, "fsdp", None),
            P("rep", None, "fsdp", None),
        ),
        check_vma=False,
    )
```

profile of v0, /device:TPU:1, one launch (start us, length us, event | category | flops | bytes accessed | tf_op | source)
XLA Modules:
  0.0 393.6 jit_solution(11826767742505102529)
XLA Ops:
  7.2 11.3 %bitcast_convert_fusion = f32[2,256,8192]{2,1,0:T(8,128)} fusion(bf16[1,1,2,256,8192]{4,3,2,1,0:T(8,128)(2,1)} %param.5), kind=kLoop, calls=%fused_computation | loop fusion | flops 4194304 | bytes 25165824 | tf_op jit(solution)/shard_map/convert_element_type | solution.py:43
  18.5 0.0 all-reduce.2.cloned.1.call-start
  18.6 174.6 %reduce-scatter.2.cloned.1.call-done = f32[2,32,8192]{2,1,0:T(8,128)} async-done(((f32[2,256,8192]{2,1,0:T(8,128)}), f32[2,32,8192]{2,1,0:T(8,128)}) %reduce-scatter.2.cloned.1.call-update) | async-done | bytes 2097168 | tf_op jit(solution)/shard_map/reduce_scatter | solution.py:45
  193.3 146.9 %all-reduce.2.cloned.1.call-done = f32[2,32,8192]{2,1,0:T(8,128)} async-done(((f32[2,32,8192]{2,1,0:T(8,128)}), f32[2,32,8192]{2,1,0:T(8,128)}) %all-reduce.2.cloned.1.call-update) | async-done | bytes 2097168 | tf_op jit(solution)/shard_map/psum | solution.py:46
  340.2 2.9 multiply_reduce_fusion
  343.0 15.5 %psum.15 = f32[]{:T(128)} all-reduce(f32[]{:T(128)} %multiply_reduce_fusion), channel_id=1, replica_groups=mesh['fsdp'=8,'rep'=16] {'fsdp'}, use_global_device_ids=true, to_apply=%region_3.0 | all-reduce | flops 1 | bytes 8 | tf_op jit(solution)/shard_map/psum | solution.py:47
  359.3 7.1 %bitcast_subtract_fusion = (f32[2,32,8192]{2,1,0:T(8,128)S(1)}, f32[2,32,8192]{2,1,0:T(8,128)}, f32[2,32,8192]{2,1,0:T(8,128)}, f32[2,32,8192]{2,1,0:T(8,128)}) fusion(f32[1,2,32,8192]{3,2,1,0:T(8,128)} %param.9, f32[2,32,8192]{2,1,0:T(8,128)} %param.6, f32[2,32,8192]{2,1,0:T(8,128)S(1)} %copy-done, f32[]{:T(128)S(6)} %sqrt.6, f32[2,32,8192]{2,1,0:T(8,128)} %param.8, ...), kind=kLoop, calls=%fused_computation.8 | loop fusion | flops 7864320 | bytes 18874372 | tf_op jit(solution)/shard_map/sub | solution.py:56
  366.4 0.4 copy.9
  366.8 0.6 fusion.1
  367.4 0.7 fusion.2
  368.1 0.1 fusion.6
  368.2 0.3 copy.18
  368.6 3.8 collective-permute-start.2
  372.4 0.1 collective-permute-start.3
  372.5 0.3 copy.19
  372.8 0.1 collective-permute-start.1
  372.9 0.1 collective-permute-start
  373.0 5.6 %collective-permute-done.3 = bf16[32,64]{1,0:T(8,128)(2,1)S(1)} collective-permute-done((bf16[32,64]{1,0:T(8,128)(2,1)S(1)}, bf16[32,64]{1,0:T(8,128)(2,1)S(1)}, u32[]{:S(2)}, u32[]{:S(2)}) %collective-permute-start.3) | collective-permute-done | bytes 4128 | tf_op jit(solution)/shard_map/ppermute | solution.py:20
  378.6 0.3 mul.88
  378.9 0.6 fusion.3
  379.6 4.7 %collective-permute-done = bf16[32,8192]{1,0:T(8,128)(2,1)S(1)} collective-permute-done((bf16[32,8192]{1,0:T(8,128)(2,1)S(1)}, bf16[32,8192]{1,0:T(8,128)(2,1)S(1)}, u32[]{:S(2)}, u32[]{:S(2)}) %collective-permute-start) | collective-permute-done | bytes 524320 | tf_op jit(solution)/shard_map/ppermute | solution.py:20
  384.3 0.3 mul.84
  384.6 0.6 fusion.4
  385.3 1.5 maximum_bitcast_fusion
  (10 shorter events, 0.1 us)
Async XLA Ops:
  7.2 186.1 %reduce-scatter.2.cloned.1.call-start = ((), (), s32[]{:S(2)}) async-start(), calls=%async_computation.1 | async-start | bytes 18874368 | tf_op jit(solution)/shard_map/reduce_scatter | solution.py:45
  18.5 321.6 %all-reduce.2.cloned.1.call-start = ((), (), s32[]{:S(2)}) async-start(), calls=%async_computation.2 | async-start | bytes 4194304 | tf_op jit(solution)/shard_map/psum | solution.py:46
  340.1 19.1 %copy-start = (f32[2,32,8192]{2,1,0:T(8,128)S(1)}, f32[2,32,8192]{2,1,0:T(8,128)}, u32[]{:S(2)}) copy-start(f32[2,32,8192]{2,1,0:T(8,128)} %all-reduce.2.cloned.1.call-done) | copy-start | bytes 6291460
  368.6 10.0 %collective-permute-start.2 = (bf16[32,8192]{1,0:T(8,128)(2,1)S(1)}, bf16[32,8192]{1,0:T(8,128)(2,1)S(1)}, u32[]{:S(2)}, u32[]{:S(2)}) collective-permute-start(bf16[32,8192]{1,0:T(8,128)(2,1)S(1)} %bitcast.54), channel_id=1, source_target_pairs={{0,1},{1,2},{2,3},{3,4},{4,5},{5,6},{6,7},{7,8},{8,9},{9,10},{10,1... | collective-permute-start | bytes 1572872 | tf_op jit(solution)/shard_map/ppermute | solution.py:20
  372.4 6.2 %collective-permute-start.3 = (bf16[32,64]{1,0:T(8,128)(2,1)S(1)}, bf16[32,64]{1,0:T(8,128)(2,1)S(1)}, u32[]{:S(2)}, u32[]{:S(2)}) collective-permute-start(bf16[32,64]{1,0:T(8,128)(2,1)S(1)} %get-tuple-element.11), channel_id=1, source_target_pairs={{0,1},{1,2},{2,3},{3,4},{4,5},{5,6},{6,7},{7,8},{8,9},{9,10},{10,1... | collective-permute-start | bytes 12296 | tf_op jit(solution)/shard_map/ppermute | solution.py:20
  372.8 6.7 %collective-permute-start.1 = (bf16[32,64]{1,0:T(8,128)(2,1)S(1)}, bf16[32,64]{1,0:T(8,128)(2,1)S(1)}, u32[]{:S(2)}, u32[]{:S(2)}) collective-permute-start(bf16[32,64]{1,0:T(8,128)(2,1)S(1)} %get-tuple-element.10), channel_id=1, source_target_pairs={{0,1},{1,2},{2,3},{3,4},{4,5},{5,6},{6,7},{7,8},{8,9},{9,10},{10,1... | collective-permute-start | bytes 12296 | tf_op jit(solution)/shard_map/ppermute | solution.py:20
  372.9 11.4 %collective-permute-start = (bf16[32,8192]{1,0:T(8,128)(2,1)S(1)}, bf16[32,8192]{1,0:T(8,128)(2,1)S(1)}, u32[]{:S(2)}, u32[]{:S(2)}) collective-permute-start(bf16[32,8192]{1,0:T(8,128)(2,1)S(1)} %bitcast.55), channel_id=1, source_target_pairs={{0,1},{1,2},{2,3},{3,4},{4,5},{5,6},{6,7},{7,8},{8,9},{9,10},{10,1... | collective-permute-start | bytes 1572872 | tf_op jit(solution)/shard_map/ppermute | solution.py:20
Sparse Core Ops, SparseCore 0:
  18.7 174.5 reduce-scatter.1
  195.7 144.3 all-reduce.1
where the time goes:
time: 400 us; the launch traced here: 394 us
  waiting for transfers between devices  332 us (83%)
  other arithmetic  25.4 us (6%)
  blocking collectives  15.5 us (4%)
  between operations  14.8 us (4%)
  starting transfers between devices  4.15 us (1%)
    reduce_scatter x1, waiting for transfers between devices, local(): lax.psum_scatter(summands, 'fsdp', scatter_dimension=1, tiled=True)  175 us
    psum x1, waiting for transfers between devices, local(): reduced = lax.psum(row_shard, 'rep')  147 us
    psum x1, blocking collectives, local(): squares = lax.psum(jnp.sum(reduced * reduced), 'fsdp')  15.5 us
    convert_element_type x1, other arithmetic, local(): summands = partial_grads[0, 0].astype(jnp.float32)  11.3 us
    ppermute x4, waiting for transfers between devices, shifted(): lax.ppermute(value, axis, [(i, (i + by) % length) for i in range(length)])  10.3 us
  transfers between devices with their start and end apart: 6, of which 4 were waited for; matrix products, arithmetic and copies ran while one was open for 0% of the time, Pallas kernels for 0%

commit v1 on v0

v1 whole, which is shorter than its diff:
```python
import jax
import jax.numpy as jnp
from jax import lax
from jax.sharding import PartitionSpec as P

QBLOCK = 128
AXES = ("fsdp", "rep")

beta_first = 0.9
beta_second = 0.95
learn_rate = 0.02
decay_rate = 0.1
adam_eps = 1e-08
scale_eps = 1e-06
rms_eps = 1e-06


def spots():
    return [
        (x, yl + 2 * yh, z, c)
        for yl in range(2)
        for x in range(4)
        for z in range(4)
        for yh in range(2)
        for c in range(2)
    ]


def rank(x, y, z, c):
    x, y, z, c = x % 4, y % 4, z % 4, c % 2
    return ((y % 2) * 4 + x) * 16 + z * 4 + (y // 2) * 2 + c


def move(value, x=0, y=0, z=0, c=0):
    pairs = [(rank(*s), rank(s[0] + x, s[1] + y, s[2] + z, s[3] + c)) for s in spots()]
    return lax.ppermute(value, AXES, pairs)


def pick(value, index, axis):
    return lax.dynamic_index_in_dim(value, index, axis, keepdims=False)


def wide(value):
    return value.astype(jnp.float32)


def narrow(value):
    return value.astype(jnp.bfloat16)


def exchange(value, axis, me, name):
    own = pick(value, me, axis)
    got = [
        move(narrow(pick(value, (me + k) % 4, axis)), **{name: k}) for k in (1, 3, 2)
    ]
    for g in got:
        own = own + wide(g)
    return own


def local(partial_grads, params, moment, second_moment, snapshot):
    fsdp = lax.axis_index("fsdp")
    rep = lax.axis_index("rep")
    x, yl = fsdp % 4, fsdp // 4
    z, yh, c = rep // 4, (rep // 2) % 2, rep % 2
    grads = partial_grads[0, 0]
    swapped = move(pick(grads, 1 - c, 0), c=1)
    base = narrow(params - snapshot[0])
    held_base = lax.ppermute(base, "rep", [(i, (i + 1) % 16) for i in range(16)])

    total = wide(pick(grads, c, 0)) + wide(swapped)
    total = total.reshape(2, 4, 4, 8, 8192)
    left, right = total[..., :4096], total[..., 4096:]
    left = exchange(left, 1, x, "x")
    right = exchange(right, 2, z, "z")
    left = exchange(left, 1, z, "z")
    right = exchange(right, 1, x, "x")
    both = jnp.concatenate([left, right], axis=-1)
    other = narrow(pick(both, 1 - yl, 0))
    mine = pick(both, yl, 0)
    mine = narrow(mine)
    side = wide(move(other, y=1)) + wide(move(other, y=3))
    piece = (wide(mine) + wide(move(mine, y=2))) + side

    squares = jnp.sum(piece * piece).reshape(1, 1)
    for name in ("x", "z"):
        side = move(squares, **{name: 1}) + move(squares, **{name: 3})
        squares = (squares + move(squares, **{name: 2})) + side
    squares = squares + move(squares, c=1)
    fs = [(i, (i + 4) % 8) for i in range(8)]
    squares = squares + lax.ppermute(squares, "fsdp", fs)

    small = narrow(piece)
    ring = jnp.stack([small] + [move(small, z=k) for k in (1, 2, 3)])
    ring = jnp.stack([pick(ring, (z - j) % 4, 0) for j in range(4)])
    ring = ring.reshape(32, 8192)
    swap = move(ring, c=1)
    reduced = wide(jnp.stack([jnp.where(c == 0, ring, swap), jnp.where(c == 0, swap, ring)]))

    clip_factor = lax.rsqrt(squares[0, 0] / (2 * 256 * 8192) + rms_eps)
    clipped = clip_factor * reduced
    new_moment = beta_first * moment + (1.0 - beta_first) * clipped
    new_second = beta_second * second_moment + (1.0 - beta_second) * clipped * clipped
    change = -learn_rate * (
        new_moment / (jnp.sqrt(new_second) + adam_eps) + decay_rate * params
    )
    new_params = params + change
    delta = change + wide(held_base)
    blocks = delta.reshape(2, 32, 64, QBLOCK)
    scales = narrow(jnp.max(jnp.abs(blocks), axis=-1) + scale_eps)
    scales = wide(lax.optimization_barrier(scales))[..., None]
    codes = lax.optimization_barrier(narrow(blocks / scales))
    held = (wide(codes) * scales).reshape(1, 2, 32, 8192)
    return (new_params, new_moment, new_second, held)


def solution(mesh):
    return jax.shard_map(
        local,
        mesh=mesh,
        in_specs=(
            P("rep", "fsdp", None, None, None),
            P(None, "fsdp", None),
            P(None, "fsdp", None),
            P(None, "fsdp", None),
            P("rep", None, "fsdp", None),
        ),
        out_specs=(
            P(None, "fsdp", None),
            P(None, "fsdp", None),
            P(None, "fsdp", None),
            P("rep", None, "fsdp", None),
        ),
        check_vma=False,
    )
```

time: 400 us -> 140 us (0.35); the launches traced: 394 us -> 140 us
  waiting for transfers between devices: 332 us -> 40.8 us
  starting transfers between devices: 4.15 us -> 51.4 us
  blocking collectives: 15.5 us -> 0 us
  local copies, waits for them, and re-layouts: 1.79 us -> 14.8 us
  between operations: 14.8 us -> 6.87 us
    reduce_scatter x1 -> x0, waiting for transfers between devices: 175 us -> none  [local(): lax.psum_scatter(summands, 'fsdp', scatter_dimension=1, tiled=True)]
    psum x1 -> x0, waiting for transfers between devices: 147 us -> none  [local(): reduced = lax.psum(row_shard, 'rep')]
    ppermute x4 -> x29, starting transfers between devices: 4.07 us -> 51.4 us  [the longest x27 49.5 us: move(): return lax.ppermute(value, AXES, pairs)]
    ppermute x4 -> x29, waiting for transfers between devices: 10.3 us -> 40.8 us  [the longest x27 39.1 us: move(): return lax.ppermute(value, AXES, pairs)]
    add x0 -> x7, other arithmetic: none -> 18 us  [the longest x1 5.55 us: local(): delta = change + wide(held_base)]
    psum x1 -> x0, blocking collectives: 15.5 us -> none  [local(): squares = lax.psum(jnp.sum(reduced * reduced), 'fsdp')]
    convert_element_type x4 -> x5, other arithmetic: 12 us -> 3.51 us  [the longest x4 3.51 us: narrow(): return value.astype(jnp.bfloat16)]
    sub x1 -> x0, other arithmetic: 7.14 us -> none  [local(): code_words, scales = encode(new_params - snapshot[0])]
  transfers between devices with their start and end apart: 6 -> 29, of which waited for: 4 -> 12; matrix products, arithmetic and copies ran while one was open for 0% -> 6% of each run, Pallas kernels for 0% -> 0%
where the time goes in v1:
time: 140 us
  starting transfers between devices  51.4 us (37%)
  waiting for transfers between devices  40.8 us (29%)
  other arithmetic  25.7 us (18%)
  local copies, waits for them, and re-layouts  14.8 us (11%)
  between operations  6.87 us (5%)
    ppermute x27, starting transfers between devices, move(): return lax.ppermute(value, AXES, pairs)  49.5 us
    ppermute x27, waiting for transfers between devices, move(): return lax.ppermute(value, AXES, pairs)  39.1 us
    add x1, other arithmetic, local(): delta = change + wide(held_base)  5.55 us
    add x1, other arithmetic, local(): total = wide(pick(grads, c, 0)) + wide(swapped)  4.89 us
    squeeze x1, local copies, waits for them, and re-layouts, pick(): return lax.dynamic_index_in_dim(value, index, axis, keepdims=False)  4.59 us
    add x1, other arithmetic, local(): new_params = params + change  4.49 us
    convert_element_type x4, other arithmetic, narrow(): return value.astype(jnp.bfloat16)  3.51 us
    add x4, other arithmetic, exchange(): own = own + wide(g)  3.02 us
  transfers between devices with their start and end apart: 29, of which 12 were waited for; matrix products, arithmetic and copies ran while one was open for 6% of the time, Pallas kernels for 0%

profile of v1, /device:TPU:1, one launch (start us, length us, event | category | flops | bytes accessed | tf_op | source)
XLA Modules:
  0.0 139.7 jit_solution(16107613067583660319)
XLA Ops:
  0.6 4.6 %dynamic-slice_bitcast_fusion = bf16[256,8192]{1,0:T(8,128)(2,1)} fusion(bf16[1,1,2,256,8192]{4,3,2,1,0:T(8,128)(2,1)} %param.5, s32[]{:T(128)S(6)} %select_n.146), kind=kLoop, calls=%fused_computation.1 | loop fusion | bytes 8388612 | tf_op jit(solution)/shard_map/jit(dynamic_index_in_dim)/squeeze | solution.py:40
  6.7 7.1 %collective-permute-done = bf16[256,8192]{1,0:T(8,128)(2,1)} collective-permute-done((bf16[256,8192]{1,0:T(8,128)(2,1)}, bf16[256,8192]{1,0:T(8,128)(2,1)}, u32[]{:S(2)}, u32[]{:S(2)}) %collective-permute-start) | collective-permute-done | bytes 4194336 | tf_op jit(solution)/shard_map/ppermute | solution.py:36
  13.8 4.9 %convert_add_fusion = f32[256,8192]{1,0:T(8,128)S(1)} fusion(bf16[256,8192]{1,0:T(8,128)(2,1)} %collective-permute-done, bf16[1,1,2,256,8192]{4,3,2,1,0:T(8,128)(2,1)} %param.5, s32[]{:T(128)S(6)} %select_n.145), kind=kLoop, calls=%fused_computation | loop fusion | flops 6291456 | bytes 16777220 | tf_op jit(solution)/shard_map/add | solution.py:71
  18.7 2.7 %fusion.35 = (f32[2,4,4,8,4096]{4,3,2,1,0:T(8,128)S(1)}, f32[2,4,4,8,4096]{4,3,2,1,0:T(8,128)}) fusion(f32[2,4,4,8,8192]{4,3,2,1,0:T(8,128)S(1)} %bitcast.102), kind=kLoop, calls=%fused_computation.85 | loop fusion | bytes 16777216 | tf_op jit(solution)/shard_map/slice | solution.py:73
  31.8 2.2 %collective-permute-start.8 = (bf16[2,4,8,4096]{3,2,0,1:T(8,128)(2,1)S(1)}, bf16[2,4,8,4096]{3,2,0,1:T(8,128)(2,1)S(1)}, u32[]{:S(2)}, u32[]{:S(2)}) collective-permute-start(bf16[2,4,8,4096]{3,2,0,1:T(8,128)(2,1)S(1)} %bitcast.109), channel_id=1, source_target_pairs={{0,12},{1,13},{2,14},{3,15},{4,0},{5,1},{6,2},{7,3},{8,4},{9,5},{1... | collective-permute-start | bytes 1572872 | tf_op jit(solution)/shard_map/ppermute | solution.py:36
  34.1 3.7 %collective-permute-done.1 = bf16[2,4,8,4096]{3,2,0,1:T(8,128)(2,1)S(1)} collective-permute-done((bf16[2,4,8,4096]{3,2,0,1:T(8,128)(2,1)S(1)}, bf16[2,4,8,4096]{3,2,0,1:T(8,128)(2,1)S(1)}, u32[]{:S(2)}, u32[]{:S(2)}) %collective-permute-start.1) | collective-permute-done | bytes 524320 | tf_op jit(solution)/shard_map/ppermute | solution.py:36
  37.8 3.7 %collective-permute-start.9 = (bf16[2,4,8,4096]{3,2,0,1:T(8,128)(2,1)S(1)}, bf16[2,4,8,4096]{3,2,0,1:T(8,128)(2,1)S(1)}, u32[]{:S(2)}, u32[]{:S(2)}) collective-permute-start(bf16[2,4,8,4096]{3,2,0,1:T(8,128)(2,1)S(1)} %bitcast.111), channel_id=1, source_target_pairs={{0,8},{1,9},{2,10},{3,11},{4,12},{5,13},{6,14},{7,15},{8,0},{9,1},... | collective-permute-start | bytes 1572872 | tf_op jit(solution)/shard_map/ppermute | solution.py:36
  41.5 8.6 %collective-permute-done.3 = bf16[2,4,8,4096]{3,2,0,1:T(8,128)(2,1)S(1)} collective-permute-done((bf16[2,4,8,4096]{3,2,0,1:T(8,128)(2,1)S(1)}, bf16[2,4,8,4096]{3,2,0,1:T(8,128)(2,1)S(1)}, u32[]{:S(2)}, u32[]{:S(2)}) %collective-permute-start.3) | collective-permute-done | bytes 524320 | tf_op jit(solution)/shard_map/ppermute | solution.py:36
  53.3 2.2 %collective-permute-start.5 = (bf16[2,8,4096]{2,1,0:T(8,128)(2,1)S(1)}, bf16[2,8,4096]{2,1,0:T(8,128)(2,1)S(1)}, u32[]{:S(2)}, u32[]{:S(2)}) collective-permute-start(bf16[2,8,4096]{2,1,0:T(8,128)(2,1)S(1)} %get-tuple-element.19), channel_id=1, source_target_pairs={{0,12},{1,13},{2,14},{3,15},{4,0},{5,1},{6,2},{7,3},{8,4},{9,5},{1... | collective-permute-start | bytes 393224 | tf_op jit(solution)/shard_map/ppermute | solution.py:36
  59.0 2.3 %collective-permute-start.11 = (bf16[2,8,4096]{2,1,0:T(8,128)(2,1)S(1)}, bf16[2,8,4096]{2,1,0:T(8,128)(2,1)S(1)}, u32[]{:S(2)}, u32[]{:S(2)}) collective-permute-start(bf16[2,8,4096]{2,1,0:T(8,128)(2,1)S(1)} %get-tuple-element.22), channel_id=1, source_target_pairs={{0,48},{1,49},{2,50},{3,51},{4,52},{5,53},{6,54},{7,55},{8,56},{9,... | collective-permute-start | bytes 393224 | tf_op jit(solution)/shard_map/ppermute | solution.py:36
  64.4 3.6 %collective-permute-done.12 = bf16[2,8,4096]{2,1,0:T(8,128)(2,1)S(1)} collective-permute-done((bf16[2,8,4096]{2,1,0:T(8,128)(2,1)S(1)}, bf16[2,8,4096]{2,1,0:T(8,128)(2,1)S(1)}, u32[]{:S(2)}, u32[]{:S(2)}) %collective-permute-start.12) | collective-permute-done | bytes 131104 | tf_op jit(solution)/shard_map/ppermute | solution.py:36
  68.2 3.0 %collective-permute-start.13 = (bf16[8,8192]{1,0:T(8,128)(2,1)S(1)}, bf16[8,8192]{1,0:T(8,128)(2,1)S(1)}, u32[]{:S(2)}, u32[]{:S(2)}) collective-permute-start(bf16[8,8192]{1,0:T(8,128)(2,1)S(1)} %get-tuple-element.29), channel_id=1, source_target_pairs={{0,2},{1,3},{2,0},{3,1},{4,6},{5,7},{6,4},{7,5},{8,10},{9,11},{10,... | collective-permute-start | bytes 393224 | tf_op jit(solution)/shard_map/ppermute | solution.py:36
  71.6 2.3 %collective-permute-start.15 = (bf16[8,8192]{1,0:T(8,128)(2,1)S(1)}, bf16[8,8192]{1,0:T(8,128)(2,1)S(1)}, u32[]{:S(2)}, u32[]{:S(2)}) collective-permute-start(bf16[8,8192]{1,0:T(8,128)(2,1)S(1)} %get-tuple-element.30), channel_id=1, source_target_pairs={{0,66},{1,67},{2,64},{3,65},{4,70},{5,71},{6,68},{7,69},{8,74},{9,... | collective-permute-start | bytes 393224 | tf_op jit(solution)/shard_map/ppermute | solution.py:36
  73.8 3.8 %collective-permute-done.14 = bf16[8,8192]{1,0:T(8,128)(2,1)S(1)} collective-permute-done((bf16[8,8192]{1,0:T(8,128)(2,1)S(1)}, bf16[8,8192]{1,0:T(8,128)(2,1)S(1)}, u32[]{:S(2)}, u32[]{:S(2)}) %collective-permute-start.14) | collective-permute-done | bytes 131104 | tf_op jit(solution)/shard_map/ppermute | solution.py:36
  81.3 3.5 %collective-permute-done.24 = bf16[8,8192]{1,0:T(8,128)(2,1)S(1)} collective-permute-done((bf16[8,8192]{1,0:T(8,128)(2,1)S(1)}, bf16[8,8192]{1,0:T(8,128)(2,1)S(1)}, u32[]{:S(2)}, u32[]{:S(2)}) %collective-permute-start.24) | collective-permute-done | bytes 131104 | tf_op jit(solution)/shard_map/ppermute | solution.py:36
  86.4 4.7 %collective-permute-start.27 = (bf16[32,8192]{1,0:T(8,128)(2,1)}, bf16[32,8192]{1,0:T(8,128)(2,1)S(1)}, u32[]{:S(2)}, u32[]{:S(2)}) collective-permute-start(bf16[32,8192]{1,0:T(8,128)(2,1)} %maximum_bitcast_fusion), channel_id=1, source_target_pairs={{0,1},{1,0},{2,3},{3,2},{4,5},{5,4},{6,7},{7,6},{8,9},{9,8},{10,11... | collective-permute-start | bytes 1572872 | tf_op jit(solution)/shard_map/ppermute | solution.py:36
  91.0 2.7 %fusion.3 = bf16[2,32,8192]{2,1,0:T(8,128)(2,1)} fusion(f32[2,32,8192]{2,1,0:T(8,128)S(1)} %copy-done, f32[1,2,32,8192]{3,2,1,0:T(8,128)} %param.9), kind=kLoop, calls=%fused_computation.9 | loop fusion | flops 1048576 | bytes 5242880 | tf_op jit(solution)/shard_map/convert_element_type | solution.py:48
  97.6 4.4 %collective-permute-done.16 = f32[1,1]{1,0:T(1,128)} collective-permute-done((f32[1,1]{1,0:T(1,128)}, f32[1,1]{1,0:T(1,128)}, u32[]{:S(2)}, u32[]{:S(2)}) %collective-permute-start.16) | collective-permute-done | bytes 36 | tf_op jit(solution)/shard_map/ppermute | solution.py:36
  105.9 2.9 %collective-permute-start.21 = (f32[1,1]{1,0:T(1,128)}, f32[1,1]{1,0:T(1,128)}, u32[]{:S(2)}, u32[]{:S(2)}) collective-permute-start(f32[1,1]{1,0:T(1,128)} %add.283), channel_id=1, source_target_pairs={{0,12},{1,13},{2,14},{3,15},{4,0},{5,1},{6,2},{7,3},{8,4},{9,5},{1... | collective-permute-start | bytes 20 | tf_op jit(solution)/shard_map/ppermute | solution.py:36
  110.4 2.4 %collective-permute-done.19 = f32[1,1]{1,0:T(1,128)} collective-permute-done((f32[1,1]{1,0:T(1,128)}, f32[1,1]{1,0:T(1,128)}, u32[]{:S(2)}, u32[]{:S(2)}) %collective-permute-start.19) | collective-permute-done | bytes 36 | tf_op jit(solution)/shard_map/ppermute | solution.py:36
  114.7 4.3 %collective-permute-start.22 = (f32[1,1]{1,0:T(1,128)}, f32[1,1]{1,0:T(1,128)}, u32[]{:S(2)}, u32[]{:S(2)}) collective-permute-start(f32[1,1]{1,0:T(1,128)} %add.286), channel_id=1, source_target_pairs={{0,1},{1,0},{2,3},{3,2},{4,5},{5,4},{6,7},{7,6},{8,9},{9,8},{10,11... | collective-permute-start | bytes 20 | tf_op jit(solution)/shard_map/ppermute | solution.py:36
  123.2 5.5 %convert_add_fusion.1 = (f32[2,32,8192]{2,1,0:T(8,128)S(1)}, f32[2,32,8192]{2,1,0:T(8,128)}, f32[2,32,8192]{2,1,0:T(8,128)}) fusion(bf16[2,32,8192]{2,1,0:T(8,128)(2,1)} %collective-permute-done.28, f32[2,32,8192]{2,1,0:T(8,128)S(1)} %copy-done, bf16[1,32,8192]{2,1,0:T(8,128)(2,1)S(1)} %get-tuple-element.16, bf16[1,32,8192]{2,1,0:T(8,128)(2,1)S(1)} %get-tuple-element.15, ...), kind=kLoop, calls=%fused_computation.11 | loop fusion | flops 8912896 | bytes 14680068 | tf_op jit(solution)/shard_map/add | solution.py:108
  132.4 2.7 %reshape.53 = f32[1,2,32,8192]{3,2,1,0:T(8,128)} reshape(f32[2,32,64,128]{3,2,1,0:T(8,128)} %convert_multiply_fusion) | data formatting | bytes 4194304 | tf_op jit(solution)/shard_map/reshape | solution.py:113
  135.2 4.5 %fusion.33 = f32[2,32,8192]{2,1,0:T(8,128)} fusion(f32[2,32,8192]{2,1,0:T(8,128)S(1)} %copy-done, f32[2,32,8192]{2,1,0:T(8,128)} %get-tuple-element.6, f32[2,32,8192]{2,1,0:T(8,128)} %get-tuple-element.5), kind=kLoop, calls=%fused_computation.84 | loop fusion | flops 3145728 | bytes 8388608 | tf_op jit(solution)/shard_map/add | solution.py:107
  (73 shorter events, 40.3 us)
Async XLA Ops:
  5.2 8.6 %collective-permute-start = (bf16[256,8192]{1,0:T(8,128)(2,1)}, bf16[256,8192]{1,0:T(8,128)(2,1)}, u32[]{:S(2)}, u32[]{:S(2)}) collective-permute-start(bf16[256,8192]{1,0:T(8,128)(2,1)} %dynamic-slice_bitcast_fusion), channel_id=1, source_target_pairs={{0,1},{1,0},{2,3},{3,2},{4,5},{5,4},{6,7},{7,6},{8,9},{9,8},{10,11... | collective-permute-start | bytes 12582920 | tf_op jit(solution)/shard_map/ppermute | solution.py:36
  23.4 14.3 %collective-permute-start.1 = (bf16[2,4,8,4096]{3,2,0,1:T(8,128)(2,1)S(1)}, bf16[2,4,8,4096]{3,2,0,1:T(8,128)(2,1)S(1)}, u32[]{:S(2)}, u32[]{:S(2)}) collective-permute-start(bf16[2,4,8,4096]{3,2,0,1:T(8,128)(2,1)S(1)} %bitcast.107), channel_id=1, source_target_pairs={{0,16},{1,17},{2,18},{3,19},{4,20},{5,21},{6,22},{7,23},{8,24},{9,... | collective-permute-start | bytes 1572872 | tf_op jit(solution)/shard_map/ppermute | solution.py:36
  24.8 16.7 %collective-permute-start.2 = (bf16[2,4,8,4096]{3,2,0,1:T(8,128)(2,1)S(1)}, bf16[2,4,8,4096]{3,2,0,1:T(8,128)(2,1)S(1)}, u32[]{:S(2)}, u32[]{:S(2)}) collective-permute-start(bf16[2,4,8,4096]{3,2,0,1:T(8,128)(2,1)S(1)} %bitcast.106), channel_id=1, source_target_pairs={{0,48},{1,49},{2,50},{3,51},{4,52},{5,53},{6,54},{7,55},{8,56},{9,... | collective-permute-start | bytes 1572872 | tf_op jit(solution)/shard_map/ppermute | solution.py:36
  26.3 23.8 %collective-permute-start.3 = (bf16[2,4,8,4096]{3,2,0,1:T(8,128)(2,1)S(1)}, bf16[2,4,8,4096]{3,2,0,1:T(8,128)(2,1)S(1)}, u32[]{:S(2)}, u32[]{:S(2)}) collective-permute-start(bf16[2,4,8,4096]{3,2,0,1:T(8,128)(2,1)S(1)} %bitcast.108), channel_id=1, source_target_pairs={{0,32},{1,33},{2,34},{3,35},{4,36},{5,37},{6,38},{7,39},{8,40},{9,... | collective-permute-start | bytes 1572872 | tf_op jit(solution)/shard_map/ppermute | solution.py:36
  30.1 25.4 %collective-permute-start.7 = (bf16[2,4,8,4096]{3,2,0,1:T(8,128)(2,1)S(1)}, bf16[2,4,8,4096]{3,2,0,1:T(8,128)(2,1)S(1)}, u32[]{:S(2)}, u32[]{:S(2)}) collective-permute-start(bf16[2,4,8,4096]{3,2,0,1:T(8,128)(2,1)S(1)} %bitcast.110), channel_id=1, source_target_pairs={{0,4},{1,5},{2,6},{3,7},{4,8},{5,9},{6,10},{7,11},{8,12},{9,13},{1... | collective-permute-start | bytes 1572872 | tf_op jit(solution)/shard_map/ppermute | solution.py:36
  31.8 24.9 %collective-permute-start.8 = (bf16[2,4,8,4096]{3,2,0,1:T(8,128)(2,1)S(1)}, bf16[2,4,8,4096]{3,2,0,1:T(8,128)(2,1)S(1)}, u32[]{:S(2)}, u32[]{:S(2)}) collective-permute-start(bf16[2,4,8,4096]{3,2,0,1:T(8,128)(2,1)S(1)} %bitcast.109), channel_id=1, source_target_pairs={{0,12},{1,13},{2,14},{3,15},{4,0},{5,1},{6,2},{7,3},{8,4},{9,5},{1... | collective-permute-start | bytes 1572872 | tf_op jit(solution)/shard_map/ppermute | solution.py:36
  37.8 19.3 %collective-permute-start.9 = (bf16[2,4,8,4096]{3,2,0,1:T(8,128)(2,1)S(1)}, bf16[2,4,8,4096]{3,2,0,1:T(8,128)(2,1)S(1)}, u32[]{:S(2)}, u32[]{:S(2)}) collective-permute-start(bf16[2,4,8,4096]{3,2,0,1:T(8,128)(2,1)S(1)} %bitcast.111), channel_id=1, source_target_pairs={{0,8},{1,9},{2,10},{3,11},{4,12},{5,13},{6,14},{7,15},{8,0},{9,1},... | collective-permute-start | bytes 1572872 | tf_op jit(solution)/shard_map/ppermute | solution.py:36
  51.6 10.7 %collective-permute-start.4 = (bf16[2,8,4096]{2,1,0:T(8,128)(2,1)S(1)}, bf16[2,8,4096]{2,1,0:T(8,128)(2,1)S(1)}, u32[]{:S(2)}, u32[]{:S(2)}) collective-permute-start(bf16[2,8,4096]{2,1,0:T(8,128)(2,1)S(1)} %get-tuple-element.17), channel_id=1, source_target_pairs={{0,4},{1,5},{2,6},{3,7},{4,8},{5,9},{6,10},{7,11},{8,12},{9,13},{1... | collective-permute-start | bytes 393224 | tf_op jit(solution)/shard_map/ppermute | solution.py:36
  53.3 11.0 %collective-permute-start.5 = (bf16[2,8,4096]{2,1,0:T(8,128)(2,1)S(1)}, bf16[2,8,4096]{2,1,0:T(8,128)(2,1)S(1)}, u32[]{:S(2)}, u32[]{:S(2)}) collective-permute-start(bf16[2,8,4096]{2,1,0:T(8,128)(2,1)S(1)} %get-tuple-element.19), channel_id=1, source_target_pairs={{0,12},{1,13},{2,14},{3,15},{4,0},{5,1},{6,2},{7,3},{8,4},{9,5},{1... | collective-permute-start | bytes 393224 | tf_op jit(solution)/shard_map/ppermute | solution.py:36
  55.5 8.8 %collective-permute-start.6 = (bf16[2,8,4096]{2,1,0:T(8,128)(2,1)S(1)}, bf16[2,8,4096]{2,1,0:T(8,128)(2,1)S(1)}, u32[]{:S(2)}, u32[]{:S(2)}) collective-permute-start(bf16[2,8,4096]{2,1,0:T(8,128)(2,1)S(1)} %get-tuple-element.18), channel_id=1, source_target_pairs={{0,8},{1,9},{2,10},{3,11},{4,12},{5,13},{6,14},{7,15},{8,0},{9,1},... | collective-permute-start | bytes 393224 | tf_op jit(solution)/shard_map/ppermute | solution.py:36
  58.6 5.8 %collective-permute-start.10 = (bf16[2,8,4096]{2,1,0:T(8,128)(2,1)S(1)}, bf16[2,8,4096]{2,1,0:T(8,128)(2,1)S(1)}, u32[]{:S(2)}, u32[]{:S(2)}) collective-permute-start(bf16[2,8,4096]{2,1,0:T(8,128)(2,1)S(1)} %get-tuple-element.20), channel_id=1, source_target_pairs={{0,16},{1,17},{2,18},{3,19},{4,20},{5,21},{6,22},{7,23},{8,24},{9,... | collective-permute-start | bytes 393224 | tf_op jit(solution)/shard_map/ppermute | solution.py:36
  62.3 5.8 %collective-permute-start.12 = (bf16[2,8,4096]{2,1,0:T(8,128)(2,1)S(1)}, bf16[2,8,4096]{2,1,0:T(8,128)(2,1)S(1)}, u32[]{:S(2)}, u32[]{:S(2)}) collective-permute-start(bf16[2,8,4096]{2,1,0:T(8,128)(2,1)S(1)} %get-tuple-element.21), channel_id=1, source_target_pairs={{0,32},{1,33},{2,34},{3,35},{4,36},{5,37},{6,38},{7,39},{8,40},{9,... | collective-permute-start | bytes 393224 | tf_op jit(solution)/shard_map/ppermute | solution.py:36
  68.2 5.7 %collective-permute-start.13 = (bf16[8,8192]{1,0:T(8,128)(2,1)S(1)}, bf16[8,8192]{1,0:T(8,128)(2,1)S(1)}, u32[]{:S(2)}, u32[]{:S(2)}) collective-permute-start(bf16[8,8192]{1,0:T(8,128)(2,1)S(1)} %get-tuple-element.29), channel_id=1, source_target_pairs={{0,2},{1,3},{2,0},{3,1},{4,6},{5,7},{6,4},{7,5},{8,10},{9,11},{10,... | collective-permute-start | bytes 393224 | tf_op jit(solution)/shard_map/ppermute | solution.py:36
  71.2 6.5 %collective-permute-start.14 = (bf16[8,8192]{1,0:T(8,128)(2,1)S(1)}, bf16[8,8192]{1,0:T(8,128)(2,1)S(1)}, u32[]{:S(2)}, u32[]{:S(2)}) collective-permute-start(bf16[8,8192]{1,0:T(8,128)(2,1)S(1)} %get-tuple-element.30), channel_id=1, source_target_pairs={{0,64},{1,65},{2,66},{3,67},{4,68},{5,69},{6,70},{7,71},{8,72},{9,... | collective-permute-start | bytes 393224 | tf_op jit(solution)/shard_map/ppermute | solution.py:36
  71.6 6.1 %collective-permute-start.15 = (bf16[8,8192]{1,0:T(8,128)(2,1)S(1)}, bf16[8,8192]{1,0:T(8,128)(2,1)S(1)}, u32[]{:S(2)}, u32[]{:S(2)}) collective-permute-start(bf16[8,8192]{1,0:T(8,128)(2,1)S(1)} %get-tuple-element.30), channel_id=1, source_target_pairs={{0,66},{1,67},{2,64},{3,65},{4,70},{5,71},{6,68},{7,69},{8,74},{9,... | collective-permute-start | bytes 393224 | tf_op jit(solution)/shard_map/ppermute | solution.py:36
  78.4 6.4 %collective-permute-start.24 = (bf16[8,8192]{1,0:T(8,128)(2,1)S(1)}, bf16[8,8192]{1,0:T(8,128)(2,1)S(1)}, u32[]{:S(2)}, u32[]{:S(2)}) collective-permute-start(bf16[8,8192]{1,0:T(8,128)(2,1)S(1)} %get-tuple-element.24), channel_id=1, source_target_pairs={{0,4},{1,5},{2,6},{3,7},{4,8},{5,9},{6,10},{7,11},{8,12},{9,13},{1... | collective-permute-start | bytes 393224 | tf_op jit(solution)/shard_map/ppermute | solution.py:36
  78.4 6.4 %collective-permute-start.25 = (bf16[8,8192]{1,0:T(8,128)(2,1)S(1)}, bf16[8,8192]{1,0:T(8,128)(2,1)S(1)}, u32[]{:S(2)}, u32[]{:S(2)}) collective-permute-start(bf16[8,8192]{1,0:T(8,128)(2,1)S(1)} %get-tuple-element.24), channel_id=1, source_target_pairs={{0,8},{1,9},{2,10},{3,11},{4,12},{5,13},{6,14},{7,15},{8,0},{9,1},... | collective-permute-start | bytes 393224 | tf_op jit(solution)/shard_map/ppermute | solution.py:36
  79.3 6.1 %collective-permute-start.26 = (bf16[8,8192]{1,0:T(8,128)(2,1)S(1)}, bf16[8,8192]{1,0:T(8,128)(2,1)S(1)}, u32[]{:S(2)}, u32[]{:S(2)}) collective-permute-start(bf16[8,8192]{1,0:T(8,128)(2,1)S(1)} %get-tuple-element.24), channel_id=1, source_target_pairs={{0,12},{1,13},{2,14},{3,15},{4,0},{5,1},{6,2},{7,3},{8,4},{9,5},{1... | collective-permute-start | bytes 393224 | tf_op jit(solution)/shard_map/ppermute | solution.py:36
  86.4 36.7 %collective-permute-start.27 = (bf16[32,8192]{1,0:T(8,128)(2,1)}, bf16[32,8192]{1,0:T(8,128)(2,1)S(1)}, u32[]{:S(2)}, u32[]{:S(2)}) collective-permute-start(bf16[32,8192]{1,0:T(8,128)(2,1)} %maximum_bitcast_fusion), channel_id=1, source_target_pairs={{0,1},{1,0},{2,3},{3,2},{4,5},{5,4},{6,7},{7,6},{8,9},{9,8},{10,11... | collective-permute-start | bytes 1572872 | tf_op jit(solution)/shard_map/ppermute | solution.py:36
  93.8 29.4 %collective-permute-start.28 = (bf16[2,32,8192]{2,1,0:T(8,128)(2,1)}, bf16[2,32,8192]{2,1,0:T(8,128)(2,1)}, u32[]{:S(2)}, u32[]{:S(2)}) collective-permute-start(bf16[2,32,8192]{2,1,0:T(8,128)(2,1)} %fusion.3), channel_id=1, source_target_pairs={{0,1},{1,2},{2,3},{3,4},{4,5},{5,6},{6,7},{7,8},{8,9},{9,10},{10,1... | collective-permute-start | bytes 3145736 | tf_op jit(solution)/shard_map/ppermute | solution.py:69
  94.9 8.4 %collective-permute-start.17 = (f32[1,1]{1,0:T(1,128)}, f32[1,1]{1,0:T(1,128)}, u32[]{:S(2)}, u32[]{:S(2)}) collective-permute-start(f32[1,1]{1,0:T(1,128)} %bitcast.21), channel_id=1, source_target_pairs={{0,16},{1,17},{2,18},{3,19},{4,20},{5,21},{6,22},{7,23},{8,24},{9,... | collective-permute-start | bytes 20 | tf_op jit(solution)/shard_map/ppermute | solution.py:36
  95.4 7.8 %collective-permute-start.18 = (f32[1,1]{1,0:T(1,128)}, f32[1,1]{1,0:T(1,128)}, u32[]{:S(2)}, u32[]{:S(2)}) collective-permute-start(f32[1,1]{1,0:T(1,128)} %bitcast.21), channel_id=1, source_target_pairs={{0,48},{1,49},{2,50},{3,51},{4,52},{5,53},{6,54},{7,55},{8,56},{9,... | collective-permute-start | bytes 20 | tf_op jit(solution)/shard_map/ppermute | solution.py:36
  104.6 8.8 %collective-permute-start.20 = (f32[1,1]{1,0:T(1,128)}, f32[1,1]{1,0:T(1,128)}, u32[]{:S(2)}, u32[]{:S(2)}) collective-permute-start(f32[1,1]{1,0:T(1,128)} %add.283), channel_id=1, source_target_pairs={{0,4},{1,5},{2,6},{3,7},{4,8},{5,9},{6,10},{7,11},{8,12},{9,13},{1... | collective-permute-start | bytes 20 | tf_op jit(solution)/shard_map/ppermute | solution.py:36
  105.9 7.5 %collective-permute-start.21 = (f32[1,1]{1,0:T(1,128)}, f32[1,1]{1,0:T(1,128)}, u32[]{:S(2)}, u32[]{:S(2)}) collective-permute-start(f32[1,1]{1,0:T(1,128)} %add.283), channel_id=1, source_target_pairs={{0,12},{1,13},{2,14},{3,15},{4,0},{5,1},{6,2},{7,3},{8,4},{9,5},{1... | collective-permute-start | bytes 20 | tf_op jit(solution)/shard_map/ppermute | solution.py:36
  (8 other events, 74.0 us)

commit v2 on v0

v2 whole, which is shorter than its diff:
```python
import jax
import jax.numpy as jnp
from jax import lax
from jax.experimental import pallas as pl
from jax.experimental.pallas import tpu as pltpu
from jax.sharding import Mesh, PartitionSpec as P

QBLOCK = 128
AXES = ("yl", "x", "z", "yh", "c")
FSDP = ("yl", "x")
REP = ("z", "yh", "c")
MIB = 1 << 20

beta_first = 0.9
beta_second = 0.95
learn_rate = 0.02
decay_rate = 0.1
adam_eps = 1e-08
scale_eps = 1e-06
rms_eps = 1e-06

BF16 = jnp.bfloat16
F32 = jnp.float32


def spots():
    return [
        (x, yl + 2 * yh, z, c)
        for yl in range(2)
        for x in range(4)
        for z in range(4)
        for yh in range(2)
        for c in range(2)
    ]


def rank(x, y, z, c):
    x, y, z, c = x % 4, y % 4, z % 4, c % 2
    return ((y % 2) * 4 + x) * 16 + z * 4 + (y // 2) * 2 + c


def move(value, x=0, y=0, z=0, c=0):
    pairs = [(rank(*s), rank(s[0] + x, s[1] + y, s[2] + z, s[3] + c)) for s in spots()]
    return lax.ppermute(value, AXES, pairs)


def swap_x(value, mask):
    pairs = [(rank(*s), rank(s[0] ^ mask, *s[1:])) for s in spots()]
    return lax.ppermute(value, AXES, pairs)


def move_yl(value, c=0):
    pairs = [(rank(*s), rank(s[0], s[1] ^ 1, s[2], s[3] + c)) for s in spots()]
    return lax.ppermute(value, AXES, pairs)


def wide(value):
    return value.astype(F32)


def narrow(value):
    return value.astype(BF16)


def vmem_call(body, where, arrays, outs, after=()):
    count = len(arrays)

    def run(where, *refs):
        body(where, *refs[:count], *refs[count + len(after) :])

    arrays = [pltpu.with_memory_space_constraint(a, pltpu.VMEM) for a in arrays]
    return pl.pallas_call(
        run,
        in_specs=[pl.BlockSpec(memory_space=pltpu.SMEM)]
        + [pl.BlockSpec(memory_space=pltpu.VMEM)] * count
        + [pl.BlockSpec(memory_space=pl.ANY)] * len(after),
        out_specs=[pl.BlockSpec(memory_space=pltpu.VMEM)] * len(outs),
        out_shape=[pltpu.VMEM(dims, kind) for dims, kind in outs],
        compiler_params=pltpu.CompilerParams(vmem_limit_bytes=12 * MIB),
        cost_estimate=pl.CostEstimate(flops=4 * MIB, bytes_accessed=4 * MIB, transcendentals=0),
    )(where, *arrays, *after)


LEFT = (2, 16, 10240)
RIGHT = (8, 16, 1536)
ORDER = (0, 2, 1, 3)

X, YL, Z, C = range(4)


def fetch(grads, where, wanted, after=()):
    def body(where, src, *refs):
        outs, sems = refs[len(after) : -1], refs[-1]
        copies = []
        for out, (own, left, offsets) in zip(outs, wanted):
            layer = where[C] if own else 1 - where[C]
            for i, k in enumerate(offsets):
                if left:
                    row = (where[X] + k) % 4
                    for f in range(2):
                        src_row, dst_row = src.at[layer, f, row], out.at[i, f]
                        copies.append((src_row.at[pl.ds(0, 16)], dst_row.at[:, pl.ds(0, 8192)]))
                        for part in range(4):
                            thin = pl.ds(2048 * part + 1536, 512)
                            to = pl.ds(8192 + 512 * part, 512)
                            copies.append((src_row.at[pl.ds(16, 16), thin], dst_row.at[:, to]))
                else:
                    cols = pl.ds(pl.multiple_of((where[Z] + k) % 4 * 2048, 2048), 1536)
                    for f in range(8):
                        copies.append(
                            (src.at[layer, f // 4, f % 4, pl.ds(16, 16), cols], out.at[i, f])
                        )
        copies = [pltpu.make_async_copy(a, b, sems.at[i]) for i, (a, b) in enumerate(copies)]
        for copy in copies:
            copy.start()
        for copy in copies:
            copy.wait()

    blocks = sum(len(offsets) for _, _, offsets in wanted)
    grads = pltpu.with_memory_space_constraint(grads.reshape(2, 2, 4, 32, 8192), pltpu.HBM)
    return pl.pallas_call(
        body,
        in_specs=[pl.BlockSpec(memory_space=pltpu.SMEM)]
        + [pl.BlockSpec(memory_space=pl.ANY)] * (1 + len(after)),
        out_specs=[pl.BlockSpec(memory_space=pl.ANY)] * len(wanted),
        out_shape=[
            pltpu.VMEM((len(offsets),) + (LEFT if left else RIGHT), BF16)
            for _, left, offsets in wanted
        ],
        scratch_shapes=[pltpu.SemaphoreType.DMA((16 * blocks,))],
        compiler_params=pltpu.CompilerParams(vmem_limit_bytes=4 * MIB),
        cost_estimate=pl.CostEstimate(flops=0, bytes_accessed=blocks * MIB, transcendentals=0),
    )(where, grads, *after)


def preload(arrays, where, before):
    count = len(arrays)

    def body(where, *refs):
        ins, outs, sems = refs[:count], refs[count + 1 : -1], refs[-1]
        copies = [
            pltpu.make_async_copy(
                a.at[l, pl.ds(8 * r, 8)], b.at[l, pl.ds(8 * r, 8)], sems.at[i, l, r]
            )
            for i, (a, b) in enumerate(zip(ins, outs))
            for l in range(2)
            for r in range(4)
        ]
        for copy in copies:
            copy.start()
        for copy in copies:
            copy.wait()

    arrays = [pltpu.with_memory_space_constraint(a, pltpu.HBM) for a in arrays]
    return pl.pallas_call(
        body,
        in_specs=[pl.BlockSpec(memory_space=pltpu.SMEM)]
        + [pl.BlockSpec(memory_space=pl.ANY)] * (count + 1),
        out_specs=[pl.BlockSpec(memory_space=pl.ANY)] * count,
        out_shape=[pltpu.VMEM(a.shape, a.dtype) for a in arrays],
        scratch_shapes=[pltpu.SemaphoreType.DMA((count, 2, 4))],
        compiler_params=pltpu.CompilerParams(vmem_limit_bytes=4 * MIB),
        cost_estimate=pl.CostEstimate(flops=MIB, bytes_accessed=6 * MIB, transcendentals=0),
    )(where, *arrays, before)


def add(*terms):
    total = terms[0]
    for t in terms[1:]:
        total = total + t
    return total


def total_of(refs, *index):
    return add(*[wide(r[index] if index else r[...]) for r in refs])


def pair_sum(where, mine, theirs, after=()):
    dims = mine.shape[1:]

    def body(where, a, b, *outs):
        for i, out in enumerate(outs):
            out[...] = narrow(wide(a[i]) + wide(b[i]))

    return list(vmem_call(body, where, (mine, theirs), [(dims, BF16)] * 3, after))


def split(where, arrays, whole, cut, width, after=()):
    dims = (2, 16, width)
    count = len(arrays)

    def body(where, *refs):
        ins = list(refs[:count]) + [r.at[3] for r in refs[count:-4]]
        for out, k in zip(refs[-4:], ORDER):
            for first, last, index in cut(where, k):
                out[:, :, first:last] = total_of(ins, *index).astype(out.dtype)

    outs = [(dims, F32)] + [(dims, BF16)] * 3
    return list(vmem_call(body, where, list(arrays) + whole, outs, after))


def travel(blocks, name):
    return [move(b, **{name: k}) for k, b in zip(ORDER[1:], blocks)]


def update(where, layer, j, pieces, state, outs):
    sq, p, m, v, base = state
    clip_factor = lax.rsqrt(sq[0:1, 0:1] / (2 * 256 * 8192) + rms_eps)
    place = (where[Z] - j + 4) % 4
    for g in range(2048 // QBLOCK):
        cols = pl.ds(pl.multiple_of(j * 2048 + g * QBLOCK, QBLOCK), QBLOCK)
        clipped = clip_factor * wide(pieces[place, :, g * QBLOCK : (g + 1) * QBLOCK])
        new_m = beta_first * m[layer, :, cols] + (1.0 - beta_first) * clipped
        new_v = beta_second * v[layer, :, cols] + (1.0 - beta_second) * clipped * clipped
        old = p[layer, :, cols]
        change = -learn_rate * (new_m / (jnp.sqrt(new_v) + adam_eps) + decay_rate * old)
        outs[0][:, cols] = old + change
        outs[1][:, cols] = new_m
        outs[2][:, cols] = new_v
        delta = change + wide(base[layer, :, cols])
        scale = jnp.max(jnp.abs(delta), axis=1, keepdims=True) + scale_eps
        scale = wide(narrow(scale))
        outs[3][:, cols] = wide(narrow(delta / scale)) * scale


def update_all(where, ours, theirs, state):
    def body(where, ours, theirs, *refs):
        state, outs, held, sems = refs[:5], refs[5:9], refs[9:13], refs[13]

        def copies(side, j):
            layer = where[C] if side == 0 else 1 - where[C]
            cols = pl.ds(pl.multiple_of(j * 2048, 2048), 2048)
            return [
                pltpu.make_async_copy(
                    held[i].at[side, :, cols], outs[i].at[layer, :, cols], sems.at[i, side, j]
                )
                for i in range(4)
            ]

        for side, pieces in enumerate((ours, theirs)):

            @pl.loop(0, 4)
            def _(j, side=side, pieces=pieces):
                layer = where[C] if side == 0 else 1 - where[C]
                update(where, layer, j, pieces, state, [h.at[side] for h in held])
                for copy in copies(side, j):
                    copy.start()

        for side in range(2):
            for j in range(4):
                for copy in copies(side, j):
                    copy.wait()

    arrays = [pltpu.with_memory_space_constraint(a, pltpu.VMEM) for a in [ours, theirs, *state]]
    return pl.pallas_call(
        body,
        in_specs=[pl.BlockSpec(memory_space=pltpu.SMEM)]
        + [pl.BlockSpec(memory_space=pltpu.VMEM)] * len(arrays),
        out_specs=[pl.BlockSpec(memory_space=pl.ANY)] * 4,
        out_shape=[pltpu.HBM((2, 32, 8192), F32)] * 4,
        scratch_shapes=[pltpu.VMEM((2, 32, 8192), F32)] * 4 + [pltpu.SemaphoreType.DMA((4, 2, 4))],
        compiler_params=pltpu.CompilerParams(vmem_limit_bytes=14 * MIB),
        cost_estimate=pl.CostEstimate(flops=9 * MIB, bytes_accessed=9 * MIB, transcendentals=0),
    )(where, *arrays)


def local(partial_grads, params, moment, second_moment, snapshot):
    where = jnp.stack([lax.axis_index(name) for name in ("x", "yl", "z", "c")]).astype(jnp.int32)
    grads = partial_grads[0, 0]

    order = ORDER[1:] + (0,)
    theirs = fetch(grads, where, [(False, True, order)])
    theirs += fetch(grads, where, [(False, False, order)], theirs)
    theirs = [move(b, c=1) for b in theirs]
    base = narrow(params - snapshot[0])
    held_base = lax.ppermute(base, REP, [(i, (i + 1) % 16) for i in range(16)])
    mine = fetch(grads, where, [(True, True, order)], (base,))
    left = pair_sum(where, mine[0], theirs[0])
    mine += fetch(grads, where, [(True, False, order)], (left[0],))
    right = pair_sum(where, mine[1], theirs[1], (held_base,))
    state = preload([params, moment, second_moment], where, right[0])
    left = travel(left, "x")
    right = travel(right, "z")

    def by_z(where, k):
        block = (where[Z] + k) % 4
        wide_part = pl.ds(pl.multiple_of(block * 2048, 2048), 2048)
        thin_part = pl.ds(pl.multiple_of(8192 + block * 512, 512), 512)
        every = slice(None)
        return (0, 2048, (every, every, wide_part)), (2048, 2560, (every, every, thin_part))

    def by_x(where, k):
        return ((0, 1536, (slice(None), (where[X] + k) % 4)),)

    left = split(where, left, [mine[0], theirs[0]], by_z, 2560, (state[0],))
    ready = left[1]
    left = left[:1] + travel(left[1:], "z")
    whole = [a.reshape(4, 2, 4, 16, 1536) for a in (mine[1], theirs[1])]
    right = split(where, [r.reshape(2, 4, 16, 1536) for r in right], whole, by_x, 1536, (ready,))
    right = right[:1] + travel(right[1:], "x")

    def join(where, *refs):
        for out, index in ((refs[8], where[YL]), (refs[9], 1 - where[YL])):
            a = narrow(total_of(refs[:4], index))
            out[:16, :] = a[:, :2048]
            out[16:, :1536] = narrow(total_of(refs[4:8], index))
            out[16:, 1536:] = a[:, 2048:]

    mine, other = vmem_call(join, where, left + right, [((32, 2048), BF16)] * 2)
    fourth = [mine, move(mine, y=2), move(other, y=1), move(other, y=3)]

    def finish(where, a, b, d, e, out):
        total = (wide(a[...]) + wide(b[...])) + (wide(d[...]) + wide(e[...]))
        squares = jnp.sum(jnp.sum(total * total, axis=0, keepdims=True), axis=1, keepdims=True)
        out[:, :2048] = narrow(total)
        high = wide(narrow(squares))
        middle = wide(narrow(squares - high))
        low = squares - high - middle
        lane = lax.broadcasted_iota(jnp.int32, (32, 128), 1)
        tail = jnp.where(lane == 0, high, jnp.where(lane == 1, middle, jnp.where(lane == 2, low, 0.0)))
        out[:, 2048:] = narrow(tail)

    piece = vmem_call(finish, where, fourth, [((32, 2176), BF16)])[0]
    ring = [piece] + [move(piece, z=k) for k in (2, 1, 3)]

    def gather(where, *refs):
        ins, out, squares = refs[:4], refs[4], refs[5]
        parts = [jnp.sum(wide(ref[:16, 2048:])[:8, :], axis=1, keepdims=True) for ref in ins]
        for k, ref in zip(ORDER, ins):
            out[k] = ref[:, :2048]
        total = (parts[0] + parts[1]) + (parts[2] + parts[3])
        squares[...] = jnp.broadcast_to(total, (8, 128))

    ours, squares = vmem_call(gather, where, ring, [((4, 32, 2048), BF16), ((8, 128), F32)])
    theirs = move(ours, c=1)
    squares = squares + swap_x(squares, 1)
    squares = squares + swap_x(squares, 3)
    side = move_yl(squares) + move_yl(squares, c=1)
    squares = (squares + move(squares, c=1)) + side
    outs = update_all(where, ours, theirs, [squares, *state, held_base])
    return (outs[0], outs[1], outs[2], outs[3][None])


def solution(mesh):
    fine = Mesh(mesh.devices.reshape(2, 4, 4, 2, 2), AXES)
    row = P(None, FSDP, None)
    held = P(REP, None, FSDP, None)
    return jax.shard_map(
        local,
        mesh=fine,
        in_specs=(P(REP, FSDP, None, None, None), row, row, row, held),
        out_specs=(row, row, row, held),
        check_vma=False,
    )
```

time: 400 us -> 102 us (0.26); the launches traced: 394 us -> 101 us
  waiting for transfers between devices: 332 us -> 31.3 us
  starting transfers between devices: 4.15 us -> 44.6 us
  other arithmetic: 25.4 us -> 0.28 us
  Pallas kernels: 0 us -> 24.5 us
  blocking collectives: 15.5 us -> 0 us
  between operations: 14.8 us -> 0.81 us
    reduce_scatter x1 -> x0, waiting for transfers between devices: 175 us -> none  [local(): lax.psum_scatter(summands, 'fsdp', scatter_dimension=1, tiled=True)]
    psum x1 -> x0, waiting for transfers between devices: 147 us -> none  [local(): reduced = lax.psum(row_shard, 'rep')]
    ppermute x4 -> x27, starting transfers between devices: 4.07 us -> 44.6 us  [the longest x22 33.6 us: move(): return lax.ppermute(value, AXES, pairs)]
    pallas_call x0 -> x13, Pallas kernels: none -> 24.5 us  [the longest x4 10.7 us: fetch(): pl.pallas_call(body, in_specs=[pl.BlockSpec(memory_space=pltpu.SMEM)] + [...]
    ppermute x4 -> x27, waiting for transfers between devices: 10.3 us -> 31.3 us  [the longest x22 26 us: move(): return lax.ppermute(value, AXES, pairs)]
    psum x1 -> x0, blocking collectives: 15.5 us -> none  [local(): squares = lax.psum(jnp.sum(reduced * reduced), 'fsdp')]
    convert_element_type x4 -> x1, other arithmetic: 12 us -> 0.19 us  [narrow(): return value.astype(BF16)]
    sub x1 -> x0, other arithmetic: 7.14 us -> none  [local(): code_words, scales = encode(new_params - snapshot[0])]
  transfers between devices with their start and end apart: 6 -> 27, of which waited for: 4 -> 15; matrix products, arithmetic and copies ran while one was open for 0% -> 0% of each run, Pallas kernels for 0% -> 14%
where the time goes in v2:
time: 102 us; the launch traced here: 101 us
  starting transfers between devices  44.6 us (44%)
  waiting for transfers between devices  31.3 us (31%)
  Pallas kernels  24.5 us (24%)
    ppermute x22, starting transfers between devices, move(): return lax.ppermute(value, AXES, pairs)  33.6 us
    ppermute x22, waiting for transfers between devices, move(): return lax.ppermute(value, AXES, pairs)  26 us
    pallas_call x4, Pallas kernels, fetch(): pl.pallas_call(body, in_specs=[pl.BlockSpec(memory_space=pltpu.SMEM)] + [...  10.7 us
    pallas_call x7, Pallas kernels, vmem_call(): pl.pallas_call(run, in_specs=[pl.BlockSpec(memory_space=pltpu.SMEM)] + [p...  5.56 us
    pallas_call x1, Pallas kernels, update_all(): pl.pallas_call(body, in_specs=[pl.BlockSpec(memory_space=pltpu.SMEM)] + [...  4.69 us
    ppermute x2, starting transfers between devices, swap_x(): return lax.ppermute(value, AXES, pairs)  4.32 us
    ppermute x2, starting transfers between devices, move_yl(): return lax.ppermute(value, AXES, pairs)  3.51 us
    pallas_call x1, Pallas kernels, preload(): pl.pallas_call(body, in_specs=[pl.BlockSpec(memory_space=pltpu.SMEM)] + [...  3.51 us
  transfers between devices with their start and end apart: 27, of which 15 were waited for; matrix products, arithmetic and copies ran while one was open for 0% of the time, Pallas kernels for 14%

profile of v2, /device:TPU:1, one launch (start us, length us, event | category | flops | bytes accessed | tf_op | source)
XLA Modules:
  0.0 101.5 jit_solution(754905966487768697)
XLA Ops:
  0.7 2.9 %shard_map.85.refs_0_ = bf16[4,2,16,10240]{3,2,1,0:T(8,128)(2,1)S(1)} custom-call(s32[4]{0:T(128)S(1)} %pad_add_fusion.where, bf16[2,2,4,32,8192]{4,3,2,1,0:T(8,128)(2,1)} %bitcast.20), custom_call_target="tpu_custom_call" | custom-call | bytes 4194304 | tf_op jit(solution)/shard_map/pallas_call | solution.py:121
  3.6 1.5 %collective-permute-start = (bf16[4,2,16,10240]{3,2,1,0:T(8,128)(2,1)S(1)}, bf16[4,2,16,10240]{3,2,1,0:T(8,128)(2,1)S(1)}, u32[]{:S(2)}, u32[]{:S(2)}) collective-permute-start(bf16[4,2,16,10240]{3,2,1,0:T(8,128)(2,1)S(1)} %shard_map.85.refs_0_), channel_id=1, source_target_pairs={{0,1},{1,0},{2,3},{3,2},{4,5},{5,4},{6,7},{7,6},{8,9},{9,8},{10,11... | collective-permute-start | bytes 7864328 | tf_op jit(solution)/shard_map/ppermute | solution.py:44
  5.1 2.5 %shard_map.88 = bf16[4,8,16,1536]{3,2,1,0:T(8,128)(2,1)S(1)} custom-call(s32[4]{0:T(128)S(1)} %pad_add_fusion.where, bf16[2,2,4,32,8192]{4,3,2,1,0:T(8,128)(2,1)} %bitcast.21, bf16[4,2,16,10240]{3,2,1,0:T(8,128)(2,1)S(1)} %shard_map.85.refs_0_), custom_call_target="tpu_custom_call" | custom-call | bytes 4194304 | tf_op jit(solution)/shard_map/pallas_call | solution.py:121
  8.2 3.1 %collective-permute-start.5 = (bf16[2,32,8192]{2,1,0:T(8,128)(2,1)S(1)}, bf16[2,32,8192]{2,1,0:T(8,128)(2,1)S(1)}, u32[]{:S(2)}, u32[]{:S(2)}) collective-permute-start(bf16[2,32,8192]{2,1,0:T(8,128)(2,1)S(1)} %fusion.refs_0_), channel_id=1, source_target_pairs={{0,1},{1,2},{2,3},{3,4},{4,5},{5,6},{6,7},{7,8},{8,9},{9,10},{10,1... | collective-permute-start | bytes 3145736 | tf_op jit(solution)/shard_map/ppermute | solution.py:276
  11.4 2.9 %shard_map.84.refs_0_.refs_3_ = bf16[4,2,16,10240]{3,2,1,0:T(8,128)(2,1)S(1)} custom-call(s32[4]{0:T(128)S(1)} %pad_add_fusion.where, bf16[2,2,4,32,8192]{4,3,2,1,0:T(8,128)(2,1)} %bitcast.22, bf16[2,32,8192]{2,1,0:T(8,128)(2,1)S(1)} %fusion.refs_0_), custom_call_target="tpu_custom_call" | custom-call | bytes 4194304 | tf_op jit(solution)/shard_map/pallas_call | solution.py:121
  18.0 1.5 %collective-permute-start.1 = (bf16[2,16,10240]{2,1,0:T(8,128)(2,1)S(1)}, bf16[2,16,10240]{2,1,0:T(8,128)(2,1)S(1)}, u32[]{:S(2)}, u32[]{:S(2)}) collective-permute-start(bf16[2,16,10240]{2,1,0:T(8,128)(2,1)S(1)} %get-tuple-element.29.refs_0_), channel_id=1, source_target_pairs={{0,32},{1,33},{2,34},{3,35},{4,36},{5,37},{6,38},{7,39},{8,40},{9,... | collective-permute-start | bytes 1966088 | tf_op jit(solution)/shard_map/ppermute | solution.py:44
  19.5 2.5 %shard_map.87.refs_0_ = bf16[4,8,16,1536]{3,2,1,0:T(8,128)(2,1)S(1)} custom-call(s32[4]{0:T(128)S(1)} %pad_add_fusion.where, bf16[2,2,4,32,8192]{4,3,2,1,0:T(8,128)(2,1)} %bitcast.23, bf16[2,16,10240]{2,1,0:T(8,128)(2,1)S(1)} %get-tuple-element.29.refs_0_), custom_call_target="tpu_custom_call" | custom-call | bytes 4194304 | tf_op jit(solution)/shard_map/pallas_call | solution.py:121
  23.9 1.7 %collective-permute-start.10 = (bf16[8,16,1536]{2,1,0:T(8,128)(2,1)S(1)}, bf16[8,16,1536]{2,1,0:T(8,128)(2,1)S(1)}, u32[]{:S(2)}, u32[]{:S(2)}) collective-permute-start(bf16[8,16,1536]{2,1,0:T(8,128)(2,1)S(1)} %get-tuple-element.38), channel_id=1, source_target_pairs={{0,4},{1,5},{2,6},{3,7},{4,8},{5,9},{6,10},{7,11},{8,12},{9,13},{1... | collective-permute-start | bytes 1179656 | tf_op jit(solution)/shard_map/ppermute | solution.py:44
  25.6 2.2 %collective-permute-start.11 = (bf16[8,16,1536]{2,1,0:T(8,128)(2,1)S(1)}, bf16[8,16,1536]{2,1,0:T(8,128)(2,1)S(1)}, u32[]{:S(2)}, u32[]{:S(2)}) collective-permute-start(bf16[8,16,1536]{2,1,0:T(8,128)(2,1)S(1)} %get-tuple-element.39), channel_id=1, source_target_pairs={{0,12},{1,13},{2,14},{3,15},{4,0},{5,1},{6,2},{7,3},{8,4},{9,5},{1... | collective-permute-start | bytes 1179656 | tf_op jit(solution)/shard_map/ppermute | solution.py:44
  27.8 4.3 %collective-permute-done.2.refs_1_ = bf16[2,16,10240]{2,1,0:T(8,128)(2,1)S(1)} collective-permute-done((bf16[2,16,10240]{2,1,0:T(8,128)(2,1)S(1)}, bf16[2,16,10240]{2,1,0:T(8,128)(2,1)S(1)}, u32[]{:S(2)}, u32[]{:S(2)}) %collective-permute-start.2) | collective-permute-done | bytes 655392 | tf_op jit(solution)/shard_map/ppermute | solution.py:44
  32.2 3.8 %collective-permute-start.9 = (bf16[8,16,1536]{2,1,0:T(8,128)(2,1)S(1)}, bf16[8,16,1536]{2,1,0:T(8,128)(2,1)S(1)}, u32[]{:S(2)}, u32[]{:S(2)}) collective-permute-start(bf16[8,16,1536]{2,1,0:T(8,128)(2,1)S(1)} %get-tuple-element.32.refs_3_), channel_id=1, source_target_pairs={{0,8},{1,9},{2,10},{3,11},{4,12},{5,13},{6,14},{7,15},{8,0},{9,1},... | collective-permute-start | bytes 1179656 | tf_op jit(solution)/shard_map/ppermute | solution.py:44
  35.9 3.5 %shard_map.90 = (f32[2,32,8192]{2,1,0:T(8,128)S(1)}, f32[2,32,8192]{2,1,0:T(8,128)S(1)}, f32[2,32,8192]{2,1,0:T(8,128)S(1)}) custom-call(s32[4]{0:T(128)S(1)} %pad_add_fusion.where, f32[2,32,8192]{2,1,0:T(8,128)} %refs_0_.1, f32[2,32,8192]{2,1,0:T(8,128)} %refs_1_.1, f32[2,32,8192]{2,1,0:T(8,128)} %refs_2_.1, bf16[8,16,1536]{2,1,0:T(8,128)(2,1)S(1)} %get-tuple-element.32.refs_3_), custom_call_target="tpu_custom_call" | custom-call | flops 1048576 | bytes 6291456 | tf_op jit(solution)/shard_map/pallas_call | solution.py:155
  39.5 6.8 %collective-permute-done.1.refs_0_ = bf16[2,16,10240]{2,1,0:T(8,128)(2,1)S(1)} collective-permute-done((bf16[2,16,10240]{2,1,0:T(8,128)(2,1)S(1)}, bf16[2,16,10240]{2,1,0:T(8,128)(2,1)S(1)}, u32[]{:S(2)}, u32[]{:S(2)}) %collective-permute-start.1) | collective-permute-done | bytes 655392 | tf_op jit(solution)/shard_map/ppermute | solution.py:44
  50.3 2.1 %collective-permute-start.8 = (bf16[2,16,2560]{2,1,0:T(8,128)(2,1)S(1)}, bf16[2,16,2560]{2,1,0:T(8,128)(2,1)S(1)}, u32[]{:S(2)}, u32[]{:S(2)}) collective-permute-start(bf16[2,16,2560]{2,1,0:T(8,128)(2,1)S(1)} %get-tuple-element.37), channel_id=1, source_target_pairs={{0,12},{1,13},{2,14},{3,15},{4,0},{5,1},{6,2},{7,3},{8,4},{9,5},{1... | collective-permute-start | bytes 491528 | tf_op jit(solution)/shard_map/ppermute | solution.py:44
  53.6 1.9 %collective-permute-start.13 = (bf16[2,16,1536]{2,1,0:T(8,128)(2,1)S(1)}, bf16[2,16,1536]{2,1,0:T(8,128)(2,1)S(1)}, u32[]{:S(2)}, u32[]{:S(2)}) collective-permute-start(bf16[2,16,1536]{2,1,0:T(8,128)(2,1)S(1)} %get-tuple-element.42), channel_id=1, source_target_pairs={{0,16},{1,17},{2,18},{3,19},{4,20},{5,21},{6,22},{7,23},{8,24},{9,... | collective-permute-start | bytes 294920 | tf_op jit(solution)/shard_map/ppermute | solution.py:44
  56.4 2.0 %collective-permute-done.13.refs_6_ = bf16[2,16,1536]{2,1,0:T(8,128)(2,1)S(1)} collective-permute-done((bf16[2,16,1536]{2,1,0:T(8,128)(2,1)S(1)}, bf16[2,16,1536]{2,1,0:T(8,128)(2,1)S(1)}, u32[]{:S(2)}, u32[]{:S(2)}) %collective-permute-start.13) | collective-permute-done | bytes 98336 | tf_op jit(solution)/shard_map/ppermute | solution.py:44
  63.1 3.0 %collective-permute-start.17 = (bf16[32,2048]{1,0:T(8,128)(2,1)S(1)}, bf16[32,2048]{1,0:T(8,128)(2,1)S(1)}, u32[]{:S(2)}, u32[]{:S(2)}) collective-permute-start(bf16[32,2048]{1,0:T(8,128)(2,1)S(1)} %get-tuple-element.45), channel_id=1, source_target_pairs={{0,66},{1,67},{2,64},{3,65},{4,70},{5,71},{6,68},{7,69},{8,74},{9,... | collective-permute-start | bytes 393224 | tf_op jit(solution)/shard_map/ppermute | solution.py:44
  67.0 2.9 %collective-permute-done.17.refs_3_ = bf16[32,2048]{1,0:T(8,128)(2,1)S(1)} collective-permute-done((bf16[32,2048]{1,0:T(8,128)(2,1)S(1)}, bf16[32,2048]{1,0:T(8,128)(2,1)S(1)}, u32[]{:S(2)}, u32[]{:S(2)}) %collective-permute-start.17) | collective-permute-done | bytes 131104 | tf_op jit(solution)/shard_map/ppermute | solution.py:44
  75.7 4.0 %collective-permute-done.19.refs_2_ = bf16[32,2176]{1,0:T(8,128)(2,1)S(1)} collective-permute-done((bf16[32,2176]{1,0:T(8,128)(2,1)S(1)}, bf16[32,2176]{1,0:T(8,128)(2,1)S(1)}, u32[]{:S(2)}, u32[]{:S(2)}) %collective-permute-start.19) | collective-permute-done | bytes 139296 | tf_op jit(solution)/shard_map/ppermute | solution.py:44
  80.3 4.0 %collective-permute-start.21 = (bf16[4,32,2048]{2,1,0:T(8,128)(2,1)S(1)}, bf16[4,32,2048]{2,1,0:T(8,128)(2,1)S(1)}, u32[]{:S(2)}, u32[]{:S(2)}) collective-permute-start(bf16[4,32,2048]{2,1,0:T(8,128)(2,1)S(1)} %get-tuple-element.46.ours), channel_id=1, source_target_pairs={{0,1},{1,0},{2,3},{3,2},{4,5},{5,4},{6,7},{7,6},{8,9},{9,8},{10,11... | collective-permute-start | bytes 1572872 | tf_op jit(solution)/shard_map/ppermute | solution.py:44
  84.3 1.9 %collective-permute-start.22 = (f32[8,128]{1,0:T(8,128)S(1)}, f32[8,128]{1,0:T(8,128)S(1)}, u32[]{:S(2)}, u32[]{:S(2)}) collective-permute-start(f32[8,128]{1,0:T(8,128)S(1)} %get-tuple-element.47), channel_id=1, source_target_pairs={{0,16},{1,17},{2,18},{3,19},{4,20},{5,21},{6,22},{7,23},{8,24},{9,... | collective-permute-start | bytes 12296 | tf_op jit(solution)/shard_map/ppermute | solution.py:49
  87.1 2.5 %collective-permute-start.23 = (f32[8,128]{1,0:T(8,128)S(1)}, f32[8,128]{1,0:T(8,128)S(1)}, u32[]{:S(2)}, u32[]{:S(2)}) collective-permute-start(f32[8,128]{1,0:T(8,128)S(1)} %add.15), channel_id=1, source_target_pairs={{0,48},{1,49},{2,50},{3,51},{4,52},{5,53},{6,54},{7,55},{8,56},{9,... | collective-permute-start | bytes 12296 | tf_op jit(solution)/shard_map/ppermute | solution.py:49
  90.8 3.5 %collective-permute-start.26 = (f32[8,128]{1,0:T(8,128)S(1)}, f32[8,128]{1,0:T(8,128)S(1)}, u32[]{:S(2)}, u32[]{:S(2)}) collective-permute-start(f32[8,128]{1,0:T(8,128)S(1)} %add.16), channel_id=1, source_target_pairs={{0,65},{1,64},{2,67},{3,66},{4,69},{5,68},{6,71},{7,70},{8,73},{9,... | collective-permute-start | bytes 12296 | tf_op jit(solution)/shard_map/ppermute | solution.py:54
  96.8 4.7 %shard_map.96 = (f32[2,32,8192]{2,1,0:T(8,128)}, f32[2,32,8192]{2,1,0:T(8,128)}, f32[2,32,8192]{2,1,0:T(8,128)}, f32[2,32,8192]{2,1,0:T(8,128)}) custom-call(s32[4]{0:T(128)S(1)} %pad_add_fusion.where, bf16[4,32,2048]{2,1,0:T(8,128)(2,1)S(1)} %get-tuple-element.46.ours, bf16[4,32,2048]{2,1,0:T(8,128)(2,1)S(1)} %collective-permute-done.21.theirs, ...), custom_call_target="tpu_custom_call" | custom-call | flops 9437184 | bytes 9437184 | tf_op jit(solution)/shard_map/pallas_call | solution.py:255
  (52 shorter events, 29.1 us)
Async XLA Ops:
  3.6 10.6 %collective-permute-start = (bf16[4,2,16,10240]{3,2,1,0:T(8,128)(2,1)S(1)}, bf16[4,2,16,10240]{3,2,1,0:T(8,128)(2,1)S(1)}, u32[]{:S(2)}, u32[]{:S(2)}) collective-permute-start(bf16[4,2,16,10240]{3,2,1,0:T(8,128)(2,1)S(1)} %shard_map.85.refs_0_), channel_id=1, source_target_pairs={{0,1},{1,0},{2,3},{3,2},{4,5},{5,4},{6,7},{7,6},{8,9},{9,8},{10,11... | collective-permute-start | bytes 7864328 | tf_op jit(solution)/shard_map/ppermute | solution.py:44
  7.6 15.5 %collective-permute-start.4 = (bf16[4,8,16,1536]{3,2,1,0:T(8,128)(2,1)S(1)}, bf16[4,8,16,1536]{3,2,1,0:T(8,128)(2,1)S(1)}, u32[]{:S(2)}, u32[]{:S(2)}) collective-permute-start(bf16[4,8,16,1536]{3,2,1,0:T(8,128)(2,1)S(1)} %shard_map.88), channel_id=1, source_target_pairs={{0,1},{1,0},{2,3},{3,2},{4,5},{5,4},{6,7},{7,6},{8,9},{9,8},{10,11... | collective-permute-start | bytes 4718600 | tf_op jit(solution)/shard_map/ppermute | solution.py:44
  8.2 14.9 %collective-permute-start.5 = (bf16[2,32,8192]{2,1,0:T(8,128)(2,1)S(1)}, bf16[2,32,8192]{2,1,0:T(8,128)(2,1)S(1)}, u32[]{:S(2)}, u32[]{:S(2)}) collective-permute-start(bf16[2,32,8192]{2,1,0:T(8,128)(2,1)S(1)} %fusion.refs_0_), channel_id=1, source_target_pairs={{0,1},{1,2},{2,3},{3,4},{4,5},{5,6},{6,7},{7,8},{8,9},{9,10},{10,1... | collective-permute-start | bytes 3145736 | tf_op jit(solution)/shard_map/ppermute | solution.py:276
  15.2 16.9 %collective-permute-start.2 = (bf16[2,16,10240]{2,1,0:T(8,128)(2,1)S(1)}, bf16[2,16,10240]{2,1,0:T(8,128)(2,1)S(1)}, u32[]{:S(2)}, u32[]{:S(2)}) collective-permute-start(bf16[2,16,10240]{2,1,0:T(8,128)(2,1)S(1)} %get-tuple-element.30), channel_id=1, source_target_pairs={{0,16},{1,17},{2,18},{3,19},{4,20},{5,21},{6,22},{7,23},{8,24},{9,... | collective-permute-start | bytes 1966088 | tf_op jit(solution)/shard_map/ppermute | solution.py:44
  16.5 22.9 %collective-permute-start.3 = (bf16[2,16,10240]{2,1,0:T(8,128)(2,1)S(1)}, bf16[2,16,10240]{2,1,0:T(8,128)(2,1)S(1)}, u32[]{:S(2)}, u32[]{:S(2)}) collective-permute-start(bf16[2,16,10240]{2,1,0:T(8,128)(2,1)S(1)} %get-tuple-element.31), channel_id=1, source_target_pairs={{0,48},{1,49},{2,50},{3,51},{4,52},{5,53},{6,54},{7,55},{8,56},{9,... | collective-permute-start | bytes 1966088 | tf_op jit(solution)/shard_map/ppermute | solution.py:44
  18.0 28.3 %collective-permute-start.1 = (bf16[2,16,10240]{2,1,0:T(8,128)(2,1)S(1)}, bf16[2,16,10240]{2,1,0:T(8,128)(2,1)S(1)}, u32[]{:S(2)}, u32[]{:S(2)}) collective-permute-start(bf16[2,16,10240]{2,1,0:T(8,128)(2,1)S(1)} %get-tuple-element.29.refs_0_), channel_id=1, source_target_pairs={{0,32},{1,33},{2,34},{3,35},{4,36},{5,37},{6,38},{7,39},{8,40},{9,... | collective-permute-start | bytes 1966088 | tf_op jit(solution)/shard_map/ppermute | solution.py:44
  23.9 23.3 %collective-permute-start.10 = (bf16[8,16,1536]{2,1,0:T(8,128)(2,1)S(1)}, bf16[8,16,1536]{2,1,0:T(8,128)(2,1)S(1)}, u32[]{:S(2)}, u32[]{:S(2)}) collective-permute-start(bf16[8,16,1536]{2,1,0:T(8,128)(2,1)S(1)} %get-tuple-element.38), channel_id=1, source_target_pairs={{0,4},{1,5},{2,6},{3,7},{4,8},{5,9},{6,10},{7,11},{8,12},{9,13},{1... | collective-permute-start | bytes 1179656 | tf_op jit(solution)/shard_map/ppermute | solution.py:44
  25.6 21.6 %collective-permute-start.11 = (bf16[8,16,1536]{2,1,0:T(8,128)(2,1)S(1)}, bf16[8,16,1536]{2,1,0:T(8,128)(2,1)S(1)}, u32[]{:S(2)}, u32[]{:S(2)}) collective-permute-start(bf16[8,16,1536]{2,1,0:T(8,128)(2,1)S(1)} %get-tuple-element.39), channel_id=1, source_target_pairs={{0,12},{1,13},{2,14},{3,15},{4,0},{5,1},{6,2},{7,3},{8,4},{9,5},{1... | collective-permute-start | bytes 1179656 | tf_op jit(solution)/shard_map/ppermute | solution.py:44
  32.2 15.1 %collective-permute-start.9 = (bf16[8,16,1536]{2,1,0:T(8,128)(2,1)S(1)}, bf16[8,16,1536]{2,1,0:T(8,128)(2,1)S(1)}, u32[]{:S(2)}, u32[]{:S(2)}) collective-permute-start(bf16[8,16,1536]{2,1,0:T(8,128)(2,1)S(1)} %get-tuple-element.32.refs_3_), channel_id=1, source_target_pairs={{0,8},{1,9},{2,10},{3,11},{4,12},{5,13},{6,14},{7,15},{8,0},{9,1},... | collective-permute-start | bytes 1179656 | tf_op jit(solution)/shard_map/ppermute | solution.py:44
  48.1 7.4 %collective-permute-start.12 = (bf16[2,16,1536]{2,1,0:T(8,128)(2,1)S(1)}, bf16[2,16,1536]{2,1,0:T(8,128)(2,1)S(1)}, u32[]{:S(2)}, u32[]{:S(2)}) collective-permute-start(bf16[2,16,1536]{2,1,0:T(8,128)(2,1)S(1)} %get-tuple-element.41), channel_id=1, source_target_pairs={{0,32},{1,33},{2,34},{3,35},{4,36},{5,37},{6,38},{7,39},{8,40},{9,... | collective-permute-start | bytes 294920 | tf_op jit(solution)/shard_map/ppermute | solution.py:44
  49.1 10.8 %collective-permute-start.7 = (bf16[2,16,2560]{2,1,0:T(8,128)(2,1)S(1)}, bf16[2,16,2560]{2,1,0:T(8,128)(2,1)S(1)}, u32[]{:S(2)}, u32[]{:S(2)}) collective-permute-start(bf16[2,16,2560]{2,1,0:T(8,128)(2,1)S(1)} %get-tuple-element.36), channel_id=1, source_target_pairs={{0,4},{1,5},{2,6},{3,7},{4,8},{5,9},{6,10},{7,11},{8,12},{9,13},{1... | collective-permute-start | bytes 491528 | tf_op jit(solution)/shard_map/ppermute | solution.py:44
  50.3 9.5 %collective-permute-start.8 = (bf16[2,16,2560]{2,1,0:T(8,128)(2,1)S(1)}, bf16[2,16,2560]{2,1,0:T(8,128)(2,1)S(1)}, u32[]{:S(2)}, u32[]{:S(2)}) collective-permute-start(bf16[2,16,2560]{2,1,0:T(8,128)(2,1)S(1)} %get-tuple-element.37), channel_id=1, source_target_pairs={{0,12},{1,13},{2,14},{3,15},{4,0},{5,1},{6,2},{7,3},{8,4},{9,5},{1... | collective-permute-start | bytes 491528 | tf_op jit(solution)/shard_map/ppermute | solution.py:44
  52.4 8.5 %collective-permute-start.6 = (bf16[2,16,2560]{2,1,0:T(8,128)(2,1)S(1)}, bf16[2,16,2560]{2,1,0:T(8,128)(2,1)S(1)}, u32[]{:S(2)}, u32[]{:S(2)}) collective-permute-start(bf16[2,16,2560]{2,1,0:T(8,128)(2,1)S(1)} %get-tuple-element.35.refs_5_), channel_id=1, source_target_pairs={{0,8},{1,9},{2,10},{3,11},{4,12},{5,13},{6,14},{7,15},{8,0},{9,1},... | collective-permute-start | bytes 491528 | tf_op jit(solution)/shard_map/ppermute | solution.py:44
  53.6 4.8 %collective-permute-start.13 = (bf16[2,16,1536]{2,1,0:T(8,128)(2,1)S(1)}, bf16[2,16,1536]{2,1,0:T(8,128)(2,1)S(1)}, u32[]{:S(2)}, u32[]{:S(2)}) collective-permute-start(bf16[2,16,1536]{2,1,0:T(8,128)(2,1)S(1)} %get-tuple-element.42), channel_id=1, source_target_pairs={{0,16},{1,17},{2,18},{3,19},{4,20},{5,21},{6,22},{7,23},{8,24},{9,... | collective-permute-start | bytes 294920 | tf_op jit(solution)/shard_map/ppermute | solution.py:44
  55.5 4.4 %collective-permute-start.14 = (bf16[2,16,1536]{2,1,0:T(8,128)(2,1)S(1)}, bf16[2,16,1536]{2,1,0:T(8,128)(2,1)S(1)}, u32[]{:S(2)}, u32[]{:S(2)}) collective-permute-start(bf16[2,16,1536]{2,1,0:T(8,128)(2,1)S(1)} %get-tuple-element.43), channel_id=1, source_target_pairs={{0,48},{1,49},{2,50},{3,51},{4,52},{5,53},{6,54},{7,55},{8,56},{9,... | collective-permute-start | bytes 294920 | tf_op jit(solution)/shard_map/ppermute | solution.py:44
  61.6 5.4 %collective-permute-start.15 = (bf16[32,2048]{1,0:T(8,128)(2,1)S(1)}, bf16[32,2048]{1,0:T(8,128)(2,1)S(1)}, u32[]{:S(2)}, u32[]{:S(2)}) collective-permute-start(bf16[32,2048]{1,0:T(8,128)(2,1)S(1)} %get-tuple-element.44.refs_0_), channel_id=1, source_target_pairs={{0,2},{1,3},{2,0},{3,1},{4,6},{5,7},{6,4},{7,5},{8,10},{9,11},{10,... | collective-permute-start | bytes 393224 | tf_op jit(solution)/shard_map/ppermute | solution.py:44
  63.1 6.9 %collective-permute-start.17 = (bf16[32,2048]{1,0:T(8,128)(2,1)S(1)}, bf16[32,2048]{1,0:T(8,128)(2,1)S(1)}, u32[]{:S(2)}, u32[]{:S(2)}) collective-permute-start(bf16[32,2048]{1,0:T(8,128)(2,1)S(1)} %get-tuple-element.45), channel_id=1, source_target_pairs={{0,66},{1,67},{2,64},{3,65},{4,70},{5,71},{6,68},{7,69},{8,74},{9,... | collective-permute-start | bytes 393224 | tf_op jit(solution)/shard_map/ppermute | solution.py:44
  66.0 5.0 %collective-permute-start.16 = (bf16[32,2048]{1,0:T(8,128)(2,1)S(1)}, bf16[32,2048]{1,0:T(8,128)(2,1)S(1)}, u32[]{:S(2)}, u32[]{:S(2)}) collective-permute-start(bf16[32,2048]{1,0:T(8,128)(2,1)S(1)} %get-tuple-element.45), channel_id=1, source_target_pairs={{0,64},{1,65},{2,66},{3,67},{4,68},{5,69},{6,70},{7,71},{8,72},{9,... | collective-permute-start | bytes 393224 | tf_op jit(solution)/shard_map/ppermute | solution.py:44
  71.8 3.9 %collective-permute-start.20 = (bf16[32,2176]{1,0:T(8,128)(2,1)S(1)}, bf16[32,2176]{1,0:T(8,128)(2,1)S(1)}, u32[]{:S(2)}, u32[]{:S(2)}) collective-permute-start(bf16[32,2176]{1,0:T(8,128)(2,1)S(1)} %shard_map.94.refs_0_), channel_id=1, source_target_pairs={{0,12},{1,13},{2,14},{3,15},{4,0},{5,1},{6,2},{7,3},{8,4},{9,5},{1... | collective-permute-start | bytes 417800 | tf_op jit(solution)/shard_map/ppermute | solution.py:44
  73.1 6.6 %collective-permute-start.19 = (bf16[32,2176]{1,0:T(8,128)(2,1)S(1)}, bf16[32,2176]{1,0:T(8,128)(2,1)S(1)}, u32[]{:S(2)}, u32[]{:S(2)}) collective-permute-start(bf16[32,2176]{1,0:T(8,128)(2,1)S(1)} %shard_map.94.refs_0_), channel_id=1, source_target_pairs={{0,4},{1,5},{2,6},{3,7},{4,8},{5,9},{6,10},{7,11},{8,12},{9,13},{1... | collective-permute-start | bytes 417800 | tf_op jit(solution)/shard_map/ppermute | solution.py:44
  73.3 6.4 %collective-permute-start.18 = (bf16[32,2176]{1,0:T(8,128)(2,1)S(1)}, bf16[32,2176]{1,0:T(8,128)(2,1)S(1)}, u32[]{:S(2)}, u32[]{:S(2)}) collective-permute-start(bf16[32,2176]{1,0:T(8,128)(2,1)S(1)} %shard_map.94.refs_0_), channel_id=1, source_target_pairs={{0,8},{1,9},{2,10},{3,11},{4,12},{5,13},{6,14},{7,15},{8,0},{9,1},... | collective-permute-start | bytes 417800 | tf_op jit(solution)/shard_map/ppermute | solution.py:44
  80.3 16.5 %collective-permute-start.21 = (bf16[4,32,2048]{2,1,0:T(8,128)(2,1)S(1)}, bf16[4,32,2048]{2,1,0:T(8,128)(2,1)S(1)}, u32[]{:S(2)}, u32[]{:S(2)}) collective-permute-start(bf16[4,32,2048]{2,1,0:T(8,128)(2,1)S(1)} %get-tuple-element.46.ours), channel_id=1, source_target_pairs={{0,1},{1,0},{2,3},{3,2},{4,5},{5,4},{6,7},{7,6},{8,9},{9,8},{10,11... | collective-permute-start | bytes 1572872 | tf_op jit(solution)/shard_map/ppermute | solution.py:44
  87.1 3.7 %collective-permute-start.23 = (f32[8,128]{1,0:T(8,128)S(1)}, f32[8,128]{1,0:T(8,128)S(1)}, u32[]{:S(2)}, u32[]{:S(2)}) collective-permute-start(f32[8,128]{1,0:T(8,128)S(1)} %add.15), channel_id=1, source_target_pairs={{0,48},{1,49},{2,50},{3,51},{4,52},{5,53},{6,54},{7,55},{8,56},{9,... | collective-permute-start | bytes 12296 | tf_op jit(solution)/shard_map/ppermute | solution.py:49
  90.8 4.8 %collective-permute-start.26 = (f32[8,128]{1,0:T(8,128)S(1)}, f32[8,128]{1,0:T(8,128)S(1)}, u32[]{:S(2)}, u32[]{:S(2)}) collective-permute-start(f32[8,128]{1,0:T(8,128)S(1)} %add.16), channel_id=1, source_target_pairs={{0,65},{1,64},{2,67},{3,66},{4,69},{5,68},{6,71},{7,70},{8,73},{9,... | collective-permute-start | bytes 12296 | tf_op jit(solution)/shard_map/ppermute | solution.py:54
  (5 other events, 16.6 us)

commit v3 on v2

--- a/solution.py
+++ b/solution.py
@@ -81,9 +81,10 @@
     )(where, *arrays, *after)
 
 
-LEFT = (2, 16, 10240)
-RIGHT = (8, 16, 1536)
-ORDER = (0, 2, 1, 3)
+LEFT = (2, 16, 8192)
+RIGHT = (8, 16, 2048)
+ORDER = (0, 1, 2, 3)
+BLOCKS = (0, 1, 2, 3)
 
 X, YL, Z, C = range(4)
 
@@ -98,14 +99,9 @@
                 if left:
                     row = (where[X] + k) % 4
                     for f in range(2):
-                        src_row, dst_row = src.at[layer, f, row], out.at[i, f]
-                        copies.append((src_row.at[pl.ds(0, 16)], dst_row.at[:, pl.ds(0, 8192)]))
-                        for part in range(4):
-                            thin = pl.ds(2048 * part + 1536, 512)
-                            to = pl.ds(8192 + 512 * part, 512)
-                            copies.append((src_row.at[pl.ds(16, 16), thin], dst_row.at[:, to]))
+                        copies.append((src.at[layer, f, row, pl.ds(0, 16)], out.at[i, f]))
                 else:
-                    cols = pl.ds(pl.multiple_of((where[Z] + k) % 4 * 2048, 2048), 1536)
+                    cols = pl.ds(pl.multiple_of((where[Z] + k) % 4 * 2048, 2048), 2048)
                     for f in range(8):
                         copies.append(
                             (src.at[layer, f // 4, f % 4, pl.ds(16, 16), cols], out.at[i, f])
@@ -127,7 +123,7 @@
             pltpu.VMEM((len(offsets),) + (LEFT if left else RIGHT), BF16)
             for _, left, offsets in wanted
         ],
-        scratch_shapes=[pltpu.SemaphoreType.DMA((16 * blocks,))],
+        scratch_shapes=[pltpu.SemaphoreType.DMA((8 * blocks,))],
         compiler_params=pltpu.CompilerParams(vmem_limit_bytes=4 * MIB),
         cost_estimate=pl.CostEstimate(flops=0, bytes_accessed=blocks * MIB, transcendentals=0),
     )(where, grads, *after)
@@ -175,25 +171,24 @@
     return add(*[wide(r[index] if index else r[...]) for r in refs])
 
 
-def pair_sum(where, mine, theirs, after=()):
+def pair_sum(where, mine, theirs, places, after=()):
     dims = mine.shape[1:]
 
     def body(where, a, b, *outs):
-        for i, out in enumerate(outs):
-            out[...] = narrow(wide(a[i]) + wide(b[i]))
-
-    return list(vmem_call(body, where, (mine, theirs), [(dims, BF16)] * 3, after))
-
-
-def split(where, arrays, whole, cut, width, after=()):
-    dims = (2, 16, width)
+        for out, k in zip(outs, places):
+            out[...] = narrow(wide(a[k]) + wide(b[k]))
+
+    return list(vmem_call(body, where, (mine, theirs), [(dims, BF16)] * len(places), after))
+
+
+def split(where, arrays, whole, cut, after):
+    dims = (2, 16, 2048)
     count = len(arrays)
 
     def body(where, *refs):
-        ins = list(refs[:count]) + [r.at[3] for r in refs[count:-4]]
+        ins = list(refs[:count]) + [r.at[0] for r in refs[count:-4]]
         for out, k in zip(refs[-4:], ORDER):
-            for first, last, index in cut(where, k):
-                out[:, :, first:last] = total_of(ins, *index).astype(out.dtype)
+            out[...] = total_of(ins, *cut(where, k)).astype(out.dtype)
 
     outs = [(dims, F32)] + [(dims, BF16)] * 3
     return list(vmem_call(body, where, list(arrays) + whole, outs, after))
@@ -268,43 +263,43 @@
     where = jnp.stack([lax.axis_index(name) for name in ("x", "yl", "z", "c")]).astype(jnp.int32)
     grads = partial_grads[0, 0]
 
-    order = ORDER[1:] + (0,)
-    theirs = fetch(grads, where, [(False, True, order)])
-    theirs += fetch(grads, where, [(False, False, order)], theirs)
-    theirs = [move(b, c=1) for b in theirs]
+    their_right = fetch(grads, where, [(False, False, BLOCKS)])[0]
+    got_right = move(their_right, c=1)
     base = narrow(params - snapshot[0])
     held_base = lax.ppermute(base, REP, [(i, (i + 1) % 16) for i in range(16)])
-    mine = fetch(grads, where, [(True, True, order)], (base,))
-    left = pair_sum(where, mine[0], theirs[0])
-    mine += fetch(grads, where, [(True, False, order)], (left[0],))
-    right = pair_sum(where, mine[1], theirs[1], (held_base,))
-    state = preload([params, moment, second_moment], where, right[0])
+    more = [(own, left, BLOCKS) for own, left in ((True, False), (False, True), (True, True))]
+    own_right, their_left, own_left = fetch(grads, where, more, (their_right,))
+    got_left = move(their_left, c=1)
+    far, near = pair_sum(where, own_right, got_right, (2, 1))
+    left = pair_sum(where, own_left, got_left, ORDER[1:], (far,))
+    state = preload([params, moment, second_moment], where, left[0])
     left = travel(left, "x")
-    right = travel(right, "z")
+
+    def relay(where, far, a, b, out):
+        out[...] = narrow(wide(far[...]) + wide(a[3]) + wide(b[3]))
+
+    relayed = [move(far, z=3), own_right, got_right]
+    relayed = vmem_call(relay, where, relayed, [(RIGHT, BF16)], (state[0],))[0]
+    right = [move(near, z=1), move(relayed, z=3)]
 
     def by_z(where, k):
-        block = (where[Z] + k) % 4
-        wide_part = pl.ds(pl.multiple_of(block * 2048, 2048), 2048)
-        thin_part = pl.ds(pl.multiple_of(8192 + block * 512, 512), 512)
-        every = slice(None)
-        return (0, 2048, (every, every, wide_part)), (2048, 2560, (every, every, thin_part))
+        cols = pl.ds(pl.multiple_of((where[Z] + k) % 4 * 2048, 2048), 2048)
+        return slice(None), slice(None), cols
 
     def by_x(where, k):
-        return ((0, 1536, (slice(None), (where[X] + k) % 4)),)
-
-    left = split(where, left, [mine[0], theirs[0]], by_z, 2560, (state[0],))
+        return slice(None), (where[X] + k) % 4
+
+    left = split(where, left, [own_left, got_left], by_z, (held_base,))
     ready = left[1]
     left = left[:1] + travel(left[1:], "z")
-    whole = [a.reshape(4, 2, 4, 16, 1536) for a in (mine[1], theirs[1])]
-    right = split(where, [r.reshape(2, 4, 16, 1536) for r in right], whole, by_x, 1536, (ready,))
+    whole = [a.reshape(4, 2, 4, 16, 2048) for a in (own_right, got_right)]
+    right = split(where, [r.reshape(2, 4, 16, 2048) for r in right], whole, by_x, (ready,))
     right = right[:1] + travel(right[1:], "x")
 
     def join(where, *refs):
         for out, index in ((refs[8], where[YL]), (refs[9], 1 - where[YL])):
-            a = narrow(total_of(refs[:4], index))
-            out[:16, :] = a[:, :2048]
-            out[16:, :1536] = narrow(total_of(refs[4:8], index))
-            out[16:, 1536:] = a[:, 2048:]
+            out[:16, :] = narrow(total_of(refs[:4], index))
+            out[16:, :] = narrow(total_of(refs[4:8], index))
 
     mine, other = vmem_call(join, where, left + right, [((32, 2048), BF16)] * 2)
     fourth = [mine, move(mine, y=2), move(other, y=1), move(other, y=3)]
@@ -326,15 +321,15 @@
     def gather(where, *refs):
         ins, out, squares = refs[:4], refs[4], refs[5]
         parts = [jnp.sum(wide(ref[:16, 2048:])[:8, :], axis=1, keepdims=True) for ref in ins]
-        for k, ref in zip(ORDER, ins):
+        for k, ref in zip((0, 2, 1, 3), ins):
             out[k] = ref[:, :2048]
         total = (parts[0] + parts[1]) + (parts[2] + parts[3])
         squares[...] = jnp.broadcast_to(total, (8, 128))
 
     ours, squares = vmem_call(gather, where, ring, [((4, 32, 2048), BF16), ((8, 128), F32)])
     theirs = move(ours, c=1)
-    squares = squares + swap_x(squares, 1)
-    squares = squares + swap_x(squares, 3)
+    side = move(squares, x=1) + move(squares, x=3)
+    squares = (squares + move(squares, x=2)) + side
     side = move_yl(squares) + move_yl(squares, c=1)
     squares = (squares + move(squares, c=1)) + side
     outs = update_all(where, ours, theirs, [squares, *state, held_base])

time: 102 us -> 96.5 us (0.946)
  Pallas kernels: 24.5 us -> 21.1 us
  starting transfers between devices: 44.6 us -> 42.7 us
    ppermute x2 -> x0, starting transfers between devices: 4.32 us -> none  [swap_x(): return lax.ppermute(value, AXES, pairs)]
    ppermute x22 -> x25, waiting for transfers between devices: 26 us -> 30.1 us  [move(): return lax.ppermute(value, AXES, pairs)]
    pallas_call x4 -> x2, Pallas kernels: 10.7 us -> 6.7 us  [fetch(): pl.pallas_call(body, in_specs=[pl.BlockSpec(memory_space=pltpu.SMEM)] + [...]
    ppermute x22 -> x25, starting transfers between devices: 33.6 us -> 36.7 us  [move(): return lax.ppermute(value, AXES, pairs)]
    ppermute x2 -> x0, waiting for transfers between devices: 2.19 us -> none  [swap_x(): return lax.ppermute(value, AXES, pairs)]
    ppermute x1, waiting for transfers between devices: 1.09 us -> 0.01 us  [local(): held_base = lax.ppermute(base, REP, [(i, (i + 1) % 16) for i in range(16)])]
    pallas_call x7 -> x8, Pallas kernels: 5.56 us -> 6.18 us  [vmem_call(): pl.pallas_call(run, in_specs=[pl.BlockSpec(memory_space=pltpu.SMEM)] + [p...]
  transfers between devices with their start and end apart: 27 -> 28, of which waited for: 15 -> 16; matrix products, arithmetic and copies ran while one was open for 0% -> 0% of each run, Pallas kernels for 14% -> 12%
where the time goes in v3:
time: 96.5 us; the launch traced here: 96.3 us
  starting transfers between devices  42.7 us (44%)
  waiting for transfers between devices  31.4 us (33%)
  Pallas kernels  21.1 us (22%)
    ppermute x25, starting transfers between devices, move(): return lax.ppermute(value, AXES, pairs)  36.7 us
    ppermute x25, waiting for transfers between devices, move(): return lax.ppermute(value, AXES, pairs)  30.1 us
    pallas_call x2, Pallas kernels, fetch(): pl.pallas_call(body, in_specs=[pl.BlockSpec(memory_space=pltpu.SMEM)] + [...  6.7 us
    pallas_call x8, Pallas kernels, vmem_call(): pl.pallas_call(run, in_specs=[pl.BlockSpec(memory_space=pltpu.SMEM)] + [p...  6.18 us
    pallas_call x1, Pallas kernels, update_all(): pl.pallas_call(body, in_specs=[pl.BlockSpec(memory_space=pltpu.SMEM)] + [...  4.7 us
    pallas_call x1, Pallas kernels, preload(): pl.pallas_call(body, in_specs=[pl.BlockSpec(memory_space=pltpu.SMEM)] + [...  3.51 us
    ppermute x1, starting transfers between devices, local(): held_base = lax.ppermute(base, REP, [(i, (i + 1) % 16) for i in range(16)])  3.15 us
    ppermute x2, starting transfers between devices, move_yl(): return lax.ppermute(value, AXES, pairs)  2.85 us
  transfers between devices with their start and end apart: 28, of which 16 were waited for; matrix products, arithmetic and copies ran while one was open for 0% of the time, Pallas kernels for 12%

profile of v3, /device:TPU:1, one launch (start us, length us, event | category | flops | bytes accessed | tf_op | source)
XLA Modules:
  0.0 96.3 jit_solution(10321477992041292144)
XLA Ops:
  0.7 2.4 %shard_map.84.refs_0_ = bf16[4,8,16,2048]{3,2,1,0:T(8,128)(2,1)S(1)} custom-call(s32[4]{0:T(128)S(1)} %pad_add_fusion.where, bf16[2,2,4,32,8192]{4,3,2,1,0:T(8,128)(2,1)} %bitcast.18), custom_call_target="tpu_custom_call" | custom-call | bytes 4194304 | tf_op jit(solution)/shard_map/pallas_call | solution.py:117
  3.2 1.5 %collective-permute-start.1 = (bf16[4,8,16,2048]{3,2,1,0:T(8,128)(2,1)S(1)}, bf16[4,8,16,2048]{3,2,1,0:T(8,128)(2,1)S(1)}, u32[]{:S(2)}, u32[]{:S(2)}) collective-permute-start(bf16[4,8,16,2048]{3,2,1,0:T(8,128)(2,1)S(1)} %shard_map.84.refs_0_), channel_id=1, source_target_pairs={{0,1},{1,0},{2,3},{3,2},{4,5},{5,4},{6,7},{7,6},{8,9},{9,8},{10,11... | collective-permute-start | bytes 6291464 | tf_op jit(solution)/shard_map/ppermute | solution.py:44
  4.7 4.3 %shard_map.85 = (bf16[4,8,16,2048]{3,2,1,0:T(8,128)(2,1)S(1)}, bf16[4,2,16,8192]{3,2,1,0:T(8,128)(2,1)S(1)}, bf16[4,2,16,8192]{3,2,1,0:T(8,128)(2,1)S(1)}) custom-call(s32[4]{0:T(128)S(1)} %pad_add_fusion.where, bf16[2,2,4,32,8192]{4,3,2,1,0:T(8,128)(2,1)} %bitcast.19, bf16[4,8,16,2048]{3,2,1,0:T(8,128)(2,1)S(1)} %shard_map.84.refs_0_), custom_call_target="tpu_custom_call" | custom-call | bytes 12582912 | tf_op jit(solution)/shard_map/pallas_call | solution.py:117
  9.6 3.2 %collective-permute-start.5 = (bf16[2,32,8192]{2,1,0:T(8,128)(2,1)S(1)}, bf16[2,32,8192]{2,1,0:T(8,128)(2,1)S(1)}, u32[]{:S(2)}, u32[]{:S(2)}) collective-permute-start(bf16[2,32,8192]{2,1,0:T(8,128)(2,1)S(1)} %fusion), channel_id=1, source_target_pairs={{0,1},{1,2},{2,3},{3,4},{4,5},{5,6},{6,7},{7,8},{8,9},{9,10},{10,1... | collective-permute-start | bytes 3145736 | tf_op jit(solution)/shard_map/ppermute | solution.py:269
  13.6 3.8 %collective-permute-start.10 = (bf16[8,16,2048]{2,1,0:T(8,128)(2,1)S(1)}, bf16[8,16,2048]{2,1,0:T(8,128)(2,1)S(1)}, u32[]{:S(2)}, u32[]{:S(2)}) collective-permute-start(bf16[8,16,2048]{2,1,0:T(8,128)(2,1)S(1)} %get-tuple-element.34.refs_2_), channel_id=1, source_target_pairs={{0,12},{1,13},{2,14},{3,15},{4,0},{5,1},{6,2},{7,3},{8,4},{9,5},{1... | collective-permute-start | bytes 1572872 | tf_op jit(solution)/shard_map/ppermute | solution.py:44
  18.3 2.8 %collective-permute-start.3 = (bf16[2,16,8192]{2,1,0:T(8,128)(2,1)S(1)}, bf16[2,16,8192]{2,1,0:T(8,128)(2,1)S(1)}, u32[]{:S(2)}, u32[]{:S(2)}) collective-permute-start(bf16[2,16,8192]{2,1,0:T(8,128)(2,1)S(1)} %get-tuple-element.36), channel_id=1, source_target_pairs={{0,32},{1,33},{2,34},{3,35},{4,36},{5,37},{6,38},{7,39},{8,40},{9,... | collective-permute-start | bytes 1572872 | tf_op jit(solution)/shard_map/ppermute | solution.py:44
  22.6 3.5 %shard_map.89 = (f32[2,32,8192]{2,1,0:T(8,128)S(1)}, f32[2,32,8192]{2,1,0:T(8,128)S(1)}, f32[2,32,8192]{2,1,0:T(8,128)S(1)}) custom-call(s32[4]{0:T(128)S(1)} %pad_add_fusion.where, f32[2,32,8192]{2,1,0:T(8,128)} %refs_0_.1, f32[2,32,8192]{2,1,0:T(8,128)} %refs_1_.1, f32[2,32,8192]{2,1,0:T(8,128)} %refs_2_.1, bf16[2,16,8192]{2,1,0:T(8,128)(2,1)S(1)} %get-tuple-element.35.refs_3_), custom_call_target="tpu_custom_call" | custom-call | flops 1048576 | bytes 6291456 | tf_op jit(solution)/shard_map/pallas_call | solution.py:151
  28.0 3.4 %collective-permute-start.11 = (bf16[8,16,2048]{2,1,0:T(8,128)(2,1)S(1)}, bf16[8,16,2048]{2,1,0:T(8,128)(2,1)S(1)}, u32[]{:S(2)}, u32[]{:S(2)}) collective-permute-start(bf16[8,16,2048]{2,1,0:T(8,128)(2,1)S(1)} %shard_map.90), channel_id=1, source_target_pairs={{0,12},{1,13},{2,14},{3,15},{4,0},{5,1},{6,2},{7,3},{8,4},{9,5},{1... | collective-permute-start | bytes 1572872 | tf_op jit(solution)/shard_map/ppermute | solution.py:44
  31.4 2.3 %collective-permute-done.3.refs_1_ = bf16[2,16,8192]{2,1,0:T(8,128)(2,1)S(1)} collective-permute-done((bf16[2,16,8192]{2,1,0:T(8,128)(2,1)S(1)}, bf16[2,16,8192]{2,1,0:T(8,128)(2,1)S(1)}, u32[]{:S(2)}, u32[]{:S(2)}) %collective-permute-start.3) | collective-permute-done | bytes 524320 | tf_op jit(solution)/shard_map/ppermute | solution.py:44
  33.7 9.6 %collective-permute-done.4.refs_2_ = bf16[2,16,8192]{2,1,0:T(8,128)(2,1)S(1)} collective-permute-done((bf16[2,16,8192]{2,1,0:T(8,128)(2,1)S(1)}, bf16[2,16,8192]{2,1,0:T(8,128)(2,1)S(1)}, u32[]{:S(2)}, u32[]{:S(2)}) %collective-permute-start.4) | collective-permute-done | bytes 524320 | tf_op jit(solution)/shard_map/ppermute | solution.py:44
  44.1 1.7 %collective-permute-start.7 = (bf16[2,16,2048]{2,1,0:T(8,128)(2,1)S(1)}, bf16[2,16,2048]{2,1,0:T(8,128)(2,1)S(1)}, u32[]{:S(2)}, u32[]{:S(2)}) collective-permute-start(bf16[2,16,2048]{2,1,0:T(8,128)(2,1)S(1)} %get-tuple-element.40), channel_id=1, source_target_pairs={{0,8},{1,9},{2,10},{3,11},{4,12},{5,13},{6,14},{7,15},{8,0},{9,1},... | collective-permute-start | bytes 393224 | tf_op jit(solution)/shard_map/ppermute | solution.py:44
  49.5 2.5 %collective-permute-start.13 = (bf16[2,16,2048]{2,1,0:T(8,128)(2,1)S(1)}, bf16[2,16,2048]{2,1,0:T(8,128)(2,1)S(1)}, u32[]{:S(2)}, u32[]{:S(2)}) collective-permute-start(bf16[2,16,2048]{2,1,0:T(8,128)(2,1)S(1)} %get-tuple-element.46), channel_id=1, source_target_pairs={{0,32},{1,33},{2,34},{3,35},{4,36},{5,37},{6,38},{7,39},{8,40},{9,... | collective-permute-start | bytes 393224 | tf_op jit(solution)/shard_map/ppermute | solution.py:44
  53.5 3.1 %collective-permute-done.13.refs_6_ = bf16[2,16,2048]{2,1,0:T(8,128)(2,1)S(1)} collective-permute-done((bf16[2,16,2048]{2,1,0:T(8,128)(2,1)S(1)}, bf16[2,16,2048]{2,1,0:T(8,128)(2,1)S(1)}, u32[]{:S(2)}, u32[]{:S(2)}) %collective-permute-start.13) | collective-permute-done | bytes 131104 | tf_op jit(solution)/shard_map/ppermute | solution.py:44
  57.5 2.6 %collective-permute-start.15 = (bf16[32,2048]{1,0:T(8,128)(2,1)S(1)}, bf16[32,2048]{1,0:T(8,128)(2,1)S(1)}, u32[]{:S(2)}, u32[]{:S(2)}) collective-permute-start(bf16[32,2048]{1,0:T(8,128)(2,1)S(1)} %get-tuple-element.48.refs_0_), channel_id=1, source_target_pairs={{0,2},{1,3},{2,0},{3,1},{4,6},{5,7},{6,4},{7,5},{8,10},{9,11},{10,... | collective-permute-start | bytes 393224 | tf_op jit(solution)/shard_map/ppermute | solution.py:44
  64.3 3.0 %collective-permute-done.16.refs_2_ = bf16[32,2048]{1,0:T(8,128)(2,1)S(1)} collective-permute-done((bf16[32,2048]{1,0:T(8,128)(2,1)S(1)}, bf16[32,2048]{1,0:T(8,128)(2,1)S(1)}, u32[]{:S(2)}, u32[]{:S(2)}) %collective-permute-start.16) | collective-permute-done | bytes 131104 | tf_op jit(solution)/shard_map/ppermute | solution.py:44
  68.0 1.6 %collective-permute-start.20 = (bf16[32,2176]{1,0:T(8,128)(2,1)S(1)}, bf16[32,2176]{1,0:T(8,128)(2,1)S(1)}, u32[]{:S(2)}, u32[]{:S(2)}) collective-permute-start(bf16[32,2176]{1,0:T(8,128)(2,1)S(1)} %shard_map.93.refs_0_), channel_id=1, source_target_pairs={{0,12},{1,13},{2,14},{3,15},{4,0},{5,1},{6,2},{7,3},{8,4},{9,5},{1... | collective-permute-start | bytes 417800 | tf_op jit(solution)/shard_map/ppermute | solution.py:44
  69.6 1.4 %collective-permute-start.18 = (bf16[32,2176]{1,0:T(8,128)(2,1)S(1)}, bf16[32,2176]{1,0:T(8,128)(2,1)S(1)}, u32[]{:S(2)}, u32[]{:S(2)}) collective-permute-start(bf16[32,2176]{1,0:T(8,128)(2,1)S(1)} %shard_map.93.refs_0_), channel_id=1, source_target_pairs={{0,8},{1,9},{2,10},{3,11},{4,12},{5,13},{6,14},{7,15},{8,0},{9,1},... | collective-permute-start | bytes 417800 | tf_op jit(solution)/shard_map/ppermute | solution.py:44
  71.9 4.3 %collective-permute-done.19.refs_2_ = bf16[32,2176]{1,0:T(8,128)(2,1)S(1)} collective-permute-done((bf16[32,2176]{1,0:T(8,128)(2,1)S(1)}, bf16[32,2176]{1,0:T(8,128)(2,1)S(1)}, u32[]{:S(2)}, u32[]{:S(2)}) %collective-permute-start.19) | collective-permute-done | bytes 139296 | tf_op jit(solution)/shard_map/ppermute | solution.py:44
  76.9 4.2 %collective-permute-start.21 = (bf16[4,32,2048]{2,1,0:T(8,128)(2,1)S(1)}, bf16[4,32,2048]{2,1,0:T(8,128)(2,1)S(1)}, u32[]{:S(2)}, u32[]{:S(2)}) collective-permute-start(bf16[4,32,2048]{2,1,0:T(8,128)(2,1)S(1)} %get-tuple-element.50.ours), channel_id=1, source_target_pairs={{0,1},{1,0},{2,3},{3,2},{4,5},{5,4},{6,7},{7,6},{8,9},{9,8},{10,11... | collective-permute-start | bytes 1572872 | tf_op jit(solution)/shard_map/ppermute | solution.py:44
  81.1 2.4 %collective-permute-start.24 = (f32[8,128]{1,0:T(8,128)S(1)}, f32[8,128]{1,0:T(8,128)S(1)}, u32[]{:S(2)}, u32[]{:S(2)}) collective-permute-start(f32[8,128]{1,0:T(8,128)S(1)} %get-tuple-element.51), channel_id=1, source_target_pairs={{0,48},{1,49},{2,50},{3,51},{4,52},{5,53},{6,54},{7,55},{8,56},{9,... | collective-permute-start | bytes 12296 | tf_op jit(solution)/shard_map/ppermute | solution.py:44
  83.5 1.4 %collective-permute-start.22 = (f32[8,128]{1,0:T(8,128)S(1)}, f32[8,128]{1,0:T(8,128)S(1)}, u32[]{:S(2)}, u32[]{:S(2)}) collective-permute-start(f32[8,128]{1,0:T(8,128)S(1)} %get-tuple-element.51), channel_id=1, source_target_pairs={{0,32},{1,33},{2,34},{3,35},{4,36},{5,37},{6,38},{7,39},{8,40},{9,... | collective-permute-start | bytes 12296 | tf_op jit(solution)/shard_map/ppermute | solution.py:44
  84.9 2.3 %collective-permute-done.23 = f32[8,128]{1,0:T(8,128)S(1)} collective-permute-done((f32[8,128]{1,0:T(8,128)S(1)}, f32[8,128]{1,0:T(8,128)S(1)}, u32[]{:S(2)}, u32[]{:S(2)}) %collective-permute-start.23) | collective-permute-done | bytes 4128 | tf_op jit(solution)/shard_map/ppermute | solution.py:44
  88.3 2.0 %collective-permute-start.26 = (f32[8,128]{1,0:T(8,128)S(1)}, f32[8,128]{1,0:T(8,128)S(1)}, u32[]{:S(2)}, u32[]{:S(2)}) collective-permute-start(f32[8,128]{1,0:T(8,128)S(1)} %add_add_fusion.1), channel_id=1, source_target_pairs={{0,64},{1,65},{2,66},{3,67},{4,68},{5,69},{6,70},{7,71},{8,72},{9,... | collective-permute-start | bytes 12296 | tf_op jit(solution)/shard_map/ppermute | solution.py:54
  91.6 4.7 %shard_map.95 = (f32[2,32,8192]{2,1,0:T(8,128)}, f32[2,32,8192]{2,1,0:T(8,128)}, f32[2,32,8192]{2,1,0:T(8,128)}, f32[2,32,8192]{2,1,0:T(8,128)}) custom-call(s32[4]{0:T(128)S(1)} %pad_add_fusion.where, bf16[4,32,2048]{2,1,0:T(8,128)(2,1)S(1)} %get-tuple-element.50.ours, bf16[4,32,2048]{2,1,0:T(8,128)(2,1)S(1)} %collective-permute-done.21.theirs, ...), custom_call_target="tpu_custom_call" | custom-call | flops 9437184 | bytes 9437184 | tf_op jit(solution)/shard_map/pallas_call | solution.py:250
  (52 shorter events, 21.6 us)
Async XLA Ops:
  3.2 9.6 %collective-permute-start.1 = (bf16[4,8,16,2048]{3,2,1,0:T(8,128)(2,1)S(1)}, bf16[4,8,16,2048]{3,2,1,0:T(8,128)(2,1)S(1)}, u32[]{:S(2)}, u32[]{:S(2)}) collective-permute-start(bf16[4,8,16,2048]{3,2,1,0:T(8,128)(2,1)S(1)} %shard_map.84.refs_0_), channel_id=1, source_target_pairs={{0,1},{1,0},{2,3},{3,2},{4,5},{5,4},{6,7},{7,6},{8,9},{9,8},{10,11... | collective-permute-start | bytes 6291464 | tf_op jit(solution)/shard_map/ppermute | solution.py:44
  9.0 8.5 %collective-permute-start = (bf16[4,2,16,8192]{3,2,1,0:T(8,128)(2,1)S(1)}, bf16[4,2,16,8192]{3,2,1,0:T(8,128)(2,1)S(1)}, u32[]{:S(2)}, u32[]{:S(2)}) collective-permute-start(bf16[4,2,16,8192]{3,2,1,0:T(8,128)(2,1)S(1)} %get-tuple-element.32), channel_id=1, source_target_pairs={{0,1},{1,0},{2,3},{3,2},{4,5},{5,4},{6,7},{7,6},{8,9},{9,8},{10,11... | collective-permute-start | bytes 6291464 | tf_op jit(solution)/shard_map/ppermute | solution.py:44
  9.6 18.3 %collective-permute-start.5 = (bf16[2,32,8192]{2,1,0:T(8,128)(2,1)S(1)}, bf16[2,32,8192]{2,1,0:T(8,128)(2,1)S(1)}, u32[]{:S(2)}, u32[]{:S(2)}) collective-permute-start(bf16[2,32,8192]{2,1,0:T(8,128)(2,1)S(1)} %fusion), channel_id=1, source_target_pairs={{0,1},{1,2},{2,3},{3,4},{4,5},{5,6},{6,7},{7,8},{8,9},{9,10},{10,1... | collective-permute-start | bytes 3145736 | tf_op jit(solution)/shard_map/ppermute | solution.py:269
  13.6 13.5 %collective-permute-start.10 = (bf16[8,16,2048]{2,1,0:T(8,128)(2,1)S(1)}, bf16[8,16,2048]{2,1,0:T(8,128)(2,1)S(1)}, u32[]{:S(2)}, u32[]{:S(2)}) collective-permute-start(bf16[8,16,2048]{2,1,0:T(8,128)(2,1)S(1)} %get-tuple-element.34.refs_2_), channel_id=1, source_target_pairs={{0,12},{1,13},{2,14},{3,15},{4,0},{5,1},{6,2},{7,3},{8,4},{9,5},{1... | collective-permute-start | bytes 1572872 | tf_op jit(solution)/shard_map/ppermute | solution.py:44
  18.3 15.3 %collective-permute-start.3 = (bf16[2,16,8192]{2,1,0:T(8,128)(2,1)S(1)}, bf16[2,16,8192]{2,1,0:T(8,128)(2,1)S(1)}, u32[]{:S(2)}, u32[]{:S(2)}) collective-permute-start(bf16[2,16,8192]{2,1,0:T(8,128)(2,1)S(1)} %get-tuple-element.36), channel_id=1, source_target_pairs={{0,32},{1,33},{2,34},{3,35},{4,36},{5,37},{6,38},{7,39},{8,40},{9,... | collective-permute-start | bytes 1572872 | tf_op jit(solution)/shard_map/ppermute | solution.py:44
  21.1 22.1 %collective-permute-start.4 = (bf16[2,16,8192]{2,1,0:T(8,128)(2,1)S(1)}, bf16[2,16,8192]{2,1,0:T(8,128)(2,1)S(1)}, u32[]{:S(2)}, u32[]{:S(2)}) collective-permute-start(bf16[2,16,8192]{2,1,0:T(8,128)(2,1)S(1)} %get-tuple-element.37), channel_id=1, source_target_pairs={{0,48},{1,49},{2,50},{3,51},{4,52},{5,53},{6,54},{7,55},{8,56},{9,... | collective-permute-start | bytes 1572872 | tf_op jit(solution)/shard_map/ppermute | solution.py:44
  22.0 21.2 %collective-permute-start.2 = (bf16[2,16,8192]{2,1,0:T(8,128)(2,1)S(1)}, bf16[2,16,8192]{2,1,0:T(8,128)(2,1)S(1)}, u32[]{:S(2)}, u32[]{:S(2)}) collective-permute-start(bf16[2,16,8192]{2,1,0:T(8,128)(2,1)S(1)} %get-tuple-element.35.refs_3_), channel_id=1, source_target_pairs={{0,16},{1,17},{2,18},{3,19},{4,20},{5,21},{6,22},{7,23},{8,24},{9,... | collective-permute-start | bytes 1572872 | tf_op jit(solution)/shard_map/ppermute | solution.py:44
  27.1 20.2 %collective-permute-start.9 = (bf16[8,16,2048]{2,1,0:T(8,128)(2,1)S(1)}, bf16[8,16,2048]{2,1,0:T(8,128)(2,1)S(1)}, u32[]{:S(2)}, u32[]{:S(2)}) collective-permute-start(bf16[8,16,2048]{2,1,0:T(8,128)(2,1)S(1)} %get-tuple-element.42), channel_id=1, source_target_pairs={{0,4},{1,5},{2,6},{3,7},{4,8},{5,9},{6,10},{7,11},{8,12},{9,13},{1... | collective-permute-start | bytes 1572872 | tf_op jit(solution)/shard_map/ppermute | solution.py:44
  28.0 19.4 %collective-permute-start.11 = (bf16[8,16,2048]{2,1,0:T(8,128)(2,1)S(1)}, bf16[8,16,2048]{2,1,0:T(8,128)(2,1)S(1)}, u32[]{:S(2)}, u32[]{:S(2)}) collective-permute-start(bf16[8,16,2048]{2,1,0:T(8,128)(2,1)S(1)} %shard_map.90), channel_id=1, source_target_pairs={{0,12},{1,13},{2,14},{3,15},{4,0},{5,1},{6,2},{7,3},{8,4},{9,5},{1... | collective-permute-start | bytes 1572872 | tf_op jit(solution)/shard_map/ppermute | solution.py:44
  44.1 7.8 %collective-permute-start.7 = (bf16[2,16,2048]{2,1,0:T(8,128)(2,1)S(1)}, bf16[2,16,2048]{2,1,0:T(8,128)(2,1)S(1)}, u32[]{:S(2)}, u32[]{:S(2)}) collective-permute-start(bf16[2,16,2048]{2,1,0:T(8,128)(2,1)S(1)} %get-tuple-element.40), channel_id=1, source_target_pairs={{0,8},{1,9},{2,10},{3,11},{4,12},{5,13},{6,14},{7,15},{8,0},{9,1},... | collective-permute-start | bytes 393224 | tf_op jit(solution)/shard_map/ppermute | solution.py:44
  45.9 7.2 %collective-permute-start.8 = (bf16[2,16,2048]{2,1,0:T(8,128)(2,1)S(1)}, bf16[2,16,2048]{2,1,0:T(8,128)(2,1)S(1)}, u32[]{:S(2)}, u32[]{:S(2)}) collective-permute-start(bf16[2,16,2048]{2,1,0:T(8,128)(2,1)S(1)} %get-tuple-element.41), channel_id=1, source_target_pairs={{0,12},{1,13},{2,14},{3,15},{4,0},{5,1},{6,2},{7,3},{8,4},{9,5},{1... | collective-permute-start | bytes 393224 | tf_op jit(solution)/shard_map/ppermute | solution.py:44
  46.3 7.0 %collective-permute-start.6 = (bf16[2,16,2048]{2,1,0:T(8,128)(2,1)S(1)}, bf16[2,16,2048]{2,1,0:T(8,128)(2,1)S(1)}, u32[]{:S(2)}, u32[]{:S(2)}) collective-permute-start(bf16[2,16,2048]{2,1,0:T(8,128)(2,1)S(1)} %get-tuple-element.39.refs_4_), channel_id=1, source_target_pairs={{0,4},{1,5},{2,6},{3,7},{4,8},{5,9},{6,10},{7,11},{8,12},{9,13},{1... | collective-permute-start | bytes 393224 | tf_op jit(solution)/shard_map/ppermute | solution.py:44
  48.2 5.4 %collective-permute-start.12 = (bf16[2,16,2048]{2,1,0:T(8,128)(2,1)S(1)}, bf16[2,16,2048]{2,1,0:T(8,128)(2,1)S(1)}, u32[]{:S(2)}, u32[]{:S(2)}) collective-permute-start(bf16[2,16,2048]{2,1,0:T(8,128)(2,1)S(1)} %get-tuple-element.45), channel_id=1, source_target_pairs={{0,16},{1,17},{2,18},{3,19},{4,20},{5,21},{6,22},{7,23},{8,24},{9,... | collective-permute-start | bytes 393224 | tf_op jit(solution)/shard_map/ppermute | solution.py:44
  49.5 7.2 %collective-permute-start.13 = (bf16[2,16,2048]{2,1,0:T(8,128)(2,1)S(1)}, bf16[2,16,2048]{2,1,0:T(8,128)(2,1)S(1)}, u32[]{:S(2)}, u32[]{:S(2)}) collective-permute-start(bf16[2,16,2048]{2,1,0:T(8,128)(2,1)S(1)} %get-tuple-element.46), channel_id=1, source_target_pairs={{0,32},{1,33},{2,34},{3,35},{4,36},{5,37},{6,38},{7,39},{8,40},{9,... | collective-permute-start | bytes 393224 | tf_op jit(solution)/shard_map/ppermute | solution.py:44
  51.9 4.9 %collective-permute-start.14 = (bf16[2,16,2048]{2,1,0:T(8,128)(2,1)S(1)}, bf16[2,16,2048]{2,1,0:T(8,128)(2,1)S(1)}, u32[]{:S(2)}, u32[]{:S(2)}) collective-permute-start(bf16[2,16,2048]{2,1,0:T(8,128)(2,1)S(1)} %get-tuple-element.47), channel_id=1, source_target_pairs={{0,48},{1,49},{2,50},{3,51},{4,52},{5,53},{6,54},{7,55},{8,56},{9,... | collective-permute-start | bytes 393224 | tf_op jit(solution)/shard_map/ppermute | solution.py:44
  57.5 5.4 %collective-permute-start.15 = (bf16[32,2048]{1,0:T(8,128)(2,1)S(1)}, bf16[32,2048]{1,0:T(8,128)(2,1)S(1)}, u32[]{:S(2)}, u32[]{:S(2)}) collective-permute-start(bf16[32,2048]{1,0:T(8,128)(2,1)S(1)} %get-tuple-element.48.refs_0_), channel_id=1, source_target_pairs={{0,2},{1,3},{2,0},{3,1},{4,6},{5,7},{6,4},{7,5},{8,10},{9,11},{10,... | collective-permute-start | bytes 393224 | tf_op jit(solution)/shard_map/ppermute | solution.py:44
  60.1 4.2 %collective-permute-start.17 = (bf16[32,2048]{1,0:T(8,128)(2,1)S(1)}, bf16[32,2048]{1,0:T(8,128)(2,1)S(1)}, u32[]{:S(2)}, u32[]{:S(2)}) collective-permute-start(bf16[32,2048]{1,0:T(8,128)(2,1)S(1)} %get-tuple-element.49), channel_id=1, source_target_pairs={{0,66},{1,67},{2,64},{3,65},{4,70},{5,71},{6,68},{7,69},{8,74},{9,... | collective-permute-start | bytes 393224 | tf_op jit(solution)/shard_map/ppermute | solution.py:44
  60.9 6.4 %collective-permute-start.16 = (bf16[32,2048]{1,0:T(8,128)(2,1)S(1)}, bf16[32,2048]{1,0:T(8,128)(2,1)S(1)}, u32[]{:S(2)}, u32[]{:S(2)}) collective-permute-start(bf16[32,2048]{1,0:T(8,128)(2,1)S(1)} %get-tuple-element.49), channel_id=1, source_target_pairs={{0,64},{1,65},{2,66},{3,67},{4,68},{5,69},{6,70},{7,71},{8,72},{9,... | collective-permute-start | bytes 393224 | tf_op jit(solution)/shard_map/ppermute | solution.py:44
  68.0 3.9 %collective-permute-start.20 = (bf16[32,2176]{1,0:T(8,128)(2,1)S(1)}, bf16[32,2176]{1,0:T(8,128)(2,1)S(1)}, u32[]{:S(2)}, u32[]{:S(2)}) collective-permute-start(bf16[32,2176]{1,0:T(8,128)(2,1)S(1)} %shard_map.93.refs_0_), channel_id=1, source_target_pairs={{0,12},{1,13},{2,14},{3,15},{4,0},{5,1},{6,2},{7,3},{8,4},{9,5},{1... | collective-permute-start | bytes 417800 | tf_op jit(solution)/shard_map/ppermute | solution.py:44
  69.6 6.6 %collective-permute-start.19 = (bf16[32,2176]{1,0:T(8,128)(2,1)S(1)}, bf16[32,2176]{1,0:T(8,128)(2,1)S(1)}, u32[]{:S(2)}, u32[]{:S(2)}) collective-permute-start(bf16[32,2176]{1,0:T(8,128)(2,1)S(1)} %shard_map.93.refs_0_), channel_id=1, source_target_pairs={{0,4},{1,5},{2,6},{3,7},{4,8},{5,9},{6,10},{7,11},{8,12},{9,13},{1... | collective-permute-start | bytes 417800 | tf_op jit(solution)/shard_map/ppermute | solution.py:44
  69.6 6.6 %collective-permute-start.18 = (bf16[32,2176]{1,0:T(8,128)(2,1)S(1)}, bf16[32,2176]{1,0:T(8,128)(2,1)S(1)}, u32[]{:S(2)}, u32[]{:S(2)}) collective-permute-start(bf16[32,2176]{1,0:T(8,128)(2,1)S(1)} %shard_map.93.refs_0_), channel_id=1, source_target_pairs={{0,8},{1,9},{2,10},{3,11},{4,12},{5,13},{6,14},{7,15},{8,0},{9,1},... | collective-permute-start | bytes 417800 | tf_op jit(solution)/shard_map/ppermute | solution.py:44
  76.9 14.7 %collective-permute-start.21 = (bf16[4,32,2048]{2,1,0:T(8,128)(2,1)S(1)}, bf16[4,32,2048]{2,1,0:T(8,128)(2,1)S(1)}, u32[]{:S(2)}, u32[]{:S(2)}) collective-permute-start(bf16[4,32,2048]{2,1,0:T(8,128)(2,1)S(1)} %get-tuple-element.50.ours), channel_id=1, source_target_pairs={{0,1},{1,0},{2,3},{3,2},{4,5},{5,4},{6,7},{7,6},{8,9},{9,8},{10,11... | collective-permute-start | bytes 1572872 | tf_op jit(solution)/shard_map/ppermute | solution.py:44
  81.1 3.8 %collective-permute-start.24 = (f32[8,128]{1,0:T(8,128)S(1)}, f32[8,128]{1,0:T(8,128)S(1)}, u32[]{:S(2)}, u32[]{:S(2)}) collective-permute-start(f32[8,128]{1,0:T(8,128)S(1)} %get-tuple-element.51), channel_id=1, source_target_pairs={{0,48},{1,49},{2,50},{3,51},{4,52},{5,53},{6,54},{7,55},{8,56},{9,... | collective-permute-start | bytes 12296 | tf_op jit(solution)/shard_map/ppermute | solution.py:44
  83.5 4.0 %collective-permute-start.22 = (f32[8,128]{1,0:T(8,128)S(1)}, f32[8,128]{1,0:T(8,128)S(1)}, u32[]{:S(2)}, u32[]{:S(2)}) collective-permute-start(f32[8,128]{1,0:T(8,128)S(1)} %get-tuple-element.51), channel_id=1, source_target_pairs={{0,32},{1,33},{2,34},{3,35},{4,36},{5,37},{6,38},{7,39},{8,40},{9,... | collective-permute-start | bytes 12296 | tf_op jit(solution)/shard_map/ppermute | solution.py:44
  (6 other events, 23.7 us)

commit v4 on v3

--- a/solution.py
+++ b/solution.py
@@ -44,9 +44,13 @@
     return lax.ppermute(value, AXES, pairs)
 
 
-def swap_x(value, mask):
-    pairs = [(rank(*s), rank(s[0] ^ mask, *s[1:])) for s in spots()]
-    return lax.ppermute(value, AXES, pairs)
+def turn(value, stage, by, by_z=None):
+    by_z = by if by_z is None else by_z
+
+    def goal(x, y, z, c):
+        return rank(x + by, y, z, c) if c == stage else rank(x, y, z + by_z, c)
+
+    return lax.ppermute(value, AXES, [(rank(*s), goal(*s)) for s in spots()])
 
 
 def move_yl(value, c=0):
@@ -81,10 +85,8 @@
     )(where, *arrays, *after)
 
 
-LEFT = (2, 16, 8192)
-RIGHT = (8, 16, 2048)
+BLOCK = (2, 4, 32, 2048)
 ORDER = (0, 1, 2, 3)
-BLOCKS = (0, 1, 2, 3)
 
 X, YL, Z, C = range(4)
 
@@ -93,36 +95,30 @@
     def body(where, src, *refs):
         outs, sems = refs[len(after) : -1], refs[-1]
         copies = []
-        for out, (own, left, offsets) in zip(outs, wanted):
+        for out, (own, offsets) in zip(outs, wanted):
             layer = where[C] if own else 1 - where[C]
+            over_x = layer == 0
             for i, k in enumerate(offsets):
-                if left:
-                    row = (where[X] + k) % 4
-                    for f in range(2):
-                        copies.append((src.at[layer, f, row, pl.ds(0, 16)], out.at[i, f]))
-                else:
-                    cols = pl.ds(pl.multiple_of((where[Z] + k) % 4 * 2048, 2048), 2048)
-                    for f in range(8):
-                        copies.append(
-                            (src.at[layer, f // 4, f % 4, pl.ds(16, 16), cols], out.at[i, f])
-                        )
+                for yl in range(2):
+                    for j in range(4):
+                        row = jnp.where(over_x, (where[X] + k) % 4, j)
+                        col = jnp.where(over_x, j, (where[Z] + k) % 4)
+                        cols = pl.ds(pl.multiple_of(col * 2048, 2048), 2048)
+                        copies.append((src.at[layer, yl, row, :, cols], out.at[i, yl, j]))
         copies = [pltpu.make_async_copy(a, b, sems.at[i]) for i, (a, b) in enumerate(copies)]
         for copy in copies:
             copy.start()
         for copy in copies:
             copy.wait()
 
-    blocks = sum(len(offsets) for _, _, offsets in wanted)
+    blocks = sum(len(offsets) for _, offsets in wanted)
     grads = pltpu.with_memory_space_constraint(grads.reshape(2, 2, 4, 32, 8192), pltpu.HBM)
     return pl.pallas_call(
         body,
         in_specs=[pl.BlockSpec(memory_space=pltpu.SMEM)]
         + [pl.BlockSpec(memory_space=pl.ANY)] * (1 + len(after)),
         out_specs=[pl.BlockSpec(memory_space=pl.ANY)] * len(wanted),
-        out_shape=[
-            pltpu.VMEM((len(offsets),) + (LEFT if left else RIGHT), BF16)
-            for _, left, offsets in wanted
-        ],
+        out_shape=[pltpu.VMEM((len(offsets),) + BLOCK, BF16) for _, offsets in wanted],
         scratch_shapes=[pltpu.SemaphoreType.DMA((8 * blocks,))],
         compiler_params=pltpu.CompilerParams(vmem_limit_bytes=4 * MIB),
         cost_estimate=pl.CostEstimate(flops=0, bytes_accessed=blocks * MIB, transcendentals=0),
@@ -167,35 +163,21 @@
     return total
 
 
-def total_of(refs, *index):
-    return add(*[wide(r[index] if index else r[...]) for r in refs])
-
-
-def pair_sum(where, mine, theirs, places, after=()):
-    dims = mine.shape[1:]
-
-    def body(where, a, b, *outs):
-        for out, k in zip(outs, places):
-            out[...] = narrow(wide(a[k]) + wide(b[k]))
-
-    return list(vmem_call(body, where, (mine, theirs), [(dims, BF16)] * len(places), after))
-
-
-def split(where, arrays, whole, cut, after):
-    dims = (2, 16, 2048)
-    count = len(arrays)
-
-    def body(where, *refs):
-        ins = list(refs[:count]) + [r.at[0] for r in refs[count:-4]]
-        for out, k in zip(refs[-4:], ORDER):
-            out[...] = total_of(ins, *cut(where, k)).astype(out.dtype)
-
-    outs = [(dims, F32)] + [(dims, BF16)] * 3
-    return list(vmem_call(body, where, list(arrays) + whole, outs, after))
-
-
-def travel(blocks, name):
-    return [move(b, **{name: k}) for k, b in zip(ORDER[1:], blocks)]
+def gate(where, value, before):
+    def body(where, value, before, out):
+        pass
+
+    value = pltpu.with_memory_space_constraint(value, pltpu.VMEM)
+    return pl.pallas_call(
+        body,
+        in_specs=[pl.BlockSpec(memory_space=pltpu.SMEM)]
+        + [pl.BlockSpec(memory_space=pl.ANY)] * 2,
+        out_specs=pl.BlockSpec(memory_space=pl.ANY),
+        out_shape=pltpu.VMEM(value.shape, value.dtype),
+        input_output_aliases={1: 0},
+        compiler_params=pltpu.CompilerParams(vmem_limit_bytes=4 * MIB),
+        cost_estimate=pl.CostEstimate(flops=MIB, bytes_accessed=MIB, transcendentals=0),
+    )(where, value, before)
 
 
 def update(where, layer, j, pieces, state, outs):
@@ -263,45 +245,52 @@
     where = jnp.stack([lax.axis_index(name) for name in ("x", "yl", "z", "c")]).astype(jnp.int32)
     grads = partial_grads[0, 0]
 
-    their_right = fetch(grads, where, [(False, False, BLOCKS)])[0]
-    got_right = move(their_right, c=1)
+    near = (1, 3, 0)
+    theirs, own = fetch(grads, where, [(False, (2,)), (True, (2,))])
+    got = move(theirs, c=1)
     base = narrow(params - snapshot[0])
     held_base = lax.ppermute(base, REP, [(i, (i + 1) % 16) for i in range(16)])
-    more = [(own, left, BLOCKS) for own, left in ((True, False), (False, True), (True, True))]
-    own_right, their_left, own_left = fetch(grads, where, more, (their_right,))
-    got_left = move(their_left, c=1)
-    far, near = pair_sum(where, own_right, got_right, (2, 1))
-    left = pair_sum(where, own_left, got_left, ORDER[1:], (far,))
-    state = preload([params, moment, second_moment], where, left[0])
-    left = travel(left, "x")
-
-    def relay(where, far, a, b, out):
-        out[...] = narrow(wide(far[...]) + wide(a[3]) + wide(b[3]))
-
-    relayed = [move(far, z=3), own_right, got_right]
-    relayed = vmem_call(relay, where, relayed, [(RIGHT, BF16)], (state[0],))[0]
-    right = [move(near, z=1), move(relayed, z=3)]
-
-    def by_z(where, k):
-        cols = pl.ds(pl.multiple_of((where[Z] + k) % 4 * 2048, 2048), 2048)
-        return slice(None), slice(None), cols
-
-    def by_x(where, k):
-        return slice(None), (where[X] + k) % 4
-
-    left = split(where, left, [own_left, got_left], by_z, (held_base,))
-    ready = left[1]
-    left = left[:1] + travel(left[1:], "z")
-    whole = [a.reshape(4, 2, 4, 16, 2048) for a in (own_right, got_right)]
-    right = split(where, [r.reshape(2, 4, 16, 2048) for r in right], whole, by_x, (ready,))
-    right = right[:1] + travel(right[1:], "x")
+    theirs = fetch(grads, where, [(False, near)], (theirs, base))[0]
+
+    def halves(where, a, b, up, down):
+        up[...] = narrow(wide(a[0, 0]) + wide(b[0, 0]))
+        down[...] = narrow(wide(a[0, 1]) + wide(b[0, 1]))
+
+    up, down = vmem_call(halves, where, [own, got], [(BLOCK[1:], BF16)] * 2)
+    got_near = move(gate(where, theirs, up), c=1)
+    own_near = fetch(grads, where, [(True, near)], (up,))[0]
+    state = preload([params, moment, second_moment], where, own_near)
+
+    def relay(where, up, down, a, b, out_up, out_down):
+        zero = jnp.zeros_like(up[...])
+        over_x = where[C] == 0
+        above, below = jnp.where(over_x, up[...], zero), jnp.where(over_x, zero, up[...])
+        out_up[0] = narrow(wide(above) + wide(a[0, 0]) + wide(b[0, 0]))
+        out_up[1] = narrow(wide(a[0, 1]) + wide(b[0, 1]))
+        out_down[0] = narrow(wide(below) + wide(a[1, 0]) + wide(b[1, 0]))
+        out_down[1] = narrow(wide(down[...]) + wide(a[1, 1]) + wide(b[1, 1]))
+
+    passed = [turn(up, 0, 1, 3), turn(down, 0, 3), own_near, got_near]
+    up, down = vmem_call(relay, where, passed, [(BLOCK, BF16)] * 2, (state[0],))
+
+    def split(where, up, down, a, b, *outs):
+        second = jnp.where(where[C] == 0, where[Z], where[X])
+        for out, k in zip(outs, ORDER):
+            j = (second + k) % 4
+            total = (wide(up[:, j]) + wide(down[:, j])) + (wide(a[2, :, j]) + wide(b[2, :, j]))
+            out[...] = total.astype(out.dtype)
+
+    dims = (2, 32, 2048)
+    received = [turn(up, 0, 1), turn(down, 0, 3), own_near, got_near]
+    outs = [(dims, F32)] + [(dims, BF16)] * 3
+    blocks = vmem_call(split, where, received, outs, (held_base,))
+    blocks = [blocks[0]] + [turn(b, 1, k) for k, b in zip(ORDER[1:], blocks[1:])]
 
     def join(where, *refs):
-        for out, index in ((refs[8], where[YL]), (refs[9], 1 - where[YL])):
-            out[:16, :] = narrow(total_of(refs[:4], index))
-            out[16:, :] = narrow(total_of(refs[4:8], index))
-
-    mine, other = vmem_call(join, where, left + right, [((32, 2048), BF16)] * 2)
+        for out, index in ((refs[4], where[YL]), (refs[5], 1 - where[YL])):
+            out[...] = narrow(add(*[wide(r[index]) for r in refs[:4]]))
+
+    mine, other = vmem_call(join, where, blocks, [((32, 2048), BF16)] * 2)
     fourth = [mine, move(mine, y=2), move(other, y=1), move(other, y=3)]
 
     def finish(where, a, b, d, e, out):
@@ -316,20 +305,20 @@
         out[:, 2048:] = narrow(tail)
 
     piece = vmem_call(finish, where, fourth, [((32, 2176), BF16)])[0]
-    ring = [piece] + [move(piece, z=k) for k in (2, 1, 3)]
+    ring = [piece] + [move(piece, z=k) for k in (1, 3, 2)]
 
     def gather(where, *refs):
         ins, out, squares = refs[:4], refs[4], refs[5]
         parts = [jnp.sum(wide(ref[:16, 2048:])[:8, :], axis=1, keepdims=True) for ref in ins]
-        for k, ref in zip((0, 2, 1, 3), ins):
+        for k, ref in zip((0, 1, 3, 2), ins):
             out[k] = ref[:, :2048]
-        total = (parts[0] + parts[1]) + (parts[2] + parts[3])
+        total = (parts[1] + parts[2]) + (parts[0] + parts[3])
         squares[...] = jnp.broadcast_to(total, (8, 128))
 
     ours, squares = vmem_call(gather, where, ring, [((4, 32, 2048), BF16), ((8, 128), F32)])
     theirs = move(ours, c=1)
     side = move(squares, x=1) + move(squares, x=3)
-    squares = (squares + move(squares, x=2)) + side
+    squares = side + (squares + move(squares, x=2))
     side = move_yl(squares) + move_yl(squares, c=1)
     squares = (squares + move(squares, c=1)) + side
     outs = update_all(where, ours, theirs, [squares, *state, held_base])

time: 96.5 us -> 92.9 us (0.963)
  starting transfers between devices: 42.7 us -> 33.5 us
  waiting for transfers between devices: 31.4 us -> 36.3 us
    ppermute x0 -> x7, waiting for transfers between devices: none -> 21.3 us  [turn(): return lax.ppermute(value, AXES, [(rank(*s), goal(*s)) for s in spots()])]
    ppermute x25 -> x13, starting transfers between devices: 36.7 us -> 16.2 us  [move(): return lax.ppermute(value, AXES, pairs)]
    ppermute x25 -> x13, waiting for transfers between devices: 30.1 us -> 13.7 us  [move(): return lax.ppermute(value, AXES, pairs)]
    ppermute x0 -> x7, starting transfers between devices: none -> 12.4 us  [turn(): return lax.ppermute(value, AXES, [(rank(*s), goal(*s)) for s in spots()])]
    pallas_call x2 -> x3, Pallas kernels: 6.7 us -> 7.96 us  [fetch(): pl.pallas_call(body, in_specs=[pl.BlockSpec(memory_space=pltpu.SMEM)] + [...]
    ppermute x1, starting transfers between devices: 3.15 us -> 1.9 us  [local(): held_base = lax.ppermute(base, REP, [(i, (i + 1) % 16) for i in range(16)])]
    pallas_call x8 -> x6, Pallas kernels: 6.18 us -> 5.11 us  [vmem_call(): pl.pallas_call(run, in_specs=[pl.BlockSpec(memory_space=pltpu.SMEM)] + [p...]
  transfers between devices with their start and end apart: 28 -> 23, of which waited for: 16 -> 13; matrix products, arithmetic and copies ran while one was open for 0% -> 0% of each run, Pallas kernels for 12% -> 11%
where the time goes in v4:
time: 92.9 us; the launch traced here: 92.7 us
  waiting for transfers between devices  36.3 us (39%)
  starting transfers between devices  33.5 us (36%)
  Pallas kernels  21.8 us (23%)
    ppermute x7, waiting for transfers between devices, turn(): return lax.ppermute(value, AXES, [(rank(*s), goal(*s)) for s in spots()])  21.3 us
    ppermute x13, starting transfers between devices, move(): return lax.ppermute(value, AXES, pairs)  16.2 us
    ppermute x13, waiting for transfers between devices, move(): return lax.ppermute(value, AXES, pairs)  13.7 us
    ppermute x7, starting transfers between devices, turn(): return lax.ppermute(value, AXES, [(rank(*s), goal(*s)) for s in spots()])  12.4 us
    pallas_call x3, Pallas kernels, fetch(): pl.pallas_call(body, in_specs=[pl.BlockSpec(memory_space=pltpu.SMEM)] + [...  7.96 us
    pallas_call x6, Pallas kernels, vmem_call(): pl.pallas_call(run, in_specs=[pl.BlockSpec(memory_space=pltpu.SMEM)] + [p...  5.11 us
    pallas_call x1, Pallas kernels, update_all(): pl.pallas_call(body, in_specs=[pl.BlockSpec(memory_space=pltpu.SMEM)] + [...  4.69 us
    pallas_call x1, Pallas kernels, preload(): pl.pallas_call(body, in_specs=[pl.BlockSpec(memory_space=pltpu.SMEM)] + [...  3.51 us
  transfers between devices with their start and end apart: 23, of which 13 were waited for; matrix products, arithmetic and copies ran while one was open for 0% of the time, Pallas kernels for 11%

profile of v4, /device:TPU:1, one launch (start us, length us, event | category | flops | bytes accessed | tf_op | source)
XLA Modules:
  0.0 92.7 jit_solution(305964933312453512)
XLA Ops:
  0.7 2.6 %shard_map.84 = (bf16[1,2,4,32,2048]{4,3,2,1,0:T(8,128)(2,1)S(1)}, bf16[1,2,4,32,2048]{4,3,2,1,0:T(8,128)(2,1)S(1)}) custom-call(s32[4]{0:T(128)S(1)} %pad_add_fusion.where, bf16[2,2,4,32,8192]{4,3,2,1,0:T(8,128)(2,1)} %bitcast.10), custom_call_target="tpu_custom_call" | custom-call | bytes 2097152 | tf_op jit(solution)/shard_map/pallas_call | solution.py:116
  3.3 1.5 %collective-permute-start = (bf16[1,2,4,32,2048]{4,3,2,1,0:T(8,128)(2,1)S(1)}, bf16[1,2,4,32,2048]{4,3,2,1,0:T(8,128)(2,1)S(1)}, u32[]{:S(2)}, u32[]{:S(2)}) collective-permute-start(bf16[1,2,4,32,2048]{4,3,2,1,0:T(8,128)(2,1)S(1)} %get-tuple-element.26.refs_0_), channel_id=1, source_target_pairs={{0,1},{1,0},{2,3},{3,2},{4,5},{5,4},{6,7},{7,6},{8,9},{9,8},{10,11... | collective-permute-start | bytes 3145736 | tf_op jit(solution)/shard_map/ppermute | solution.py:44
  5.1 2.7 %shard_map.87.value = bf16[3,2,4,32,2048]{4,3,2,1,0:T(8,128)(2,1)S(1)} custom-call(s32[4]{0:T(128)S(1)} %pad_add_fusion.where, bf16[2,2,4,32,8192]{4,3,2,1,0:T(8,128)(2,1)} %bitcast.11, bf16[1,2,4,32,2048]{4,3,2,1,0:T(8,128)(2,1)S(1)} %get-tuple-element.26.refs_0_, bf16[2,32,8192]{2,1,0:T(8,128)(2,1)S(1)} %fusion.refs_1_), custom_call_target="tpu_custom_call" | custom-call | bytes 3145728 | tf_op jit(solution)/shard_map/pallas_call | solution.py:116
  9.5 3.8 %collective-permute-start.2 = (bf16[4,32,2048]{2,1,0:T(8,128)(2,1)S(1)}, bf16[4,32,2048]{2,1,0:T(8,128)(2,1)S(1)}, u32[]{:S(2)}, u32[]{:S(2)}) collective-permute-start(bf16[4,32,2048]{2,1,0:T(8,128)(2,1)S(1)} %get-tuple-element.28), channel_id=1, source_target_pairs={{0,48},{1,13},{2,50},{3,15},{4,52},{5,1},{6,54},{7,3},{8,56},{9,5}... | collective-permute-start | bytes 1572872 | tf_op jit(solution)/shard_map/ppermute | solution.py:53
  13.5 1.9 %collective-permute-start.6 = (bf16[2,32,8192]{2,1,0:T(8,128)(2,1)S(1)}, bf16[2,32,8192]{2,1,0:T(8,128)(2,1)S(1)}, u32[]{:S(2)}, u32[]{:S(2)}) collective-permute-start(bf16[2,32,8192]{2,1,0:T(8,128)(2,1)S(1)} %fusion.refs_1_), channel_id=1, source_target_pairs={{0,1},{1,2},{2,3},{3,4},{4,5},{5,6},{6,7},{7,8},{8,9},{9,10},{10,1... | collective-permute-start | bytes 3145736 | tf_op jit(solution)/shard_map/ppermute | solution.py:252
  15.4 2.7 %shard_map.86.refs_3_.refs_2_ = bf16[3,2,4,32,2048]{4,3,2,1,0:T(8,128)(2,1)S(1)} custom-call(s32[4]{0:T(128)S(1)} %pad_add_fusion.where, bf16[2,2,4,32,8192]{4,3,2,1,0:T(8,128)(2,1)} %bitcast.12, bf16[4,32,2048]{2,1,0:T(8,128)(2,1)S(1)} %get-tuple-element.27.refs_0_.before), custom_call_target="tpu_custom_call" | custom-call | bytes 3145728 | tf_op jit(solution)/shard_map/pallas_call | solution.py:116
  18.1 3.5 %shard_map.89 = (f32[2,32,8192]{2,1,0:T(8,128)S(1)}, f32[2,32,8192]{2,1,0:T(8,128)S(1)}, f32[2,32,8192]{2,1,0:T(8,128)S(1)}) custom-call(s32[4]{0:T(128)S(1)} %pad_add_fusion.where, f32[2,32,8192]{2,1,0:T(8,128)} %refs_0_.1, f32[2,32,8192]{2,1,0:T(8,128)} %refs_1_.1, f32[2,32,8192]{2,1,0:T(8,128)} %refs_2_.1, ...), custom_call_target="tpu_custom_call" | custom-call | flops 1048576 | bytes 6291456 | tf_op jit(solution)/shard_map/pallas_call | solution.py:147
  21.6 3.5 %collective-permute-done.1.refs_0_ = bf16[4,32,2048]{2,1,0:T(8,128)(2,1)S(1)} collective-permute-done((bf16[4,32,2048]{2,1,0:T(8,128)(2,1)S(1)}, bf16[4,32,2048]{2,1,0:T(8,128)(2,1)S(1)}, u32[]{:S(2)}, u32[]{:S(2)}) %collective-permute-start.1) | collective-permute-done | bytes 524320 | tf_op jit(solution)/shard_map/ppermute | solution.py:53
  26.7 3.2 %collective-permute-start.5 = (bf16[2,4,32,2048]{3,2,1,0:T(8,128)(2,1)S(1)}, bf16[2,4,32,2048]{3,2,1,0:T(8,128)(2,1)S(1)}, u32[]{:S(2)}, u32[]{:S(2)}) collective-permute-start(bf16[2,4,32,2048]{3,2,1,0:T(8,128)(2,1)S(1)} %get-tuple-element.31), channel_id=1, source_target_pairs={{0,48},{1,13},{2,50},{3,15},{4,52},{5,1},{6,54},{7,3},{8,56},{9,5}... | collective-permute-start | bytes 3145736 | tf_op jit(solution)/shard_map/ppermute | solution.py:53
  29.9 12.1 %collective-permute-done.4.refs_0_ = bf16[2,4,32,2048]{3,2,1,0:T(8,128)(2,1)S(1)} collective-permute-done((bf16[2,4,32,2048]{3,2,1,0:T(8,128)(2,1)S(1)}, bf16[2,4,32,2048]{3,2,1,0:T(8,128)(2,1)S(1)}, u32[]{:S(2)}, u32[]{:S(2)}) %collective-permute-start.4) | collective-permute-done | bytes 1048608 | tf_op jit(solution)/shard_map/ppermute | solution.py:53
  44.4 2.5 %collective-permute-start.8 = (bf16[2,32,2048]{2,1,0:T(8,128)(2,1)S(1)}, bf16[2,32,2048]{2,1,0:T(8,128)(2,1)S(1)}, u32[]{:S(2)}, u32[]{:S(2)}) collective-permute-start(bf16[2,32,2048]{2,1,0:T(8,128)(2,1)S(1)} %get-tuple-element.34), channel_id=1, source_target_pairs={{0,8},{1,33},{2,10},{3,35},{4,12},{5,37},{6,14},{7,39},{8,0},{9,41... | collective-permute-start | bytes 786440 | tf_op jit(solution)/shard_map/ppermute | solution.py:53
  48.0 1.6 %collective-permute-done.7.refs_1_ = bf16[2,32,2048]{2,1,0:T(8,128)(2,1)S(1)} collective-permute-done((bf16[2,32,2048]{2,1,0:T(8,128)(2,1)S(1)}, bf16[2,32,2048]{2,1,0:T(8,128)(2,1)S(1)}, u32[]{:S(2)}, u32[]{:S(2)}) %collective-permute-start.7) | collective-permute-done | bytes 262176 | tf_op jit(solution)/shard_map/ppermute | solution.py:53
  49.6 4.1 %collective-permute-done.8.refs_2_ = bf16[2,32,2048]{2,1,0:T(8,128)(2,1)S(1)} collective-permute-done((bf16[2,32,2048]{2,1,0:T(8,128)(2,1)S(1)}, bf16[2,32,2048]{2,1,0:T(8,128)(2,1)S(1)}, u32[]{:S(2)}, u32[]{:S(2)}) %collective-permute-start.8) | collective-permute-done | bytes 262176 | tf_op jit(solution)/shard_map/ppermute | solution.py:53
  54.4 2.8 %collective-permute-start.10 = (bf16[32,2048]{1,0:T(8,128)(2,1)S(1)}, bf16[32,2048]{1,0:T(8,128)(2,1)S(1)}, u32[]{:S(2)}, u32[]{:S(2)}) collective-permute-start(bf16[32,2048]{1,0:T(8,128)(2,1)S(1)} %get-tuple-element.36.refs_0_), channel_id=1, source_target_pairs={{0,2},{1,3},{2,0},{3,1},{4,6},{5,7},{6,4},{7,5},{8,10},{9,11},{10,... | collective-permute-start | bytes 393224 | tf_op jit(solution)/shard_map/ppermute | solution.py:44
  58.7 1.9 %collective-permute-done.10.refs_1_ = bf16[32,2048]{1,0:T(8,128)(2,1)S(1)} collective-permute-done((bf16[32,2048]{1,0:T(8,128)(2,1)S(1)}, bf16[32,2048]{1,0:T(8,128)(2,1)S(1)}, u32[]{:S(2)}, u32[]{:S(2)}) %collective-permute-start.10) | collective-permute-done | bytes 131104 | tf_op jit(solution)/shard_map/ppermute | solution.py:44
  60.6 3.1 %collective-permute-done.12.refs_3_ = bf16[32,2048]{1,0:T(8,128)(2,1)S(1)} collective-permute-done((bf16[32,2048]{1,0:T(8,128)(2,1)S(1)}, bf16[32,2048]{1,0:T(8,128)(2,1)S(1)}, u32[]{:S(2)}, u32[]{:S(2)}) %collective-permute-start.12) | collective-permute-done | bytes 131104 | tf_op jit(solution)/shard_map/ppermute | solution.py:44
  64.5 2.5 %collective-permute-start.15 = (bf16[32,2176]{1,0:T(8,128)(2,1)S(1)}, bf16[32,2176]{1,0:T(8,128)(2,1)S(1)}, u32[]{:S(2)}, u32[]{:S(2)}) collective-permute-start(bf16[32,2176]{1,0:T(8,128)(2,1)S(1)} %shard_map.93.refs_0_), channel_id=1, source_target_pairs={{0,8},{1,9},{2,10},{3,11},{4,12},{5,13},{6,14},{7,15},{8,0},{9,1},... | collective-permute-start | bytes 417800 | tf_op jit(solution)/shard_map/ppermute | solution.py:44
  68.4 1.5 %collective-permute-done.15.refs_3_ = bf16[32,2176]{1,0:T(8,128)(2,1)S(1)} collective-permute-done((bf16[32,2176]{1,0:T(8,128)(2,1)S(1)}, bf16[32,2176]{1,0:T(8,128)(2,1)S(1)}, u32[]{:S(2)}, u32[]{:S(2)}) %collective-permute-start.15) | collective-permute-done | bytes 139296 | tf_op jit(solution)/shard_map/ppermute | solution.py:44
  69.9 4.1 %collective-permute-done.14.refs_2_ = bf16[32,2176]{1,0:T(8,128)(2,1)S(1)} collective-permute-done((bf16[32,2176]{1,0:T(8,128)(2,1)S(1)}, bf16[32,2176]{1,0:T(8,128)(2,1)S(1)}, u32[]{:S(2)}, u32[]{:S(2)}) %collective-permute-start.14) | collective-permute-done | bytes 139296 | tf_op jit(solution)/shard_map/ppermute | solution.py:44
  74.6 2.5 %collective-permute-start.16 = (bf16[4,32,2048]{2,1,0:T(8,128)(2,1)S(1)}, bf16[4,32,2048]{2,1,0:T(8,128)(2,1)S(1)}, u32[]{:S(2)}, u32[]{:S(2)}) collective-permute-start(bf16[4,32,2048]{2,1,0:T(8,128)(2,1)S(1)} %get-tuple-element.38.ours), channel_id=1, source_target_pairs={{0,1},{1,0},{2,3},{3,2},{4,5},{5,4},{6,7},{7,6},{8,9},{9,8},{10,11... | collective-permute-start | bytes 1572872 | tf_op jit(solution)/shard_map/ppermute | solution.py:44
  77.1 1.9 %collective-permute-start.19 = (f32[8,128]{1,0:T(8,128)S(1)}, f32[8,128]{1,0:T(8,128)S(1)}, u32[]{:S(2)}, u32[]{:S(2)}) collective-permute-start(f32[8,128]{1,0:T(8,128)S(1)} %get-tuple-element.39), channel_id=1, source_target_pairs={{0,32},{1,33},{2,34},{3,35},{4,36},{5,37},{6,38},{7,39},{8,40},{9,... | collective-permute-start | bytes 12296 | tf_op jit(solution)/shard_map/ppermute | solution.py:44
  81.9 1.8 %collective-permute-done.17 = f32[8,128]{1,0:T(8,128)S(1)} collective-permute-done((f32[8,128]{1,0:T(8,128)S(1)}, f32[8,128]{1,0:T(8,128)S(1)}, u32[]{:S(2)}, u32[]{:S(2)}) %collective-permute-start.17) | collective-permute-done | bytes 4128 | tf_op jit(solution)/shard_map/ppermute | solution.py:44
  85.1 1.6 %collective-permute-start.21 = (f32[8,128]{1,0:T(8,128)S(1)}, f32[8,128]{1,0:T(8,128)S(1)}, u32[]{:S(2)}, u32[]{:S(2)}) collective-permute-start(f32[8,128]{1,0:T(8,128)S(1)} %add_add_fusion.1), channel_id=1, source_target_pairs={{0,64},{1,65},{2,66},{3,67},{4,68},{5,69},{6,70},{7,71},{8,72},{9,... | collective-permute-start | bytes 12296 | tf_op jit(solution)/shard_map/ppermute | solution.py:58
  88.0 4.7 %shard_map.95 = (f32[2,32,8192]{2,1,0:T(8,128)}, f32[2,32,8192]{2,1,0:T(8,128)}, f32[2,32,8192]{2,1,0:T(8,128)}, f32[2,32,8192]{2,1,0:T(8,128)}) custom-call(s32[4]{0:T(128)S(1)} %pad_add_fusion.where, bf16[4,32,2048]{2,1,0:T(8,128)(2,1)S(1)} %get-tuple-element.38.ours, bf16[4,32,2048]{2,1,0:T(8,128)(2,1)S(1)} %collective-permute-done.16.theirs, ...), custom_call_target="tpu_custom_call" | custom-call | flops 9437184 | bytes 9437184 | tf_op jit(solution)/shard_map/pallas_call | solution.py:232
  (42 shorter events, 17.7 us)
Async XLA Ops:
  0.7 4.1 %copy-start.1 = (f32[1,2,32,8192]{3,2,1,0:T(8,128)S(1)}, f32[1,2,32,8192]{3,2,1,0:T(8,128)}, u32[]{:S(2)}) copy-start(f32[1,2,32,8192]{3,2,1,0:T(8,128)} %param.9) | copy-start | bytes 6291460
  3.3 4.5 %collective-permute-start = (bf16[1,2,4,32,2048]{4,3,2,1,0:T(8,128)(2,1)S(1)}, bf16[1,2,4,32,2048]{4,3,2,1,0:T(8,128)(2,1)S(1)}, u32[]{:S(2)}, u32[]{:S(2)}) collective-permute-start(bf16[1,2,4,32,2048]{4,3,2,1,0:T(8,128)(2,1)S(1)} %get-tuple-element.26.refs_0_), channel_id=1, source_target_pairs={{0,1},{1,0},{2,3},{3,2},{4,5},{5,4},{6,7},{7,6},{8,9},{9,8},{10,11... | collective-permute-start | bytes 3145736 | tf_op jit(solution)/shard_map/ppermute | solution.py:44
  9.1 16.0 %collective-permute-start.3 = (bf16[3,2,4,32,2048]{4,3,2,1,0:T(8,128)(2,1)S(1)}, bf16[3,2,4,32,2048]{4,3,2,1,0:T(8,128)(2,1)S(1)}, u32[]{:S(2)}, u32[]{:S(2)}) collective-permute-start(bf16[3,2,4,32,2048]{4,3,2,1,0:T(8,128)(2,1)S(1)} %shard_map.88), channel_id=1, source_target_pairs={{0,1},{1,0},{2,3},{3,2},{4,5},{5,4},{6,7},{7,6},{8,9},{9,8},{10,11... | collective-permute-start | bytes 9437192 | tf_op jit(solution)/shard_map/ppermute | solution.py:44
  9.5 12.1 %collective-permute-start.2 = (bf16[4,32,2048]{2,1,0:T(8,128)(2,1)S(1)}, bf16[4,32,2048]{2,1,0:T(8,128)(2,1)S(1)}, u32[]{:S(2)}, u32[]{:S(2)}) collective-permute-start(bf16[4,32,2048]{2,1,0:T(8,128)(2,1)S(1)} %get-tuple-element.28), channel_id=1, source_target_pairs={{0,48},{1,13},{2,50},{3,15},{4,52},{5,1},{6,54},{7,3},{8,56},{9,5}... | collective-permute-start | bytes 1572872 | tf_op jit(solution)/shard_map/ppermute | solution.py:53
  13.4 11.7 %collective-permute-start.1 = (bf16[4,32,2048]{2,1,0:T(8,128)(2,1)S(1)}, bf16[4,32,2048]{2,1,0:T(8,128)(2,1)S(1)}, u32[]{:S(2)}, u32[]{:S(2)}) collective-permute-start(bf16[4,32,2048]{2,1,0:T(8,128)(2,1)S(1)} %get-tuple-element.27.refs_0_.before), channel_id=1, source_target_pairs={{0,16},{1,13},{2,18},{3,15},{4,20},{5,1},{6,22},{7,3},{8,24},{9,5}... | collective-permute-start | bytes 1572872 | tf_op jit(solution)/shard_map/ppermute | solution.py:53
  13.5 16.5 %collective-permute-start.6 = (bf16[2,32,8192]{2,1,0:T(8,128)(2,1)S(1)}, bf16[2,32,8192]{2,1,0:T(8,128)(2,1)S(1)}, u32[]{:S(2)}, u32[]{:S(2)}) collective-permute-start(bf16[2,32,8192]{2,1,0:T(8,128)(2,1)S(1)} %fusion.refs_1_), channel_id=1, source_target_pairs={{0,1},{1,2},{2,3},{3,4},{4,5},{5,6},{6,7},{7,8},{8,9},{9,10},{10,1... | collective-permute-start | bytes 3145736 | tf_op jit(solution)/shard_map/ppermute | solution.py:252
  26.4 15.7 %collective-permute-start.4 = (bf16[2,4,32,2048]{3,2,1,0:T(8,128)(2,1)S(1)}, bf16[2,4,32,2048]{3,2,1,0:T(8,128)(2,1)S(1)}, u32[]{:S(2)}, u32[]{:S(2)}) collective-permute-start(bf16[2,4,32,2048]{3,2,1,0:T(8,128)(2,1)S(1)} %get-tuple-element.30), channel_id=1, source_target_pairs={{0,16},{1,5},{2,18},{3,7},{4,20},{5,9},{6,22},{7,11},{8,24},{9,13}... | collective-permute-start | bytes 3145736 | tf_op jit(solution)/shard_map/ppermute | solution.py:53
  26.7 15.3 %collective-permute-start.5 = (bf16[2,4,32,2048]{3,2,1,0:T(8,128)(2,1)S(1)}, bf16[2,4,32,2048]{3,2,1,0:T(8,128)(2,1)S(1)}, u32[]{:S(2)}, u32[]{:S(2)}) collective-permute-start(bf16[2,4,32,2048]{3,2,1,0:T(8,128)(2,1)S(1)} %get-tuple-element.31), channel_id=1, source_target_pairs={{0,48},{1,13},{2,50},{3,15},{4,52},{5,1},{6,54},{7,3},{8,56},{9,5}... | collective-permute-start | bytes 3145736 | tf_op jit(solution)/shard_map/ppermute | solution.py:53
  43.1 6.5 %collective-permute-start.7 = (bf16[2,32,2048]{2,1,0:T(8,128)(2,1)S(1)}, bf16[2,32,2048]{2,1,0:T(8,128)(2,1)S(1)}, u32[]{:S(2)}, u32[]{:S(2)}) collective-permute-start(bf16[2,32,2048]{2,1,0:T(8,128)(2,1)S(1)} %get-tuple-element.33), channel_id=1, source_target_pairs={{0,4},{1,17},{2,6},{3,19},{4,8},{5,21},{6,10},{7,23},{8,12},{9,25}... | collective-permute-start | bytes 786440 | tf_op jit(solution)/shard_map/ppermute | solution.py:53
  44.4 9.3 %collective-permute-start.8 = (bf16[2,32,2048]{2,1,0:T(8,128)(2,1)S(1)}, bf16[2,32,2048]{2,1,0:T(8,128)(2,1)S(1)}, u32[]{:S(2)}, u32[]{:S(2)}) collective-permute-start(bf16[2,32,2048]{2,1,0:T(8,128)(2,1)S(1)} %get-tuple-element.34), channel_id=1, source_target_pairs={{0,8},{1,33},{2,10},{3,35},{4,12},{5,37},{6,14},{7,39},{8,0},{9,41... | collective-permute-start | bytes 786440 | tf_op jit(solution)/shard_map/ppermute | solution.py:53
  46.8 6.9 %collective-permute-start.9 = (bf16[2,32,2048]{2,1,0:T(8,128)(2,1)S(1)}, bf16[2,32,2048]{2,1,0:T(8,128)(2,1)S(1)}, u32[]{:S(2)}, u32[]{:S(2)}) collective-permute-start(bf16[2,32,2048]{2,1,0:T(8,128)(2,1)S(1)} %get-tuple-element.35), channel_id=1, source_target_pairs={{0,12},{1,49},{2,14},{3,51},{4,0},{5,53},{6,2},{7,55},{8,4},{9,57}... | collective-permute-start | bytes 786440 | tf_op jit(solution)/shard_map/ppermute | solution.py:53
  54.4 6.3 %collective-permute-start.10 = (bf16[32,2048]{1,0:T(8,128)(2,1)S(1)}, bf16[32,2048]{1,0:T(8,128)(2,1)S(1)}, u32[]{:S(2)}, u32[]{:S(2)}) collective-permute-start(bf16[32,2048]{1,0:T(8,128)(2,1)S(1)} %get-tuple-element.36.refs_0_), channel_id=1, source_target_pairs={{0,2},{1,3},{2,0},{3,1},{4,6},{5,7},{6,4},{7,5},{8,10},{9,11},{10,... | collective-permute-start | bytes 393224 | tf_op jit(solution)/shard_map/ppermute | solution.py:44
  57.2 6.6 %collective-permute-start.12 = (bf16[32,2048]{1,0:T(8,128)(2,1)S(1)}, bf16[32,2048]{1,0:T(8,128)(2,1)S(1)}, u32[]{:S(2)}, u32[]{:S(2)}) collective-permute-start(bf16[32,2048]{1,0:T(8,128)(2,1)S(1)} %get-tuple-element.37), channel_id=1, source_target_pairs={{0,66},{1,67},{2,64},{3,65},{4,70},{5,71},{6,68},{7,69},{8,74},{9,... | collective-permute-start | bytes 393224 | tf_op jit(solution)/shard_map/ppermute | solution.py:44
  58.1 5.6 %collective-permute-start.11 = (bf16[32,2048]{1,0:T(8,128)(2,1)S(1)}, bf16[32,2048]{1,0:T(8,128)(2,1)S(1)}, u32[]{:S(2)}, u32[]{:S(2)}) collective-permute-start(bf16[32,2048]{1,0:T(8,128)(2,1)S(1)} %get-tuple-element.37), channel_id=1, source_target_pairs={{0,64},{1,65},{2,66},{3,67},{4,68},{5,69},{6,70},{7,71},{8,72},{9,... | collective-permute-start | bytes 393224 | tf_op jit(solution)/shard_map/ppermute | solution.py:44
  64.5 5.4 %collective-permute-start.15 = (bf16[32,2176]{1,0:T(8,128)(2,1)S(1)}, bf16[32,2176]{1,0:T(8,128)(2,1)S(1)}, u32[]{:S(2)}, u32[]{:S(2)}) collective-permute-start(bf16[32,2176]{1,0:T(8,128)(2,1)S(1)} %shard_map.93.refs_0_), channel_id=1, source_target_pairs={{0,8},{1,9},{2,10},{3,11},{4,12},{5,13},{6,14},{7,15},{8,0},{9,1},... | collective-permute-start | bytes 417800 | tf_op jit(solution)/shard_map/ppermute | solution.py:44
  67.0 7.0 %collective-permute-start.14 = (bf16[32,2176]{1,0:T(8,128)(2,1)S(1)}, bf16[32,2176]{1,0:T(8,128)(2,1)S(1)}, u32[]{:S(2)}, u32[]{:S(2)}) collective-permute-start(bf16[32,2176]{1,0:T(8,128)(2,1)S(1)} %shard_map.93.refs_0_), channel_id=1, source_target_pairs={{0,12},{1,13},{2,14},{3,15},{4,0},{5,1},{6,2},{7,3},{8,4},{9,5},{1... | collective-permute-start | bytes 417800 | tf_op jit(solution)/shard_map/ppermute | solution.py:44
  67.6 6.4 %collective-permute-start.13 = (bf16[32,2176]{1,0:T(8,128)(2,1)S(1)}, bf16[32,2176]{1,0:T(8,128)(2,1)S(1)}, u32[]{:S(2)}, u32[]{:S(2)}) collective-permute-start(bf16[32,2176]{1,0:T(8,128)(2,1)S(1)} %shard_map.93.refs_0_), channel_id=1, source_target_pairs={{0,4},{1,5},{2,6},{3,7},{4,8},{5,9},{6,10},{7,11},{8,12},{9,13},{1... | collective-permute-start | bytes 417800 | tf_op jit(solution)/shard_map/ppermute | solution.py:44
  74.6 13.4 %collective-permute-start.16 = (bf16[4,32,2048]{2,1,0:T(8,128)(2,1)S(1)}, bf16[4,32,2048]{2,1,0:T(8,128)(2,1)S(1)}, u32[]{:S(2)}, u32[]{:S(2)}) collective-permute-start(bf16[4,32,2048]{2,1,0:T(8,128)(2,1)S(1)} %get-tuple-element.38.ours), channel_id=1, source_target_pairs={{0,1},{1,0},{2,3},{3,2},{4,5},{5,4},{6,7},{7,6},{8,9},{9,8},{10,11... | collective-permute-start | bytes 1572872 | tf_op jit(solution)/shard_map/ppermute | solution.py:44
  77.1 4.0 %collective-permute-start.19 = (f32[8,128]{1,0:T(8,128)S(1)}, f32[8,128]{1,0:T(8,128)S(1)}, u32[]{:S(2)}, u32[]{:S(2)}) collective-permute-start(f32[8,128]{1,0:T(8,128)S(1)} %get-tuple-element.39), channel_id=1, source_target_pairs={{0,32},{1,33},{2,34},{3,35},{4,36},{5,37},{6,38},{7,39},{8,40},{9,... | collective-permute-start | bytes 12296 | tf_op jit(solution)/shard_map/ppermute | solution.py:44
  79.1 2.9 %collective-permute-start.18 = (f32[8,128]{1,0:T(8,128)S(1)}, f32[8,128]{1,0:T(8,128)S(1)}, u32[]{:S(2)}, u32[]{:S(2)}) collective-permute-start(f32[8,128]{1,0:T(8,128)S(1)} %get-tuple-element.39), channel_id=1, source_target_pairs={{0,48},{1,49},{2,50},{3,51},{4,52},{5,53},{6,54},{7,55},{8,56},{9,... | collective-permute-start | bytes 12296 | tf_op jit(solution)/shard_map/ppermute | solution.py:44
  80.1 3.7 %collective-permute-start.17 = (f32[8,128]{1,0:T(8,128)S(1)}, f32[8,128]{1,0:T(8,128)S(1)}, u32[]{:S(2)}, u32[]{:S(2)}) collective-permute-start(f32[8,128]{1,0:T(8,128)S(1)} %get-tuple-element.39), channel_id=1, source_target_pairs={{0,16},{1,17},{2,18},{3,19},{4,20},{5,21},{6,22},{7,23},{8,24},{9,... | collective-permute-start | bytes 12296 | tf_op jit(solution)/shard_map/ppermute | solution.py:44
  83.8 3.0 %collective-permute-start.22 = (f32[8,128]{1,0:T(8,128)S(1)}, f32[8,128]{1,0:T(8,128)S(1)}, u32[]{:S(2)}, u32[]{:S(2)}) collective-permute-start(f32[8,128]{1,0:T(8,128)S(1)} %add_add_fusion.1), channel_id=1, source_target_pairs={{0,65},{1,64},{2,67},{3,66},{4,69},{5,68},{6,71},{7,70},{8,73},{9,... | collective-permute-start | bytes 12296 | tf_op jit(solution)/shard_map/ppermute | solution.py:58
  85.1 2.9 %collective-permute-start.21 = (f32[8,128]{1,0:T(8,128)S(1)}, f32[8,128]{1,0:T(8,128)S(1)}, u32[]{:S(2)}, u32[]{:S(2)}) collective-permute-start(f32[8,128]{1,0:T(8,128)S(1)} %add_add_fusion.1), channel_id=1, source_target_pairs={{0,64},{1,65},{2,66},{3,67},{4,68},{5,69},{6,70},{7,71},{8,72},{9,... | collective-permute-start | bytes 12296 | tf_op jit(solution)/shard_map/ppermute | solution.py:58
  86.7 1.3 %collective-permute-start.20 = (f32[8,128]{1,0:T(8,128)S(1)}, f32[8,128]{1,0:T(8,128)S(1)}, u32[]{:S(2)}, u32[]{:S(2)}) collective-permute-start(f32[8,128]{1,0:T(8,128)S(1)} %add_add_fusion.1), channel_id=1, source_target_pairs={{0,1},{1,0},{2,3},{3,2},{4,5},{5,4},{6,7},{7,6},{8,9},{9,8},{10,11... | collective-permute-start | bytes 12296 | tf_op jit(solution)/shard_map/ppermute | solution.py:44
  (1 other events, 4.1 us)

commit v5 on v4

--- a/solution.py
+++ b/solution.py
@@ -86,7 +86,7 @@
 
 
 BLOCK = (2, 4, 32, 2048)
-ORDER = (0, 1, 2, 3)
+ORDER = (0, 2, 1, 3)
 
 X, YL, Z, C = range(4)
 
@@ -125,11 +125,11 @@
     )(where, grads, *after)
 
 
-def preload(arrays, where, before):
+def preload(arrays, where, *before):
     count = len(arrays)
 
     def body(where, *refs):
-        ins, outs, sems = refs[:count], refs[count + 1 : -1], refs[-1]
+        ins, outs, sems = refs[:count], refs[-1 - count : -1], refs[-1]
         copies = [
             pltpu.make_async_copy(
                 a.at[l, pl.ds(8 * r, 8)], b.at[l, pl.ds(8 * r, 8)], sems.at[i, l, r]
@@ -147,13 +147,13 @@
     return pl.pallas_call(
         body,
         in_specs=[pl.BlockSpec(memory_space=pltpu.SMEM)]
-        + [pl.BlockSpec(memory_space=pl.ANY)] * (count + 1),
+        + [pl.BlockSpec(memory_space=pl.ANY)] * (count + len(before)),
         out_specs=[pl.BlockSpec(memory_space=pl.ANY)] * count,
         out_shape=[pltpu.VMEM(a.shape, a.dtype) for a in arrays],
         scratch_shapes=[pltpu.SemaphoreType.DMA((count, 2, 4))],
         compiler_params=pltpu.CompilerParams(vmem_limit_bytes=4 * MIB),
         cost_estimate=pl.CostEstimate(flops=MIB, bytes_accessed=6 * MIB, transcendentals=0),
-    )(where, *arrays, before)
+    )(where, *arrays, *before)
 
 
 def add(*terms):
@@ -163,41 +163,28 @@
     return total
 
 
-def gate(where, value, before):
-    def body(where, value, before, out):
-        pass
-
-    value = pltpu.with_memory_space_constraint(value, pltpu.VMEM)
-    return pl.pallas_call(
-        body,
-        in_specs=[pl.BlockSpec(memory_space=pltpu.SMEM)]
-        + [pl.BlockSpec(memory_space=pl.ANY)] * 2,
-        out_specs=pl.BlockSpec(memory_space=pl.ANY),
-        out_shape=pltpu.VMEM(value.shape, value.dtype),
-        input_output_aliases={1: 0},
-        compiler_params=pltpu.CompilerParams(vmem_limit_bytes=4 * MIB),
-        cost_estimate=pl.CostEstimate(flops=MIB, bytes_accessed=MIB, transcendentals=0),
-    )(where, value, before)
-
-
 def update(where, layer, j, pieces, state, outs):
     sq, p, m, v, base = state
     clip_factor = lax.rsqrt(sq[0:1, 0:1] / (2 * 256 * 8192) + rms_eps)
     place = (where[Z] - j + 4) % 4
+    first_gain = (1.0 - beta_first) * clip_factor
+    second_gain = (1.0 - beta_second) * clip_factor * clip_factor
     for g in range(2048 // QBLOCK):
         cols = pl.ds(pl.multiple_of(j * 2048 + g * QBLOCK, QBLOCK), QBLOCK)
-        clipped = clip_factor * wide(pieces[place, :, g * QBLOCK : (g + 1) * QBLOCK])
-        new_m = beta_first * m[layer, :, cols] + (1.0 - beta_first) * clipped
-        new_v = beta_second * v[layer, :, cols] + (1.0 - beta_second) * clipped * clipped
+        summed = wide(pieces[place, :, g * QBLOCK : (g + 1) * QBLOCK])
+        new_m = beta_first * m[layer, :, cols] + first_gain * summed
+        new_v = beta_second * v[layer, :, cols] + second_gain * summed * summed
+        root = new_v * lax.rsqrt(new_v)
         old = p[layer, :, cols]
-        change = -learn_rate * (new_m / (jnp.sqrt(new_v) + adam_eps) + decay_rate * old)
+        change = -learn_rate * (new_m / (root + adam_eps) + decay_rate * old)
         outs[0][:, cols] = old + change
         outs[1][:, cols] = new_m
         outs[2][:, cols] = new_v
         delta = change + wide(base[layer, :, cols])
         scale = jnp.max(jnp.abs(delta), axis=1, keepdims=True) + scale_eps
         scale = wide(narrow(scale))
-        outs[3][:, cols] = wide(narrow(delta / scale)) * scale
+        held = wide(narrow(delta * (1.0 / scale)))
+        outs[3][:, cols] = held * scale
 
 
 def update_all(where, ours, theirs, state):
@@ -252,38 +239,57 @@
     held_base = lax.ppermute(base, REP, [(i, (i + 1) % 16) for i in range(16)])
     theirs = fetch(grads, where, [(False, near)], (theirs, base))[0]
 
-    def halves(where, a, b, up, down):
+    def halves(where, a, b, rest, up, down, same):
         up[...] = narrow(wide(a[0, 0]) + wide(b[0, 0]))
         down[...] = narrow(wide(a[0, 1]) + wide(b[0, 1]))
 
-    up, down = vmem_call(halves, where, [own, got], [(BLOCK[1:], BF16)] * 2)
-    got_near = move(gate(where, theirs, up), c=1)
+    passed = [pltpu.with_memory_space_constraint(r, pltpu.VMEM) for r in (own, got, theirs)]
+    up, down, theirs = pl.pallas_call(
+        halves,
+        in_specs=[pl.BlockSpec(memory_space=pltpu.SMEM)]
+        + [pl.BlockSpec(memory_space=pltpu.VMEM)] * 2
+        + [pl.BlockSpec(memory_space=pl.ANY)],
+        out_specs=[pl.BlockSpec(memory_space=pltpu.VMEM)] * 2 + [pl.BlockSpec(memory_space=pl.ANY)],
+        out_shape=[pltpu.VMEM(BLOCK[1:], BF16)] * 2 + [pltpu.VMEM(theirs.shape, BF16)],
+        input_output_aliases={3: 2},
+        compiler_params=pltpu.CompilerParams(vmem_limit_bytes=12 * MIB),
+        cost_estimate=pl.CostEstimate(flops=4 * MIB, bytes_accessed=4 * MIB, transcendentals=0),
+    )(where, *passed)
+    got_near = move(theirs, c=1)
     own_near = fetch(grads, where, [(True, near)], (up,))[0]
-    state = preload([params, moment, second_moment], where, own_near)
-
-    def relay(where, up, down, a, b, out_up, out_down):
+
+    def relay_down(where, down, a, b, out, up_1):
+        out[...] = narrow(wide(down[...]) + wide(a[1, 1]) + wide(b[1, 1]))
+        up_1[...] = narrow(wide(a[0, 1]) + wide(b[0, 1]))
+
+    passed = [turn(down, 0, 3), own_near, got_near]
+    down, up_1 = vmem_call(relay_down, where, passed, [(BLOCK[1:], BF16)] * 2)
+
+    def relay_up(where, up, a, b, other, up_0):
         zero = jnp.zeros_like(up[...])
         over_x = where[C] == 0
         above, below = jnp.where(over_x, up[...], zero), jnp.where(over_x, zero, up[...])
-        out_up[0] = narrow(wide(above) + wide(a[0, 0]) + wide(b[0, 0]))
-        out_up[1] = narrow(wide(a[0, 1]) + wide(b[0, 1]))
-        out_down[0] = narrow(wide(below) + wide(a[1, 0]) + wide(b[1, 0]))
-        out_down[1] = narrow(wide(down[...]) + wide(a[1, 1]) + wide(b[1, 1]))
-
-    passed = [turn(up, 0, 1, 3), turn(down, 0, 3), own_near, got_near]
-    up, down = vmem_call(relay, where, passed, [(BLOCK, BF16)] * 2, (state[0],))
-
-    def split(where, up, down, a, b, *outs):
-        second = jnp.where(where[C] == 0, where[Z], where[X])
+        other[...] = narrow(wide(below) + wide(a[1, 0]) + wide(b[1, 0]))
+        up_0[...] = narrow(wide(above) + wide(a[0, 0]) + wide(b[0, 0]))
+
+    passed = [turn(up, 0, 1, 3), own_near, got_near]
+    outs = [(BLOCK[1:], BF16)] * 2
+    other, up_0 = vmem_call(relay_up, where, passed, outs, (down,))
+
+    def split(where, first, second, up_0, up_1, a, b, *outs):
+        axis = jnp.where(where[C] == 0, where[Z], where[X])
         for out, k in zip(outs, ORDER):
-            j = (second + k) % 4
-            total = (wide(up[:, j]) + wide(down[:, j])) + (wide(a[2, :, j]) + wide(b[2, :, j]))
-            out[...] = total.astype(out.dtype)
+            j = (axis + k) % 4
+            for yl, (up, down) in enumerate(((up_0, second), (up_1, first))):
+                total = (wide(up[j]) + wide(down[j])) + (wide(a[2, yl, j]) + wide(b[2, yl, j]))
+                out[yl] = total.astype(out.dtype)
 
     dims = (2, 32, 2048)
-    received = [turn(up, 0, 1), turn(down, 0, 3), own_near, got_near]
+    received = [turn(down, 0, 3), turn(other, 0, 3), turn(up_0, 0, 1), turn(up_1, 0, 1)]
+    state = preload([params, moment, second_moment], where, received[0], received[3])
     outs = [(dims, F32)] + [(dims, BF16)] * 3
-    blocks = vmem_call(split, where, received, outs, (held_base,))
+    received += [own_near, got_near]
+    blocks = vmem_call(split, where, received, outs, (held_base, state[0]))
     blocks = [blocks[0]] + [turn(b, 1, k) for k, b in zip(ORDER[1:], blocks[1:])]
 
     def join(where, *refs):

time: 92.9 us -> 89.7 us (0.966)
  waiting for transfers between devices: 36.3 us -> 33.1 us
    ppermute x7 -> x9, waiting for transfers between devices: 21.3 us -> 15.9 us  [turn(): return lax.ppermute(value, AXES, [(rank(*s), goal(*s)) for s in spots()])]
    ppermute x7 -> x9, starting transfers between devices: 12.4 us -> 15.8 us  [turn(): return lax.ppermute(value, AXES, [(rank(*s), goal(*s)) for s in spots()])]
    ppermute x13, starting transfers between devices: 16.2 us -> 13.1 us  [move(): return lax.ppermute(value, AXES, pairs)]
    ppermute x13, waiting for transfers between devices: 13.7 us -> 15.9 us  [move(): return lax.ppermute(value, AXES, pairs)]
  transfers between devices with their start and end apart: 23 -> 25, of which waited for: 13 -> 16; matrix products, arithmetic and copies ran while one was open for 0% -> 0% of each run, Pallas kernels for 11% -> 12%
where the time goes in v5:
time: 89.7 us; the launch traced here: 89.5 us
  starting transfers between devices  33.9 us (38%)
  waiting for transfers between devices  33.1 us (37%)
  Pallas kernels  21.5 us (24%)
    ppermute x13, waiting for transfers between devices, move(): return lax.ppermute(value, AXES, pairs)  15.9 us
    ppermute x9, waiting for transfers between devices, turn(): return lax.ppermute(value, AXES, [(rank(*s), goal(*s)) for s in spots()])  15.9 us
    ppermute x9, starting transfers between devices, turn(): return lax.ppermute(value, AXES, [(rank(*s), goal(*s)) for s in spots()])  15.8 us
    ppermute x13, starting transfers between devices, move(): return lax.ppermute(value, AXES, pairs)  13.1 us
    pallas_call x3, Pallas kernels, fetch(): pl.pallas_call(body, in_specs=[pl.BlockSpec(memory_space=pltpu.SMEM)] + [...  7.96 us
    pallas_call x6, Pallas kernels, vmem_call(): pl.pallas_call(run, in_specs=[pl.BlockSpec(memory_space=pltpu.SMEM)] + [p...  4.87 us
    pallas_call x1, Pallas kernels, update_all(): pl.pallas_call(body, in_specs=[pl.BlockSpec(memory_space=pltpu.SMEM)] + [...  4.34 us
    pallas_call x1, Pallas kernels, preload(): pl.pallas_call(body, in_specs=[pl.BlockSpec(memory_space=pltpu.SMEM)] + [...  3.51 us
  transfers between devices with their start and end apart: 25, of which 16 were waited for; matrix products, arithmetic and copies ran while one was open for 0% of the time, Pallas kernels for 12%

profile of v5, /device:TPU:1, one launch (start us, length us, event | category | flops | bytes accessed | tf_op | source)
XLA Modules:
  0.0 89.5 jit_solution(4482802839815787490)
XLA Ops:
  0.7 2.6 %shard_map.84 = (bf16[1,2,4,32,2048]{4,3,2,1,0:T(8,128)(2,1)S(1)}, bf16[1,2,4,32,2048]{4,3,2,1,0:T(8,128)(2,1)S(1)}) custom-call(s32[4]{0:T(128)S(1)} %pad_add_fusion.where, bf16[2,2,4,32,8192]{4,3,2,1,0:T(8,128)(2,1)} %bitcast.10), custom_call_target="tpu_custom_call" | custom-call | bytes 2097152 | tf_op jit(solution)/shard_map/pallas_call | solution.py:116
  5.0 2.7 %shard_map.85.rest = bf16[3,2,4,32,2048]{4,3,2,1,0:T(8,128)(2,1)S(1)} custom-call(s32[4]{0:T(128)S(1)} %pad_add_fusion.where, bf16[2,2,4,32,8192]{4,3,2,1,0:T(8,128)(2,1)} %bitcast.11, bf16[1,2,4,32,2048]{4,3,2,1,0:T(8,128)(2,1)S(1)} %get-tuple-element.29.refs_0_, bf16[2,32,8192]{2,1,0:T(8,128)(2,1)S(1)} %fusion.refs_1_), custom_call_target="tpu_custom_call" | custom-call | bytes 3145728 | tf_op jit(solution)/shard_map/pallas_call | solution.py:116
  8.9 3.8 %collective-permute-start.1 = (bf16[4,32,2048]{2,1,0:T(8,128)(2,1)S(1)}, bf16[4,32,2048]{2,1,0:T(8,128)(2,1)S(1)}, u32[]{:S(2)}, u32[]{:S(2)}) collective-permute-start(bf16[4,32,2048]{2,1,0:T(8,128)(2,1)S(1)} %get-tuple-element.30), channel_id=1, source_target_pairs={{0,48},{1,13},{2,50},{3,15},{4,52},{5,1},{6,54},{7,3},{8,56},{9,5}... | collective-permute-start | bytes 1572872 | tf_op jit(solution)/shard_map/ppermute | solution.py:53
  12.8 1.9 %collective-permute-start.8 = (bf16[2,32,8192]{2,1,0:T(8,128)(2,1)S(1)}, bf16[2,32,8192]{2,1,0:T(8,128)(2,1)S(1)}, u32[]{:S(2)}, u32[]{:S(2)}) collective-permute-start(bf16[2,32,8192]{2,1,0:T(8,128)(2,1)S(1)} %fusion.refs_1_), channel_id=1, source_target_pairs={{0,1},{1,2},{2,3},{3,4},{4,5},{5,6},{6,7},{7,8},{8,9},{9,10},{10,1... | collective-permute-start | bytes 3145736 | tf_op jit(solution)/shard_map/ppermute | solution.py:239
  14.7 2.7 %shard_map.87.refs_1_.refs_4_ = bf16[3,2,4,32,2048]{4,3,2,1,0:T(8,128)(2,1)S(1)} custom-call(s32[4]{0:T(128)S(1)} %pad_add_fusion.where, bf16[2,2,4,32,8192]{4,3,2,1,0:T(8,128)(2,1)} %bitcast.12, bf16[4,32,2048]{2,1,0:T(8,128)(2,1)S(1)} %get-tuple-element.31.refs_0_), custom_call_target="tpu_custom_call" | custom-call | bytes 3145728 | tf_op jit(solution)/shard_map/pallas_call | solution.py:116
  20.0 3.2 %collective-permute-start.3 = (bf16[4,32,2048]{2,1,0:T(8,128)(2,1)S(1)}, bf16[4,32,2048]{2,1,0:T(8,128)(2,1)S(1)}, u32[]{:S(2)}, u32[]{:S(2)}) collective-permute-start(bf16[4,32,2048]{2,1,0:T(8,128)(2,1)S(1)} %get-tuple-element.33.refs_3_), channel_id=1, source_target_pairs={{0,48},{1,13},{2,50},{3,15},{4,52},{5,1},{6,54},{7,3},{8,56},{9,5}... | collective-permute-start | bytes 1572872 | tf_op jit(solution)/shard_map/ppermute | solution.py:53
  25.4 3.5 %collective-permute-start.5 = (bf16[4,32,2048]{2,1,0:T(8,128)(2,1)S(1)}, bf16[4,32,2048]{2,1,0:T(8,128)(2,1)S(1)}, u32[]{:S(2)}, u32[]{:S(2)}) collective-permute-start(bf16[4,32,2048]{2,1,0:T(8,128)(2,1)S(1)} %get-tuple-element.34), channel_id=1, source_target_pairs={{0,48},{1,13},{2,50},{3,15},{4,52},{5,1},{6,54},{7,3},{8,56},{9,5}... | collective-permute-start | bytes 1572872 | tf_op jit(solution)/shard_map/ppermute | solution.py:53
  28.9 6.1 %collective-permute-done.7.refs_4_.refs_3_ = bf16[4,32,2048]{2,1,0:T(8,128)(2,1)S(1)} collective-permute-done((bf16[4,32,2048]{2,1,0:T(8,128)(2,1)S(1)}, bf16[4,32,2048]{2,1,0:T(8,128)(2,1)S(1)}, u32[]{:S(2)}, u32[]{:S(2)}) %collective-permute-start.7) | collective-permute-done | bytes 524320 | tf_op jit(solution)/shard_map/ppermute | solution.py:53
  35.0 3.5 %shard_map.90 = (f32[2,32,8192]{2,1,0:T(8,128)S(1)}, f32[2,32,8192]{2,1,0:T(8,128)S(1)}, f32[2,32,8192]{2,1,0:T(8,128)S(1)}) custom-call(s32[4]{0:T(128)S(1)} %pad_add_fusion.where, f32[2,32,8192]{2,1,0:T(8,128)} %refs_0_.1, f32[2,32,8192]{2,1,0:T(8,128)} %refs_1_.1, f32[2,32,8192]{2,1,0:T(8,128)} %refs_2_.1, ...), custom_call_target="tpu_custom_call" | custom-call | flops 1048576 | bytes 6291456 | tf_op jit(solution)/shard_map/pallas_call | solution.py:147
  38.5 1.8 %collective-permute-done.6.refs_2_ = bf16[4,32,2048]{2,1,0:T(8,128)(2,1)S(1)} collective-permute-done((bf16[4,32,2048]{2,1,0:T(8,128)(2,1)S(1)}, bf16[4,32,2048]{2,1,0:T(8,128)(2,1)S(1)}, u32[]{:S(2)}, u32[]{:S(2)}) %collective-permute-start.6) | collective-permute-done | bytes 524320 | tf_op jit(solution)/shard_map/ppermute | solution.py:53
  41.4 2.1 %collective-permute-start.9 = (bf16[2,32,2048]{2,1,0:T(8,128)(2,1)S(1)}, bf16[2,32,2048]{2,1,0:T(8,128)(2,1)S(1)}, u32[]{:S(2)}, u32[]{:S(2)}) collective-permute-start(bf16[2,32,2048]{2,1,0:T(8,128)(2,1)S(1)} %get-tuple-element.39), channel_id=1, source_target_pairs={{0,8},{1,33},{2,10},{3,35},{4,12},{5,37},{6,14},{7,39},{8,0},{9,41... | collective-permute-start | bytes 786440 | tf_op jit(solution)/shard_map/ppermute | solution.py:53
  43.5 1.5 %collective-permute-start.10 = (bf16[2,32,2048]{2,1,0:T(8,128)(2,1)S(1)}, bf16[2,32,2048]{2,1,0:T(8,128)(2,1)S(1)}, u32[]{:S(2)}, u32[]{:S(2)}) collective-permute-start(bf16[2,32,2048]{2,1,0:T(8,128)(2,1)S(1)} %get-tuple-element.40), channel_id=1, source_target_pairs={{0,4},{1,17},{2,6},{3,19},{4,8},{5,21},{6,10},{7,23},{8,12},{9,25}... | collective-permute-start | bytes 786440 | tf_op jit(solution)/shard_map/ppermute | solution.py:53
  46.1 2.1 %collective-permute-done.9.refs_1_ = bf16[2,32,2048]{2,1,0:T(8,128)(2,1)S(1)} collective-permute-done((bf16[2,32,2048]{2,1,0:T(8,128)(2,1)S(1)}, bf16[2,32,2048]{2,1,0:T(8,128)(2,1)S(1)}, u32[]{:S(2)}, u32[]{:S(2)}) %collective-permute-start.9) | collective-permute-done | bytes 262176 | tf_op jit(solution)/shard_map/ppermute | solution.py:53
  48.3 2.7 %collective-permute-done.10.refs_2_ = bf16[2,32,2048]{2,1,0:T(8,128)(2,1)S(1)} collective-permute-done((bf16[2,32,2048]{2,1,0:T(8,128)(2,1)S(1)}, bf16[2,32,2048]{2,1,0:T(8,128)(2,1)S(1)}, u32[]{:S(2)}, u32[]{:S(2)}) %collective-permute-start.10) | collective-permute-done | bytes 262176 | tf_op jit(solution)/shard_map/ppermute | solution.py:53
  52.7 3.3 %collective-permute-start.14 = (bf16[32,2048]{1,0:T(8,128)(2,1)S(1)}, bf16[32,2048]{1,0:T(8,128)(2,1)S(1)}, u32[]{:S(2)}, u32[]{:S(2)}) collective-permute-start(bf16[32,2048]{1,0:T(8,128)(2,1)S(1)} %get-tuple-element.43), channel_id=1, source_target_pairs={{0,66},{1,67},{2,64},{3,65},{4,70},{5,71},{6,68},{7,69},{8,74},{9,... | collective-permute-start | bytes 393224 | tf_op jit(solution)/shard_map/ppermute | solution.py:44
  56.0 2.2 %collective-permute-done.12.refs_1_ = bf16[32,2048]{1,0:T(8,128)(2,1)S(1)} collective-permute-done((bf16[32,2048]{1,0:T(8,128)(2,1)S(1)}, bf16[32,2048]{1,0:T(8,128)(2,1)S(1)}, u32[]{:S(2)}, u32[]{:S(2)}) %collective-permute-start.12) | collective-permute-done | bytes 131104 | tf_op jit(solution)/shard_map/ppermute | solution.py:44
  59.7 2.1 %collective-permute-done.13.refs_2_ = bf16[32,2048]{1,0:T(8,128)(2,1)S(1)} collective-permute-done((bf16[32,2048]{1,0:T(8,128)(2,1)S(1)}, bf16[32,2048]{1,0:T(8,128)(2,1)S(1)}, u32[]{:S(2)}, u32[]{:S(2)}) %collective-permute-start.13) | collective-permute-done | bytes 131104 | tf_op jit(solution)/shard_map/ppermute | solution.py:44
  62.5 1.9 %collective-permute-start.17 = (bf16[32,2176]{1,0:T(8,128)(2,1)S(1)}, bf16[32,2176]{1,0:T(8,128)(2,1)S(1)}, u32[]{:S(2)}, u32[]{:S(2)}) collective-permute-start(bf16[32,2176]{1,0:T(8,128)(2,1)S(1)} %shard_map.93.refs_0_), channel_id=1, source_target_pairs={{0,8},{1,9},{2,10},{3,11},{4,12},{5,13},{6,14},{7,15},{8,0},{9,1},... | collective-permute-start | bytes 417800 | tf_op jit(solution)/shard_map/ppermute | solution.py:44
  65.8 3.4 %collective-permute-done.17.refs_3_ = bf16[32,2176]{1,0:T(8,128)(2,1)S(1)} collective-permute-done((bf16[32,2176]{1,0:T(8,128)(2,1)S(1)}, bf16[32,2176]{1,0:T(8,128)(2,1)S(1)}, u32[]{:S(2)}, u32[]{:S(2)}) %collective-permute-start.17) | collective-permute-done | bytes 139296 | tf_op jit(solution)/shard_map/ppermute | solution.py:44
  69.3 3.6 %collective-permute-done.16.refs_2_ = bf16[32,2176]{1,0:T(8,128)(2,1)S(1)} collective-permute-done((bf16[32,2176]{1,0:T(8,128)(2,1)S(1)}, bf16[32,2176]{1,0:T(8,128)(2,1)S(1)}, u32[]{:S(2)}, u32[]{:S(2)}) %collective-permute-start.16) | collective-permute-done | bytes 139296 | tf_op jit(solution)/shard_map/ppermute | solution.py:44
  74.0 2.1 %collective-permute-start.21 = (f32[8,128]{1,0:T(8,128)S(1)}, f32[8,128]{1,0:T(8,128)S(1)}, u32[]{:S(2)}, u32[]{:S(2)}) collective-permute-start(f32[8,128]{1,0:T(8,128)S(1)} %get-tuple-element.45), channel_id=1, source_target_pairs={{0,32},{1,33},{2,34},{3,35},{4,36},{5,37},{6,38},{7,39},{8,40},{9,... | collective-permute-start | bytes 12296 | tf_op jit(solution)/shard_map/ppermute | solution.py:44
  78.8 1.9 %collective-permute-done.19 = f32[8,128]{1,0:T(8,128)S(1)} collective-permute-done((f32[8,128]{1,0:T(8,128)S(1)}, f32[8,128]{1,0:T(8,128)S(1)}, u32[]{:S(2)}, u32[]{:S(2)}) %collective-permute-start.19) | collective-permute-done | bytes 4128 | tf_op jit(solution)/shard_map/ppermute | solution.py:44
  80.7 1.7 %collective-permute-start.24 = (f32[8,128]{1,0:T(8,128)S(1)}, f32[8,128]{1,0:T(8,128)S(1)}, u32[]{:S(2)}, u32[]{:S(2)}) collective-permute-start(f32[8,128]{1,0:T(8,128)S(1)} %add_add_fusion.1), channel_id=1, source_target_pairs={{0,65},{1,64},{2,67},{3,66},{4,69},{5,68},{6,71},{7,70},{8,73},{9,... | collective-permute-start | bytes 12296 | tf_op jit(solution)/shard_map/ppermute | solution.py:58
  85.2 4.3 %shard_map.95 = (f32[2,32,8192]{2,1,0:T(8,128)}, f32[2,32,8192]{2,1,0:T(8,128)}, f32[2,32,8192]{2,1,0:T(8,128)}, f32[2,32,8192]{2,1,0:T(8,128)}) custom-call(s32[4]{0:T(128)S(1)} %pad_add_fusion.where, bf16[4,32,2048]{2,1,0:T(8,128)(2,1)S(1)} %get-tuple-element.44.ours, bf16[4,32,2048]{2,1,0:T(8,128)(2,1)S(1)} %collective-permute-done.18.theirs, ...), custom_call_target="tpu_custom_call" | custom-call | flops 9437184 | bytes 9437184 | tf_op jit(solution)/shard_map/pallas_call | solution.py:219
  (46 shorter events, 22.0 us)
Async XLA Ops:
  3.3 4.4 %collective-permute-start = (bf16[1,2,4,32,2048]{4,3,2,1,0:T(8,128)(2,1)S(1)}, bf16[1,2,4,32,2048]{4,3,2,1,0:T(8,128)(2,1)S(1)}, u32[]{:S(2)}, u32[]{:S(2)}) collective-permute-start(bf16[1,2,4,32,2048]{4,3,2,1,0:T(8,128)(2,1)S(1)} %get-tuple-element.29.refs_0_), channel_id=1, source_target_pairs={{0,1},{1,0},{2,3},{3,2},{4,5},{5,4},{6,7},{7,6},{8,9},{9,8},{10,11... | collective-permute-start | bytes 3145736 | tf_op jit(solution)/shard_map/ppermute | solution.py:44
  8.5 10.3 %collective-permute-start.2 = (bf16[3,2,4,32,2048]{4,3,2,1,0:T(8,128)(2,1)S(1)}, bf16[3,2,4,32,2048]{4,3,2,1,0:T(8,128)(2,1)S(1)}, u32[]{:S(2)}, u32[]{:S(2)}) collective-permute-start(bf16[3,2,4,32,2048]{4,3,2,1,0:T(8,128)(2,1)S(1)} %get-tuple-element.32), channel_id=1, source_target_pairs={{0,1},{1,0},{2,3},{3,2},{4,5},{5,4},{6,7},{7,6},{8,9},{9,8},{10,11... | collective-permute-start | bytes 9437192 | tf_op jit(solution)/shard_map/ppermute | solution.py:44
  8.9 10.0 %collective-permute-start.1 = (bf16[4,32,2048]{2,1,0:T(8,128)(2,1)S(1)}, bf16[4,32,2048]{2,1,0:T(8,128)(2,1)S(1)}, u32[]{:S(2)}, u32[]{:S(2)}) collective-permute-start(bf16[4,32,2048]{2,1,0:T(8,128)(2,1)S(1)} %get-tuple-element.30), channel_id=1, source_target_pairs={{0,48},{1,13},{2,50},{3,15},{4,52},{5,1},{6,54},{7,3},{8,56},{9,5}... | collective-permute-start | bytes 1572872 | tf_op jit(solution)/shard_map/ppermute | solution.py:53
  12.7 11.7 %collective-permute-start.4 = (bf16[4,32,2048]{2,1,0:T(8,128)(2,1)S(1)}, bf16[4,32,2048]{2,1,0:T(8,128)(2,1)S(1)}, u32[]{:S(2)}, u32[]{:S(2)}) collective-permute-start(bf16[4,32,2048]{2,1,0:T(8,128)(2,1)S(1)} %get-tuple-element.31.refs_0_), channel_id=1, source_target_pairs={{0,16},{1,13},{2,18},{3,15},{4,20},{5,1},{6,22},{7,3},{8,24},{9,5}... | collective-permute-start | bytes 1572872 | tf_op jit(solution)/shard_map/ppermute | solution.py:53
  12.8 25.7 %collective-permute-start.8 = (bf16[2,32,8192]{2,1,0:T(8,128)(2,1)S(1)}, bf16[2,32,8192]{2,1,0:T(8,128)(2,1)S(1)}, u32[]{:S(2)}, u32[]{:S(2)}) collective-permute-start(bf16[2,32,8192]{2,1,0:T(8,128)(2,1)S(1)} %fusion.refs_1_), channel_id=1, source_target_pairs={{0,1},{1,2},{2,3},{3,4},{4,5},{5,6},{6,7},{7,8},{8,9},{9,10},{10,1... | collective-permute-start | bytes 3145736 | tf_op jit(solution)/shard_map/ppermute | solution.py:239
  19.7 15.3 %collective-permute-start.7 = (bf16[4,32,2048]{2,1,0:T(8,128)(2,1)S(1)}, bf16[4,32,2048]{2,1,0:T(8,128)(2,1)S(1)}, u32[]{:S(2)}, u32[]{:S(2)}) collective-permute-start(bf16[4,32,2048]{2,1,0:T(8,128)(2,1)S(1)} %get-tuple-element.36), channel_id=1, source_target_pairs={{0,16},{1,5},{2,18},{3,7},{4,20},{5,9},{6,22},{7,11},{8,24},{9,13}... | collective-permute-start | bytes 1572872 | tf_op jit(solution)/shard_map/ppermute | solution.py:53
  20.0 15.0 %collective-permute-start.3 = (bf16[4,32,2048]{2,1,0:T(8,128)(2,1)S(1)}, bf16[4,32,2048]{2,1,0:T(8,128)(2,1)S(1)}, u32[]{:S(2)}, u32[]{:S(2)}) collective-permute-start(bf16[4,32,2048]{2,1,0:T(8,128)(2,1)S(1)} %get-tuple-element.33.refs_3_), channel_id=1, source_target_pairs={{0,48},{1,13},{2,50},{3,15},{4,52},{5,1},{6,54},{7,3},{8,56},{9,5}... | collective-permute-start | bytes 1572872 | tf_op jit(solution)/shard_map/ppermute | solution.py:53
  25.4 13.1 %collective-permute-start.5 = (bf16[4,32,2048]{2,1,0:T(8,128)(2,1)S(1)}, bf16[4,32,2048]{2,1,0:T(8,128)(2,1)S(1)}, u32[]{:S(2)}, u32[]{:S(2)}) collective-permute-start(bf16[4,32,2048]{2,1,0:T(8,128)(2,1)S(1)} %get-tuple-element.34), channel_id=1, source_target_pairs={{0,48},{1,13},{2,50},{3,15},{4,52},{5,1},{6,54},{7,3},{8,56},{9,5}... | collective-permute-start | bytes 1572872 | tf_op jit(solution)/shard_map/ppermute | solution.py:53
  28.9 11.4 %collective-permute-start.6 = (bf16[4,32,2048]{2,1,0:T(8,128)(2,1)S(1)}, bf16[4,32,2048]{2,1,0:T(8,128)(2,1)S(1)}, u32[]{:S(2)}, u32[]{:S(2)}) collective-permute-start(bf16[4,32,2048]{2,1,0:T(8,128)(2,1)S(1)} %get-tuple-element.35), channel_id=1, source_target_pairs={{0,16},{1,5},{2,18},{3,7},{4,20},{5,9},{6,22},{7,11},{8,24},{9,13}... | collective-permute-start | bytes 1572872 | tf_op jit(solution)/shard_map/ppermute | solution.py:53
  41.4 6.9 %collective-permute-start.9 = (bf16[2,32,2048]{2,1,0:T(8,128)(2,1)S(1)}, bf16[2,32,2048]{2,1,0:T(8,128)(2,1)S(1)}, u32[]{:S(2)}, u32[]{:S(2)}) collective-permute-start(bf16[2,32,2048]{2,1,0:T(8,128)(2,1)S(1)} %get-tuple-element.39), channel_id=1, source_target_pairs={{0,8},{1,33},{2,10},{3,35},{4,12},{5,37},{6,14},{7,39},{8,0},{9,41... | collective-permute-start | bytes 786440 | tf_op jit(solution)/shard_map/ppermute | solution.py:53
  43.5 7.5 %collective-permute-start.10 = (bf16[2,32,2048]{2,1,0:T(8,128)(2,1)S(1)}, bf16[2,32,2048]{2,1,0:T(8,128)(2,1)S(1)}, u32[]{:S(2)}, u32[]{:S(2)}) collective-permute-start(bf16[2,32,2048]{2,1,0:T(8,128)(2,1)S(1)} %get-tuple-element.40), channel_id=1, source_target_pairs={{0,4},{1,17},{2,6},{3,19},{4,8},{5,21},{6,10},{7,23},{8,12},{9,25}... | collective-permute-start | bytes 786440 | tf_op jit(solution)/shard_map/ppermute | solution.py:53
  45.0 6.6 %collective-permute-start.11 = (bf16[2,32,2048]{2,1,0:T(8,128)(2,1)S(1)}, bf16[2,32,2048]{2,1,0:T(8,128)(2,1)S(1)}, u32[]{:S(2)}, u32[]{:S(2)}) collective-permute-start(bf16[2,32,2048]{2,1,0:T(8,128)(2,1)S(1)} %get-tuple-element.41), channel_id=1, source_target_pairs={{0,12},{1,49},{2,14},{3,51},{4,0},{5,53},{6,2},{7,55},{8,4},{9,57}... | collective-permute-start | bytes 786440 | tf_op jit(solution)/shard_map/ppermute | solution.py:53
  52.2 6.0 %collective-permute-start.12 = (bf16[32,2048]{1,0:T(8,128)(2,1)S(1)}, bf16[32,2048]{1,0:T(8,128)(2,1)S(1)}, u32[]{:S(2)}, u32[]{:S(2)}) collective-permute-start(bf16[32,2048]{1,0:T(8,128)(2,1)S(1)} %get-tuple-element.42.refs_0_), channel_id=1, source_target_pairs={{0,2},{1,3},{2,0},{3,1},{4,6},{5,7},{6,4},{7,5},{8,10},{9,11},{10,... | collective-permute-start | bytes 393224 | tf_op jit(solution)/shard_map/ppermute | solution.py:44
  52.7 7.0 %collective-permute-start.14 = (bf16[32,2048]{1,0:T(8,128)(2,1)S(1)}, bf16[32,2048]{1,0:T(8,128)(2,1)S(1)}, u32[]{:S(2)}, u32[]{:S(2)}) collective-permute-start(bf16[32,2048]{1,0:T(8,128)(2,1)S(1)} %get-tuple-element.43), channel_id=1, source_target_pairs={{0,66},{1,67},{2,64},{3,65},{4,70},{5,71},{6,68},{7,69},{8,74},{9,... | collective-permute-start | bytes 393224 | tf_op jit(solution)/shard_map/ppermute | solution.py:44
  56.0 5.8 %collective-permute-start.13 = (bf16[32,2048]{1,0:T(8,128)(2,1)S(1)}, bf16[32,2048]{1,0:T(8,128)(2,1)S(1)}, u32[]{:S(2)}, u32[]{:S(2)}) collective-permute-start(bf16[32,2048]{1,0:T(8,128)(2,1)S(1)} %get-tuple-element.43), channel_id=1, source_target_pairs={{0,64},{1,65},{2,66},{3,67},{4,68},{5,69},{6,70},{7,71},{8,72},{9,... | collective-permute-start | bytes 393224 | tf_op jit(solution)/shard_map/ppermute | solution.py:44
  62.5 6.8 %collective-permute-start.17 = (bf16[32,2176]{1,0:T(8,128)(2,1)S(1)}, bf16[32,2176]{1,0:T(8,128)(2,1)S(1)}, u32[]{:S(2)}, u32[]{:S(2)}) collective-permute-start(bf16[32,2176]{1,0:T(8,128)(2,1)S(1)} %shard_map.93.refs_0_), channel_id=1, source_target_pairs={{0,8},{1,9},{2,10},{3,11},{4,12},{5,13},{6,14},{7,15},{8,0},{9,1},... | collective-permute-start | bytes 417800 | tf_op jit(solution)/shard_map/ppermute | solution.py:44
  64.4 8.5 %collective-permute-start.16 = (bf16[32,2176]{1,0:T(8,128)(2,1)S(1)}, bf16[32,2176]{1,0:T(8,128)(2,1)S(1)}, u32[]{:S(2)}, u32[]{:S(2)}) collective-permute-start(bf16[32,2176]{1,0:T(8,128)(2,1)S(1)} %shard_map.93.refs_0_), channel_id=1, source_target_pairs={{0,12},{1,13},{2,14},{3,15},{4,0},{5,1},{6,2},{7,3},{8,4},{9,5},{1... | collective-permute-start | bytes 417800 | tf_op jit(solution)/shard_map/ppermute | solution.py:44
  65.7 7.1 %collective-permute-start.15 = (bf16[32,2176]{1,0:T(8,128)(2,1)S(1)}, bf16[32,2176]{1,0:T(8,128)(2,1)S(1)}, u32[]{:S(2)}, u32[]{:S(2)}) collective-permute-start(bf16[32,2176]{1,0:T(8,128)(2,1)S(1)} %shard_map.93.refs_0_), channel_id=1, source_target_pairs={{0,4},{1,5},{2,6},{3,7},{4,8},{5,9},{6,10},{7,11},{8,12},{9,13},{1... | collective-permute-start | bytes 417800 | tf_op jit(solution)/shard_map/ppermute | solution.py:44
  73.5 11.7 %collective-permute-start.18 = (bf16[4,32,2048]{2,1,0:T(8,128)(2,1)S(1)}, bf16[4,32,2048]{2,1,0:T(8,128)(2,1)S(1)}, u32[]{:S(2)}, u32[]{:S(2)}) collective-permute-start(bf16[4,32,2048]{2,1,0:T(8,128)(2,1)S(1)} %get-tuple-element.44.ours), channel_id=1, source_target_pairs={{0,1},{1,0},{2,3},{3,2},{4,5},{5,4},{6,7},{7,6},{8,9},{9,8},{10,11... | collective-permute-start | bytes 1572872 | tf_op jit(solution)/shard_map/ppermute | solution.py:44
  74.0 4.0 %collective-permute-start.21 = (f32[8,128]{1,0:T(8,128)S(1)}, f32[8,128]{1,0:T(8,128)S(1)}, u32[]{:S(2)}, u32[]{:S(2)}) collective-permute-start(f32[8,128]{1,0:T(8,128)S(1)} %get-tuple-element.45), channel_id=1, source_target_pairs={{0,32},{1,33},{2,34},{3,35},{4,36},{5,37},{6,38},{7,39},{8,40},{9,... | collective-permute-start | bytes 12296 | tf_op jit(solution)/shard_map/ppermute | solution.py:44
  76.1 2.7 %collective-permute-start.20 = (f32[8,128]{1,0:T(8,128)S(1)}, f32[8,128]{1,0:T(8,128)S(1)}, u32[]{:S(2)}, u32[]{:S(2)}) collective-permute-start(f32[8,128]{1,0:T(8,128)S(1)} %get-tuple-element.45), channel_id=1, source_target_pairs={{0,48},{1,49},{2,50},{3,51},{4,52},{5,53},{6,54},{7,55},{8,56},{9,... | collective-permute-start | bytes 12296 | tf_op jit(solution)/shard_map/ppermute | solution.py:44
  77.0 3.7 %collective-permute-start.19 = (f32[8,128]{1,0:T(8,128)S(1)}, f32[8,128]{1,0:T(8,128)S(1)}, u32[]{:S(2)}, u32[]{:S(2)}) collective-permute-start(f32[8,128]{1,0:T(8,128)S(1)} %get-tuple-element.45), channel_id=1, source_target_pairs={{0,16},{1,17},{2,18},{3,19},{4,20},{5,21},{6,22},{7,23},{8,24},{9,... | collective-permute-start | bytes 12296 | tf_op jit(solution)/shard_map/ppermute | solution.py:44
  80.7 3.1 %collective-permute-start.24 = (f32[8,128]{1,0:T(8,128)S(1)}, f32[8,128]{1,0:T(8,128)S(1)}, u32[]{:S(2)}, u32[]{:S(2)}) collective-permute-start(f32[8,128]{1,0:T(8,128)S(1)} %add_add_fusion.1), channel_id=1, source_target_pairs={{0,65},{1,64},{2,67},{3,66},{4,69},{5,68},{6,71},{7,70},{8,73},{9,... | collective-permute-start | bytes 12296 | tf_op jit(solution)/shard_map/ppermute | solution.py:58
  82.4 2.7 %collective-permute-start.23 = (f32[8,128]{1,0:T(8,128)S(1)}, f32[8,128]{1,0:T(8,128)S(1)}, u32[]{:S(2)}, u32[]{:S(2)}) collective-permute-start(f32[8,128]{1,0:T(8,128)S(1)} %add_add_fusion.1), channel_id=1, source_target_pairs={{0,64},{1,65},{2,66},{3,67},{4,68},{5,69},{6,70},{7,71},{8,72},{9,... | collective-permute-start | bytes 12296 | tf_op jit(solution)/shard_map/ppermute | solution.py:58
  (3 other events, 9.4 us)

commit v6 on v5

--- a/solution.py
+++ b/solution.py
@@ -203,7 +203,7 @@
 
         for side, pieces in enumerate((ours, theirs)):
 
-            @pl.loop(0, 4)
+            @pl.loop(0, 4, unroll=True)
             def _(j, side=side, pieces=pieces):
                 layer = where[C] if side == 0 else 1 - where[C]
                 update(where, layer, j, pieces, state, [h.at[side] for h in held])

time: 89.7 us -> 89.6 us (level)
  no operation moved by 1% of the time
where the time goes in v6:
time: 89.6 us; the launch traced here: 89.5 us
  starting transfers between devices  33.9 us (38%)
  waiting for transfers between devices  33.1 us (37%)
  Pallas kernels  21.4 us (24%)
    ppermute x13, waiting for transfers between devices, move(): return lax.ppermute(value, AXES, pairs)  15.9 us
    ppermute x9, waiting for transfers between devices, turn(): return lax.ppermute(value, AXES, [(rank(*s), goal(*s)) for s in spots()])  15.9 us
    ppermute x9, starting transfers between devices, turn(): return lax.ppermute(value, AXES, [(rank(*s), goal(*s)) for s in spots()])  15.8 us
    ppermute x13, starting transfers between devices, move(): return lax.ppermute(value, AXES, pairs)  13.1 us
    pallas_call x3, Pallas kernels, fetch(): pl.pallas_call(body, in_specs=[pl.BlockSpec(memory_space=pltpu.SMEM)] + [...  7.96 us
    pallas_call x6, Pallas kernels, vmem_call(): pl.pallas_call(run, in_specs=[pl.BlockSpec(memory_space=pltpu.SMEM)] + [p...  4.87 us
    pallas_call x1, Pallas kernels, update_all(): pl.pallas_call(body, in_specs=[pl.BlockSpec(memory_space=pltpu.SMEM)] + [...  4.31 us
    pallas_call x1, Pallas kernels, preload(): pl.pallas_call(body, in_specs=[pl.BlockSpec(memory_space=pltpu.SMEM)] + [...  3.51 us
  transfers between devices with their start and end apart: 25, of which 16 were waited for; matrix products, arithmetic and copies ran while one was open for 0% of the time, Pallas kernels for 12%

profile of v6, /device:TPU:1, one launch (start us, length us, event | category | flops | bytes accessed | tf_op | source)
XLA Modules:
  0.0 89.5 jit_solution(17738877236730984180)
XLA Ops:
  0.7 2.6 %shard_map.84 = (bf16[1,2,4,32,2048]{4,3,2,1,0:T(8,128)(2,1)S(1)}, bf16[1,2,4,32,2048]{4,3,2,1,0:T(8,128)(2,1)S(1)}) custom-call(s32[4]{0:T(128)S(1)} %pad_add_fusion.where, bf16[2,2,4,32,8192]{4,3,2,1,0:T(8,128)(2,1)} %bitcast.10), custom_call_target="tpu_custom_call" | custom-call | bytes 2097152 | tf_op jit(solution)/shard_map/pallas_call | solution.py:116
  5.0 2.7 %shard_map.85.rest = bf16[3,2,4,32,2048]{4,3,2,1,0:T(8,128)(2,1)S(1)} custom-call(s32[4]{0:T(128)S(1)} %pad_add_fusion.where, bf16[2,2,4,32,8192]{4,3,2,1,0:T(8,128)(2,1)} %bitcast.11, bf16[1,2,4,32,2048]{4,3,2,1,0:T(8,128)(2,1)S(1)} %get-tuple-element.29.refs_0_, bf16[2,32,8192]{2,1,0:T(8,128)(2,1)S(1)} %fusion.refs_1_), custom_call_target="tpu_custom_call" | custom-call | bytes 3145728 | tf_op jit(solution)/shard_map/pallas_call | solution.py:116
  8.9 3.8 %collective-permute-start.1 = (bf16[4,32,2048]{2,1,0:T(8,128)(2,1)S(1)}, bf16[4,32,2048]{2,1,0:T(8,128)(2,1)S(1)}, u32[]{:S(2)}, u32[]{:S(2)}) collective-permute-start(bf16[4,32,2048]{2,1,0:T(8,128)(2,1)S(1)} %get-tuple-element.30), channel_id=1, source_target_pairs={{0,48},{1,13},{2,50},{3,15},{4,52},{5,1},{6,54},{7,3},{8,56},{9,5}... | collective-permute-start | bytes 1572872 | tf_op jit(solution)/shard_map/ppermute | solution.py:53
  12.8 1.9 %collective-permute-start.8 = (bf16[2,32,8192]{2,1,0:T(8,128)(2,1)S(1)}, bf16[2,32,8192]{2,1,0:T(8,128)(2,1)S(1)}, u32[]{:S(2)}, u32[]{:S(2)}) collective-permute-start(bf16[2,32,8192]{2,1,0:T(8,128)(2,1)S(1)} %fusion.refs_1_), channel_id=1, source_target_pairs={{0,1},{1,2},{2,3},{3,4},{4,5},{5,6},{6,7},{7,8},{8,9},{9,10},{10,1... | collective-permute-start | bytes 3145736 | tf_op jit(solution)/shard_map/ppermute | solution.py:239
  14.7 2.7 %shard_map.87.refs_1_.refs_4_ = bf16[3,2,4,32,2048]{4,3,2,1,0:T(8,128)(2,1)S(1)} custom-call(s32[4]{0:T(128)S(1)} %pad_add_fusion.where, bf16[2,2,4,32,8192]{4,3,2,1,0:T(8,128)(2,1)} %bitcast.12, bf16[4,32,2048]{2,1,0:T(8,128)(2,1)S(1)} %get-tuple-element.31.refs_0_), custom_call_target="tpu_custom_call" | custom-call | bytes 3145728 | tf_op jit(solution)/shard_map/pallas_call | solution.py:116
  20.0 3.2 %collective-permute-start.3 = (bf16[4,32,2048]{2,1,0:T(8,128)(2,1)S(1)}, bf16[4,32,2048]{2,1,0:T(8,128)(2,1)S(1)}, u32[]{:S(2)}, u32[]{:S(2)}) collective-permute-start(bf16[4,32,2048]{2,1,0:T(8,128)(2,1)S(1)} %get-tuple-element.33.refs_3_), channel_id=1, source_target_pairs={{0,48},{1,13},{2,50},{3,15},{4,52},{5,1},{6,54},{7,3},{8,56},{9,5}... | collective-permute-start | bytes 1572872 | tf_op jit(solution)/shard_map/ppermute | solution.py:53
  25.4 3.5 %collective-permute-start.5 = (bf16[4,32,2048]{2,1,0:T(8,128)(2,1)S(1)}, bf16[4,32,2048]{2,1,0:T(8,128)(2,1)S(1)}, u32[]{:S(2)}, u32[]{:S(2)}) collective-permute-start(bf16[4,32,2048]{2,1,0:T(8,128)(2,1)S(1)} %get-tuple-element.34), channel_id=1, source_target_pairs={{0,48},{1,13},{2,50},{3,15},{4,52},{5,1},{6,54},{7,3},{8,56},{9,5}... | collective-permute-start | bytes 1572872 | tf_op jit(solution)/shard_map/ppermute | solution.py:53
  28.9 6.1 %collective-permute-done.7.refs_4_.refs_3_ = bf16[4,32,2048]{2,1,0:T(8,128)(2,1)S(1)} collective-permute-done((bf16[4,32,2048]{2,1,0:T(8,128)(2,1)S(1)}, bf16[4,32,2048]{2,1,0:T(8,128)(2,1)S(1)}, u32[]{:S(2)}, u32[]{:S(2)}) %collective-permute-start.7) | collective-permute-done | bytes 524320 | tf_op jit(solution)/shard_map/ppermute | solution.py:53
  35.0 3.5 %shard_map.90 = (f32[2,32,8192]{2,1,0:T(8,128)S(1)}, f32[2,32,8192]{2,1,0:T(8,128)S(1)}, f32[2,32,8192]{2,1,0:T(8,128)S(1)}) custom-call(s32[4]{0:T(128)S(1)} %pad_add_fusion.where, f32[2,32,8192]{2,1,0:T(8,128)} %refs_0_.1, f32[2,32,8192]{2,1,0:T(8,128)} %refs_1_.1, f32[2,32,8192]{2,1,0:T(8,128)} %refs_2_.1, ...), custom_call_target="tpu_custom_call" | custom-call | flops 1048576 | bytes 6291456 | tf_op jit(solution)/shard_map/pallas_call | solution.py:147
  38.5 1.8 %collective-permute-done.6.refs_2_ = bf16[4,32,2048]{2,1,0:T(8,128)(2,1)S(1)} collective-permute-done((bf16[4,32,2048]{2,1,0:T(8,128)(2,1)S(1)}, bf16[4,32,2048]{2,1,0:T(8,128)(2,1)S(1)}, u32[]{:S(2)}, u32[]{:S(2)}) %collective-permute-start.6) | collective-permute-done | bytes 524320 | tf_op jit(solution)/shard_map/ppermute | solution.py:53
  41.4 2.1 %collective-permute-start.9 = (bf16[2,32,2048]{2,1,0:T(8,128)(2,1)S(1)}, bf16[2,32,2048]{2,1,0:T(8,128)(2,1)S(1)}, u32[]{:S(2)}, u32[]{:S(2)}) collective-permute-start(bf16[2,32,2048]{2,1,0:T(8,128)(2,1)S(1)} %get-tuple-element.39), channel_id=1, source_target_pairs={{0,8},{1,33},{2,10},{3,35},{4,12},{5,37},{6,14},{7,39},{8,0},{9,41... | collective-permute-start | bytes 786440 | tf_op jit(solution)/shard_map/ppermute | solution.py:53
  43.5 1.5 %collective-permute-start.10 = (bf16[2,32,2048]{2,1,0:T(8,128)(2,1)S(1)}, bf16[2,32,2048]{2,1,0:T(8,128)(2,1)S(1)}, u32[]{:S(2)}, u32[]{:S(2)}) collective-permute-start(bf16[2,32,2048]{2,1,0:T(8,128)(2,1)S(1)} %get-tuple-element.40), channel_id=1, source_target_pairs={{0,4},{1,17},{2,6},{3,19},{4,8},{5,21},{6,10},{7,23},{8,12},{9,25}... | collective-permute-start | bytes 786440 | tf_op jit(solution)/shard_map/ppermute | solution.py:53
  46.1 2.1 %collective-permute-done.9.refs_1_ = bf16[2,32,2048]{2,1,0:T(8,128)(2,1)S(1)} collective-permute-done((bf16[2,32,2048]{2,1,0:T(8,128)(2,1)S(1)}, bf16[2,32,2048]{2,1,0:T(8,128)(2,1)S(1)}, u32[]{:S(2)}, u32[]{:S(2)}) %collective-permute-start.9) | collective-permute-done | bytes 262176 | tf_op jit(solution)/shard_map/ppermute | solution.py:53
  48.3 2.7 %collective-permute-done.10.refs_2_ = bf16[2,32,2048]{2,1,0:T(8,128)(2,1)S(1)} collective-permute-done((bf16[2,32,2048]{2,1,0:T(8,128)(2,1)S(1)}, bf16[2,32,2048]{2,1,0:T(8,128)(2,1)S(1)}, u32[]{:S(2)}, u32[]{:S(2)}) %collective-permute-start.10) | collective-permute-done | bytes 262176 | tf_op jit(solution)/shard_map/ppermute | solution.py:53
  52.7 3.3 %collective-permute-start.14 = (bf16[32,2048]{1,0:T(8,128)(2,1)S(1)}, bf16[32,2048]{1,0:T(8,128)(2,1)S(1)}, u32[]{:S(2)}, u32[]{:S(2)}) collective-permute-start(bf16[32,2048]{1,0:T(8,128)(2,1)S(1)} %get-tuple-element.43), channel_id=1, source_target_pairs={{0,66},{1,67},{2,64},{3,65},{4,70},{5,71},{6,68},{7,69},{8,74},{9,... | collective-permute-start | bytes 393224 | tf_op jit(solution)/shard_map/ppermute | solution.py:44
  56.0 2.2 %collective-permute-done.12.refs_1_ = bf16[32,2048]{1,0:T(8,128)(2,1)S(1)} collective-permute-done((bf16[32,2048]{1,0:T(8,128)(2,1)S(1)}, bf16[32,2048]{1,0:T(8,128)(2,1)S(1)}, u32[]{:S(2)}, u32[]{:S(2)}) %collective-permute-start.12) | collective-permute-done | bytes 131104 | tf_op jit(solution)/shard_map/ppermute | solution.py:44
  59.7 2.1 %collective-permute-done.13.refs_2_ = bf16[32,2048]{1,0:T(8,128)(2,1)S(1)} collective-permute-done((bf16[32,2048]{1,0:T(8,128)(2,1)S(1)}, bf16[32,2048]{1,0:T(8,128)(2,1)S(1)}, u32[]{:S(2)}, u32[]{:S(2)}) %collective-permute-start.13) | collective-permute-done | bytes 131104 | tf_op jit(solution)/shard_map/ppermute | solution.py:44
  62.5 1.9 %collective-permute-start.17 = (bf16[32,2176]{1,0:T(8,128)(2,1)S(1)}, bf16[32,2176]{1,0:T(8,128)(2,1)S(1)}, u32[]{:S(2)}, u32[]{:S(2)}) collective-permute-start(bf16[32,2176]{1,0:T(8,128)(2,1)S(1)} %shard_map.93.refs_0_), channel_id=1, source_target_pairs={{0,8},{1,9},{2,10},{3,11},{4,12},{5,13},{6,14},{7,15},{8,0},{9,1},... | collective-permute-start | bytes 417800 | tf_op jit(solution)/shard_map/ppermute | solution.py:44
  65.8 3.4 %collective-permute-done.17.refs_3_ = bf16[32,2176]{1,0:T(8,128)(2,1)S(1)} collective-permute-done((bf16[32,2176]{1,0:T(8,128)(2,1)S(1)}, bf16[32,2176]{1,0:T(8,128)(2,1)S(1)}, u32[]{:S(2)}, u32[]{:S(2)}) %collective-permute-start.17) | collective-permute-done | bytes 139296 | tf_op jit(solution)/shard_map/ppermute | solution.py:44
  69.3 3.6 %collective-permute-done.16.refs_2_ = bf16[32,2176]{1,0:T(8,128)(2,1)S(1)} collective-permute-done((bf16[32,2176]{1,0:T(8,128)(2,1)S(1)}, bf16[32,2176]{1,0:T(8,128)(2,1)S(1)}, u32[]{:S(2)}, u32[]{:S(2)}) %collective-permute-start.16) | collective-permute-done | bytes 139296 | tf_op jit(solution)/shard_map/ppermute | solution.py:44
  74.0 2.1 %collective-permute-start.21 = (f32[8,128]{1,0:T(8,128)S(1)}, f32[8,128]{1,0:T(8,128)S(1)}, u32[]{:S(2)}, u32[]{:S(2)}) collective-permute-start(f32[8,128]{1,0:T(8,128)S(1)} %get-tuple-element.45), channel_id=1, source_target_pairs={{0,32},{1,33},{2,34},{3,35},{4,36},{5,37},{6,38},{7,39},{8,40},{9,... | collective-permute-start | bytes 12296 | tf_op jit(solution)/shard_map/ppermute | solution.py:44
  78.8 1.9 %collective-permute-done.19 = f32[8,128]{1,0:T(8,128)S(1)} collective-permute-done((f32[8,128]{1,0:T(8,128)S(1)}, f32[8,128]{1,0:T(8,128)S(1)}, u32[]{:S(2)}, u32[]{:S(2)}) %collective-permute-start.19) | collective-permute-done | bytes 4128 | tf_op jit(solution)/shard_map/ppermute | solution.py:44
  80.7 1.7 %collective-permute-start.24 = (f32[8,128]{1,0:T(8,128)S(1)}, f32[8,128]{1,0:T(8,128)S(1)}, u32[]{:S(2)}, u32[]{:S(2)}) collective-permute-start(f32[8,128]{1,0:T(8,128)S(1)} %add_add_fusion.1), channel_id=1, source_target_pairs={{0,65},{1,64},{2,67},{3,66},{4,69},{5,68},{6,71},{7,70},{8,73},{9,... | collective-permute-start | bytes 12296 | tf_op jit(solution)/shard_map/ppermute | solution.py:58
  85.2 4.3 %shard_map.95 = (f32[2,32,8192]{2,1,0:T(8,128)}, f32[2,32,8192]{2,1,0:T(8,128)}, f32[2,32,8192]{2,1,0:T(8,128)}, f32[2,32,8192]{2,1,0:T(8,128)}) custom-call(s32[4]{0:T(128)S(1)} %pad_add_fusion.where, bf16[4,32,2048]{2,1,0:T(8,128)(2,1)S(1)} %get-tuple-element.44.ours, bf16[4,32,2048]{2,1,0:T(8,128)(2,1)S(1)} %collective-permute-done.18.theirs, ...), custom_call_target="tpu_custom_call" | custom-call | flops 9437184 | bytes 9437184 | tf_op jit(solution)/shard_map/pallas_call | solution.py:219
  (46 shorter events, 22.0 us)
Async XLA Ops:
  3.3 4.4 %collective-permute-start = (bf16[1,2,4,32,2048]{4,3,2,1,0:T(8,128)(2,1)S(1)}, bf16[1,2,4,32,2048]{4,3,2,1,0:T(8,128)(2,1)S(1)}, u32[]{:S(2)}, u32[]{:S(2)}) collective-permute-start(bf16[1,2,4,32,2048]{4,3,2,1,0:T(8,128)(2,1)S(1)} %get-tuple-element.29.refs_0_), channel_id=1, source_target_pairs={{0,1},{1,0},{2,3},{3,2},{4,5},{5,4},{6,7},{7,6},{8,9},{9,8},{10,11... | collective-permute-start | bytes 3145736 | tf_op jit(solution)/shard_map/ppermute | solution.py:44
  8.5 10.3 %collective-permute-start.2 = (bf16[3,2,4,32,2048]{4,3,2,1,0:T(8,128)(2,1)S(1)}, bf16[3,2,4,32,2048]{4,3,2,1,0:T(8,128)(2,1)S(1)}, u32[]{:S(2)}, u32[]{:S(2)}) collective-permute-start(bf16[3,2,4,32,2048]{4,3,2,1,0:T(8,128)(2,1)S(1)} %get-tuple-element.32), channel_id=1, source_target_pairs={{0,1},{1,0},{2,3},{3,2},{4,5},{5,4},{6,7},{7,6},{8,9},{9,8},{10,11... | collective-permute-start | bytes 9437192 | tf_op jit(solution)/shard_map/ppermute | solution.py:44
  8.9 10.0 %collective-permute-start.1 = (bf16[4,32,2048]{2,1,0:T(8,128)(2,1)S(1)}, bf16[4,32,2048]{2,1,0:T(8,128)(2,1)S(1)}, u32[]{:S(2)}, u32[]{:S(2)}) collective-permute-start(bf16[4,32,2048]{2,1,0:T(8,128)(2,1)S(1)} %get-tuple-element.30), channel_id=1, source_target_pairs={{0,48},{1,13},{2,50},{3,15},{4,52},{5,1},{6,54},{7,3},{8,56},{9,5}... | collective-permute-start | bytes 1572872 | tf_op jit(solution)/shard_map/ppermute | solution.py:53
  12.7 11.7 %collective-permute-start.4 = (bf16[4,32,2048]{2,1,0:T(8,128)(2,1)S(1)}, bf16[4,32,2048]{2,1,0:T(8,128)(2,1)S(1)}, u32[]{:S(2)}, u32[]{:S(2)}) collective-permute-start(bf16[4,32,2048]{2,1,0:T(8,128)(2,1)S(1)} %get-tuple-element.31.refs_0_), channel_id=1, source_target_pairs={{0,16},{1,13},{2,18},{3,15},{4,20},{5,1},{6,22},{7,3},{8,24},{9,5}... | collective-permute-start | bytes 1572872 | tf_op jit(solution)/shard_map/ppermute | solution.py:53
  12.8 25.7 %collective-permute-start.8 = (bf16[2,32,8192]{2,1,0:T(8,128)(2,1)S(1)}, bf16[2,32,8192]{2,1,0:T(8,128)(2,1)S(1)}, u32[]{:S(2)}, u32[]{:S(2)}) collective-permute-start(bf16[2,32,8192]{2,1,0:T(8,128)(2,1)S(1)} %fusion.refs_1_), channel_id=1, source_target_pairs={{0,1},{1,2},{2,3},{3,4},{4,5},{5,6},{6,7},{7,8},{8,9},{9,10},{10,1... | collective-permute-start | bytes 3145736 | tf_op jit(solution)/shard_map/ppermute | solution.py:239
  19.7 15.3 %collective-permute-start.7 = (bf16[4,32,2048]{2,1,0:T(8,128)(2,1)S(1)}, bf16[4,32,2048]{2,1,0:T(8,128)(2,1)S(1)}, u32[]{:S(2)}, u32[]{:S(2)}) collective-permute-start(bf16[4,32,2048]{2,1,0:T(8,128)(2,1)S(1)} %get-tuple-element.36), channel_id=1, source_target_pairs={{0,16},{1,5},{2,18},{3,7},{4,20},{5,9},{6,22},{7,11},{8,24},{9,13}... | collective-permute-start | bytes 1572872 | tf_op jit(solution)/shard_map/ppermute | solution.py:53
  20.0 15.0 %collective-permute-start.3 = (bf16[4,32,2048]{2,1,0:T(8,128)(2,1)S(1)}, bf16[4,32,2048]{2,1,0:T(8,128)(2,1)S(1)}, u32[]{:S(2)}, u32[]{:S(2)}) collective-permute-start(bf16[4,32,2048]{2,1,0:T(8,128)(2,1)S(1)} %get-tuple-element.33.refs_3_), channel_id=1, source_target_pairs={{0,48},{1,13},{2,50},{3,15},{4,52},{5,1},{6,54},{7,3},{8,56},{9,5}... | collective-permute-start | bytes 1572872 | tf_op jit(solution)/shard_map/ppermute | solution.py:53
  25.4 13.1 %collective-permute-start.5 = (bf16[4,32,2048]{2,1,0:T(8,128)(2,1)S(1)}, bf16[4,32,2048]{2,1,0:T(8,128)(2,1)S(1)}, u32[]{:S(2)}, u32[]{:S(2)}) collective-permute-start(bf16[4,32,2048]{2,1,0:T(8,128)(2,1)S(1)} %get-tuple-element.34), channel_id=1, source_target_pairs={{0,48},{1,13},{2,50},{3,15},{4,52},{5,1},{6,54},{7,3},{8,56},{9,5}... | collective-permute-start | bytes 1572872 | tf_op jit(solution)/shard_map/ppermute | solution.py:53
  28.9 11.4 %collective-permute-start.6 = (bf16[4,32,2048]{2,1,0:T(8,128)(2,1)S(1)}, bf16[4,32,2048]{2,1,0:T(8,128)(2,1)S(1)}, u32[]{:S(2)}, u32[]{:S(2)}) collective-permute-start(bf16[4,32,2048]{2,1,0:T(8,128)(2,1)S(1)} %get-tuple-element.35), channel_id=1, source_target_pairs={{0,16},{1,5},{2,18},{3,7},{4,20},{5,9},{6,22},{7,11},{8,24},{9,13}... | collective-permute-start | bytes 1572872 | tf_op jit(solution)/shard_map/ppermute | solution.py:53
  41.4 6.9 %collective-permute-start.9 = (bf16[2,32,2048]{2,1,0:T(8,128)(2,1)S(1)}, bf16[2,32,2048]{2,1,0:T(8,128)(2,1)S(1)}, u32[]{:S(2)}, u32[]{:S(2)}) collective-permute-start(bf16[2,32,2048]{2,1,0:T(8,128)(2,1)S(1)} %get-tuple-element.39), channel_id=1, source_target_pairs={{0,8},{1,33},{2,10},{3,35},{4,12},{5,37},{6,14},{7,39},{8,0},{9,41... | collective-permute-start | bytes 786440 | tf_op jit(solution)/shard_map/ppermute | solution.py:53
  43.5 7.5 %collective-permute-start.10 = (bf16[2,32,2048]{2,1,0:T(8,128)(2,1)S(1)}, bf16[2,32,2048]{2,1,0:T(8,128)(2,1)S(1)}, u32[]{:S(2)}, u32[]{:S(2)}) collective-permute-start(bf16[2,32,2048]{2,1,0:T(8,128)(2,1)S(1)} %get-tuple-element.40), channel_id=1, source_target_pairs={{0,4},{1,17},{2,6},{3,19},{4,8},{5,21},{6,10},{7,23},{8,12},{9,25}... | collective-permute-start | bytes 786440 | tf_op jit(solution)/shard_map/ppermute | solution.py:53
  45.0 6.6 %collective-permute-start.11 = (bf16[2,32,2048]{2,1,0:T(8,128)(2,1)S(1)}, bf16[2,32,2048]{2,1,0:T(8,128)(2,1)S(1)}, u32[]{:S(2)}, u32[]{:S(2)}) collective-permute-start(bf16[2,32,2048]{2,1,0:T(8,128)(2,1)S(1)} %get-tuple-element.41), channel_id=1, source_target_pairs={{0,12},{1,49},{2,14},{3,51},{4,0},{5,53},{6,2},{7,55},{8,4},{9,57}... | collective-permute-start | bytes 786440 | tf_op jit(solution)/shard_map/ppermute | solution.py:53
  52.2 6.0 %collective-permute-start.12 = (bf16[32,2048]{1,0:T(8,128)(2,1)S(1)}, bf16[32,2048]{1,0:T(8,128)(2,1)S(1)}, u32[]{:S(2)}, u32[]{:S(2)}) collective-permute-start(bf16[32,2048]{1,0:T(8,128)(2,1)S(1)} %get-tuple-element.42.refs_0_), channel_id=1, source_target_pairs={{0,2},{1,3},{2,0},{3,1},{4,6},{5,7},{6,4},{7,5},{8,10},{9,11},{10,... | collective-permute-start | bytes 393224 | tf_op jit(solution)/shard_map/ppermute | solution.py:44
  52.7 7.0 %collective-permute-start.14 = (bf16[32,2048]{1,0:T(8,128)(2,1)S(1)}, bf16[32,2048]{1,0:T(8,128)(2,1)S(1)}, u32[]{:S(2)}, u32[]{:S(2)}) collective-permute-start(bf16[32,2048]{1,0:T(8,128)(2,1)S(1)} %get-tuple-element.43), channel_id=1, source_target_pairs={{0,66},{1,67},{2,64},{3,65},{4,70},{5,71},{6,68},{7,69},{8,74},{9,... | collective-permute-start | bytes 393224 | tf_op jit(solution)/shard_map/ppermute | solution.py:44
  56.0 5.8 %collective-permute-start.13 = (bf16[32,2048]{1,0:T(8,128)(2,1)S(1)}, bf16[32,2048]{1,0:T(8,128)(2,1)S(1)}, u32[]{:S(2)}, u32[]{:S(2)}) collective-permute-start(bf16[32,2048]{1,0:T(8,128)(2,1)S(1)} %get-tuple-element.43), channel_id=1, source_target_pairs={{0,64},{1,65},{2,66},{3,67},{4,68},{5,69},{6,70},{7,71},{8,72},{9,... | collective-permute-start | bytes 393224 | tf_op jit(solution)/shard_map/ppermute | solution.py:44
  62.5 6.8 %collective-permute-start.17 = (bf16[32,2176]{1,0:T(8,128)(2,1)S(1)}, bf16[32,2176]{1,0:T(8,128)(2,1)S(1)}, u32[]{:S(2)}, u32[]{:S(2)}) collective-permute-start(bf16[32,2176]{1,0:T(8,128)(2,1)S(1)} %shard_map.93.refs_0_), channel_id=1, source_target_pairs={{0,8},{1,9},{2,10},{3,11},{4,12},{5,13},{6,14},{7,15},{8,0},{9,1},... | collective-permute-start | bytes 417800 | tf_op jit(solution)/shard_map/ppermute | solution.py:44
  64.4 8.5 %collective-permute-start.16 = (bf16[32,2176]{1,0:T(8,128)(2,1)S(1)}, bf16[32,2176]{1,0:T(8,128)(2,1)S(1)}, u32[]{:S(2)}, u32[]{:S(2)}) collective-permute-start(bf16[32,2176]{1,0:T(8,128)(2,1)S(1)} %shard_map.93.refs_0_), channel_id=1, source_target_pairs={{0,12},{1,13},{2,14},{3,15},{4,0},{5,1},{6,2},{7,3},{8,4},{9,5},{1... | collective-permute-start | bytes 417800 | tf_op jit(solution)/shard_map/ppermute | solution.py:44
  65.7 7.1 %collective-permute-start.15 = (bf16[32,2176]{1,0:T(8,128)(2,1)S(1)}, bf16[32,2176]{1,0:T(8,128)(2,1)S(1)}, u32[]{:S(2)}, u32[]{:S(2)}) collective-permute-start(bf16[32,2176]{1,0:T(8,128)(2,1)S(1)} %shard_map.93.refs_0_), channel_id=1, source_target_pairs={{0,4},{1,5},{2,6},{3,7},{4,8},{5,9},{6,10},{7,11},{8,12},{9,13},{1... | collective-permute-start | bytes 417800 | tf_op jit(solution)/shard_map/ppermute | solution.py:44
  73.5 11.7 %collective-permute-start.18 = (bf16[4,32,2048]{2,1,0:T(8,128)(2,1)S(1)}, bf16[4,32,2048]{2,1,0:T(8,128)(2,1)S(1)}, u32[]{:S(2)}, u32[]{:S(2)}) collective-permute-start(bf16[4,32,2048]{2,1,0:T(8,128)(2,1)S(1)} %get-tuple-element.44.ours), channel_id=1, source_target_pairs={{0,1},{1,0},{2,3},{3,2},{4,5},{5,4},{6,7},{7,6},{8,9},{9,8},{10,11... | collective-permute-start | bytes 1572872 | tf_op jit(solution)/shard_map/ppermute | solution.py:44
  74.0 4.0 %collective-permute-start.21 = (f32[8,128]{1,0:T(8,128)S(1)}, f32[8,128]{1,0:T(8,128)S(1)}, u32[]{:S(2)}, u32[]{:S(2)}) collective-permute-start(f32[8,128]{1,0:T(8,128)S(1)} %get-tuple-element.45), channel_id=1, source_target_pairs={{0,32},{1,33},{2,34},{3,35},{4,36},{5,37},{6,38},{7,39},{8,40},{9,... | collective-permute-start | bytes 12296 | tf_op jit(solution)/shard_map/ppermute | solution.py:44
  76.1 2.7 %collective-permute-start.20 = (f32[8,128]{1,0:T(8,128)S(1)}, f32[8,128]{1,0:T(8,128)S(1)}, u32[]{:S(2)}, u32[]{:S(2)}) collective-permute-start(f32[8,128]{1,0:T(8,128)S(1)} %get-tuple-element.45), channel_id=1, source_target_pairs={{0,48},{1,49},{2,50},{3,51},{4,52},{5,53},{6,54},{7,55},{8,56},{9,... | collective-permute-start | bytes 12296 | tf_op jit(solution)/shard_map/ppermute | solution.py:44
  77.0 3.7 %collective-permute-start.19 = (f32[8,128]{1,0:T(8,128)S(1)}, f32[8,128]{1,0:T(8,128)S(1)}, u32[]{:S(2)}, u32[]{:S(2)}) collective-permute-start(f32[8,128]{1,0:T(8,128)S(1)} %get-tuple-element.45), channel_id=1, source_target_pairs={{0,16},{1,17},{2,18},{3,19},{4,20},{5,21},{6,22},{7,23},{8,24},{9,... | collective-permute-start | bytes 12296 | tf_op jit(solution)/shard_map/ppermute | solution.py:44
  80.7 3.1 %collective-permute-start.24 = (f32[8,128]{1,0:T(8,128)S(1)}, f32[8,128]{1,0:T(8,128)S(1)}, u32[]{:S(2)}, u32[]{:S(2)}) collective-permute-start(f32[8,128]{1,0:T(8,128)S(1)} %add_add_fusion.1), channel_id=1, source_target_pairs={{0,65},{1,64},{2,67},{3,66},{4,69},{5,68},{6,71},{7,70},{8,73},{9,... | collective-permute-start | bytes 12296 | tf_op jit(solution)/shard_map/ppermute | solution.py:58
  82.4 2.7 %collective-permute-start.23 = (f32[8,128]{1,0:T(8,128)S(1)}, f32[8,128]{1,0:T(8,128)S(1)}, u32[]{:S(2)}, u32[]{:S(2)}) collective-permute-start(f32[8,128]{1,0:T(8,128)S(1)} %add_add_fusion.1), channel_id=1, source_target_pairs={{0,64},{1,65},{2,66},{3,67},{4,68},{5,69},{6,70},{7,71},{8,72},{9,... | collective-permute-start | bytes 12296 | tf_op jit(solution)/shard_map/ppermute | solution.py:58
  (3 other events, 9.4 us)
